TPU v7x, 32 devices: a whole 2x2x4 slice. The times are simulated.
32 devices in a mesh: expert: 8 (over z, y), context: 4 (over x, core).
Axes of the slice: x: 2, y: 2, z: 4, core: 2. Of those that a mesh axis runs over, the one named last changes fastest.
Arguments:
- tokens: bfloat16 [8, 512, 2048], P('expert', 'context'), may hold values from -6 to 6
- route: int32 [8, 512, 1], P('expert'), may hold values from 0 to 7; in each aligned block of 128 rows (0 to 127, 128 to 255, ..., all dimensions but the last counted through in order) at most 32 rows name the same one
- w_inner: bfloat16 [8, 2048, 2, 4096], P('expert', None, None, 'context'), may hold values from -0.125 to 0.125
- w_state: bfloat16 [8, 2048, 128], P('expert'), may hold values from -0.015625 to 0.015625
- w_step: bfloat16 [8, 2048, 64], P('expert', None, 'context'), may hold values from -0.125 to 0.125
- step_bias: float32 [64], P('context'), may hold values from -2 to 0.5
- decay_log: float32 [64], P('context'), may hold values from -7 to -2.5
- skip_gain: float32 [64], P('context'), may hold values from 0.5 to 1.5
- conv_weight: float32 [4, 4096], P(None, 'context'), may hold values from -3 to 3
- conv_bias: float32 [4096], P('context'), may hold values from -1.5 to 1.5
- w_out: bfloat16 [8, 4096, 2048], P('expert', 'context'), may hold values from -0.09375 to 0.09375
Outputs:
- mixed: bfloat16 [8, 512, 2048], P('expert', 'context')
Inputs may be any that keep to these rules, and one draw needn't show every extreme that they name: `route`: in each aligned block of 128 positions (the rows of one device) no expert is named more than 32 times, a bound that some block reaches.
All inputs are finite; a program needn't handle non-finite values.
Results may differ from a plain program's by a relative error of at most 0.014.
Values may be sent and summed in bfloat16 or wider, within the bound.
No kernel may reach another device: no remote copies, remote signals or barrier semaphores. Data moves between devices by JAX's collectives and lax.ppermute only.
A program may use at most 128 MiB of HBM per device.

v0:
```python
import functools

import jax
import jax.numpy as jnp
from jax import lax
from jax.experimental import pallas as pl
from jax.experimental.pallas import tpu as pltpu
from jax.sharding import PartitionSpec as P

HEAD_DIM = 64
LANES = 128
BF16 = jnp.bfloat16
F32 = jnp.float32


def iota(shape, axis):
    return lax.broadcasted_iota(jnp.int32, shape, axis)


def dot(a, b):
    return jnp.dot(a, b, preferred_element_type=F32)


def flat_rows(pieces):
    count, rows, lanes = pieces.shape
    if rows % 16:
        return pieces.astype(F32).reshape(count * rows, lanes).astype(BF16)
    return pieces.reshape(count * rows, lanes)


def slot_rows(ids, experts, cap):
    tok_rows = ids.shape[1]
    onehot = jnp.where(iota((experts, tok_rows), 0) == ids, 1.0, 0.0)
    upto = jnp.where(iota((tok_rows, tok_rows), 0) <= iota((tok_rows, tok_rows), 1), 1.0, 0.0)
    before = dot(onehot.astype(BF16), upto.astype(BF16))
    rank = jnp.sum(onehot * before, axis=0, keepdims=True) - 1.0
    slot = ids * cap + rank.astype(jnp.int32)
    return jnp.where(iota((experts * cap, tok_rows), 0) == slot, 1.0, 0.0)


VMEM = pl.BlockSpec(memory_space=pltpu.VMEM)
SMEM = pl.BlockSpec(memory_space=pltpu.SMEM)
HBM = pl.BlockSpec(memory_space=pltpu.HBM)


class Stream:
    def __init__(self, copies, ahead):
        self.copies, self.ahead, self.started, self.done = copies, ahead, 0, set()
        self.start(ahead)

    def start(self, upto):
        while self.started < min(upto, len(self.copies)):
            self.copies[self.started].start()
            self.started += 1

    def need(self, i):
        self.start(i + self.ahead)
        if i not in self.done:
            self.copies[i].wait()
            self.done.add(i)


class Operand:
    def __init__(self, held, stream=None, first=0, count=0):
        self.held, self.stream, self.first, self.count = held, stream, first, count

    def piece(self, t):
        if self.stream:
            self.stream.need(self.first + t)
        return self.held

    def whole(self):
        for t in range(self.count):
            self.piece(t)
        return self.held


class Result:
    def __init__(self, held, copies=()):
        self.held, self.copies = held, copies

    def send(self, t):
        if self.copies:
            self.copies[t].start()

    def finish(self):
        for copy in self.copies:
            copy.wait()


def in_hbm(array):
    return pltpu.with_memory_space_constraint(array, pltpu.HBM)


def in_vmem(array):
    return pltpu.with_memory_space_constraint(array, pltpu.VMEM)


def kept_in_vmem(array):
    return (array, None, None)


def full(array):
    return (array, array.shape, [(Ellipsis, Ellipsis)])


def firsts(array):
    return (array, array.shape, [(t, t) for t in range(array.shape[0])])


def columns(array, start, count, tile):
    cuts = [
        ((slice(None), pl.ds(start + lo, tile)), (slice(None), pl.ds(lo, tile)))
        for lo in range(0, count, tile)
    ]
    return (array, (array.shape[0], count), cuts)


def place_of(array, at):
    held = (array.shape[0], *array.shape[2:])
    return (array, held, [((slice(None), at), Ellipsis)])


def call(
    kernel, info, big, outs, small=(), after=(), alias=None, scratch=(), flops=0, exps=0, limit=32
):
    moved = sum(2 * a.size for a, _, _ in big) + sum(2 * o.size for o, _ in outs)
    held = []
    for array, dims, pieces in big:
        if pieces:
            held.append(pltpu.VMEM(dims, array.dtype))
    for out, pieces in outs:
        if pieces:
            held.append(pltpu.VMEM(out.shape, out.dtype))
    fetches = sum(len(pieces or ()) for _, _, pieces in big)
    sends = sum(len(pieces or ()) for _, pieces in outs)
    held += [pltpu.SemaphoreType.DMA((max(count, 1),)) for count in (fetches, sends)]

    def body(*refs):
        refs = list(refs)

        def take(count):
            taken = refs[:count]
            del refs[:count]
            return taken

        info_ref = take(1)[0]
        small_refs, big_refs = take(len(small)), take(len(big))
        take(len(after) + (alias is not None))
        out_refs = take(len(outs))
        held_refs = [take(1)[0] if pieces else ref for ref, (_, _, pieces) in zip(big_refs, big)]
        made_refs = [take(1)[0] if pieces else ref for ref, (_, pieces) in zip(out_refs, outs)]
        fetch_sems, send_sems = take(2)
        copies, spans = [], []
        for source, target, (_, _, pieces) in zip(big_refs, held_refs, big):
            spans.append((len(copies), len(pieces or ())))
            for there, here in pieces or ():
                sem = fetch_sems.at[len(copies)]
                copies.append(pltpu.make_async_copy(source.at[there], target.at[here], sem))
        stream = Stream(copies, 3)
        operands = [
            Operand(ref, stream if count else None, at, count)
            for ref, (at, count) in zip(held_refs, spans)
        ]
        results, used = [], 0
        for target, source, (_, pieces) in zip(out_refs, made_refs, outs):
            sent = []
            for at in pieces or ():
                sent.append(pltpu.make_async_copy(source.at[at], target.at[at], send_sems.at[used]))
                used += 1
            results.append(Result(source, sent))
        kernel(info_ref, *small_refs, *operands, *results, *refs)
        for i in range(len(copies)):
            stream.need(i)
        for result in results:
            result.finish()

    arrays = [in_hbm(a) if pieces else in_vmem(a) for a, _, pieces in big]
    arrays += [in_hbm(array) for array in after] + ([in_hbm(alias)] if alias is not None else [])
    return pl.pallas_call(
        body,
        out_shape=[(pltpu.HBM if pieces else pltpu.VMEM)(o.shape, o.dtype) for o, pieces in outs],
        in_specs=[SMEM]
        + [VMEM] * len(small)
        + [HBM if pieces else VMEM for _, _, pieces in big]
        + [HBM] * (len(after) + (alias is not None)),
        out_specs=[HBM if pieces else VMEM for _, pieces in outs],
        scratch_shapes=held + list(scratch),
        input_output_aliases={len(small) + len(arrays): 0} if alias is not None else {},
        compiler_params=pltpu.CompilerParams(vmem_limit_bytes=limit << 20),
        cost_estimate=pl.CostEstimate(flops=flops, bytes_accessed=moved, transcendentals=exps),
    )(info, *small, *arrays)


def shape(*dims):
    return jax.ShapeDtypeStruct(dims, BF16)


def tie(value, *after):
    return pl.pallas_call(
        lambda *refs: None,
        out_shape=pltpu.VMEM(value.shape, value.dtype),
        in_specs=[VMEM] + [HBM] * len(after),
        out_specs=VMEM,
        input_output_aliases={0: 0},
        compiler_params=pltpu.CompilerParams(vmem_limit_bytes=4 << 20),
    )(in_vmem(value), *(in_hbm(array) for array in after))


def dispatch_kernel(experts, cap, info_ref, ids, tokens, out):
    place = slot_rows(ids.whole()[info_ref[0]], experts, cap).astype(BF16)
    out.held[...] = dot(place, tokens.whole()[...]).astype(BF16)
    out.send(0)


def collect_kernel(experts, cap, info_ref, ids_ref, rows, out):
    place = slot_rows(ids_ref[info_ref[0]], experts, cap).T.astype(BF16)
    out.held[...] = dot(place, rows.whole()[...]).astype(BF16)
    out.send(0)


def side_kernel(experts, cap, info_ref, ids_ref, near, out):
    place = slot_rows(ids_ref[info_ref[0]], experts, cap).T.astype(BF16)
    rows_ref = near.whole()
    for i in range(2):
        rows = flat_rows(rows_ref[:, i])
        out.held[:, i * LANES : (i + 1) * LANES] = dot(place, rows).astype(BF16)
    out.send(0)


def project_rows(places, experts, cap, rows, weight, out, tile):
    chans = weight.held.shape[1]
    for lo in range(0, chans, tile):
        part = weight.piece(lo // tile)[:, lo : lo + tile]
        for at, block in zip(places, rows):
            store_rows(out, at, lo, dot(block.whole()[...], part), experts, cap)
        out.send(lo // tile)


def store_rows(out, at, lo, made, experts, cap):
    made = made.astype(BF16)
    for e in range(experts):
        out.held[e, at, :, lo : lo + made.shape[1]] = made[e * cap : (e + 1) * cap, :]


def own_kernel(experts, cap, tile, info_ref, rows, weight, states, *refs):
    steps, out = refs[:-1], refs[-1]
    chans = weight.held.shape[1]
    project_rows([0], experts, cap, [rows], weight, out, tile)
    first = rows.whole()[...]
    store_rows(out, 0, chans, dot(first, states.whole()[...]), experts, cap)
    steps = [ref.whole()[...].astype(F32) for ref in steps]
    spare = LANES - sum(part.shape[0] for part in steps)
    steps.append(jnp.zeros((spare, steps[0].shape[1]), F32))
    steps = jnp.concatenate(steps, axis=0).astype(BF16)
    made = lax.dot_general(first, steps, (((1,), (1,)), ((), ())), preferred_element_type=F32)
    store_rows(out, 1, chans, made, experts, cap)
    out.send(chans // tile)


def project_kernel(places, experts, cap, tile, info_ref, *refs):
    rows, weight, out = refs[: len(places)], refs[-2], refs[-1]
    project_rows(places, experts, cap, rows, weight, out, tile)


def gate_kernel(tile, info_ref, *refs):
    count = len(refs) // 2
    rows, weight, outs = refs[:count], refs[count], refs[count + 1 :]
    for lo in range(0, weight.held.shape[1], tile):
        for block, out in zip(rows, outs):
            made = dot(block.whole()[...], weight.piece(lo // tile)[:, lo : lo + tile])
            out.held[:, lo : lo + tile] = made.astype(BF16)
    for out in outs:
        out.send(0)


def output_kernel(tile, info_ref, scanned, gate, weight, out):
    gates = jax.nn.silu(gate.whole()[...].astype(F32))
    gated = (flat_rows(scanned.whole()[...]).astype(F32) * gates).astype(BF16)
    for lo in range(0, weight.held.shape[1], tile):
        part = weight.piece(lo // tile)[:, lo : lo + tile]
        out.held[:, lo : lo + tile] = dot(gated, part).astype(BF16)


def factors_kernel(cfg, info_ref, ids_ref, head_ref, near, side, weights, kept, tail, last, placed):
    experts, cap, tok_rows, nstate, chn, heads = cfg
    blocks = ids_ref.shape[0]
    lower = iota((tok_rows, tok_rows), 0) >= iota((tok_rows, tok_rows), 1)
    ones = jnp.where(lower, 1.0, 0.0)
    first = iota((tok_rows, LANES), 1) < HEAD_DIM
    spread = jnp.where(
        iota((2 * LANES, chn), 0) % LANES == iota((2 * LANES, chn), 1) // HEAD_DIM, 1.0, 0.0
    ).astype(BF16)
    for q in range(2):
        place = slot_rows(ids_ref[info_ref[1 + q]], experts, cap).T.astype(BF16)
        placed.held[q] = dot(place, flat_rows(near.whole()[:, q, :, :chn])).astype(BF16)
    placed.send(0)
    side_ref = side.whole()
    for b in range(blocks):
        q = info_ref[1 + blocks + b]
        own_head = iota((LANES, LANES), 0) == iota((LANES, LANES), 1) + info_ref[
            1 + 2 * blocks + b
        ] * heads
        own_head = jnp.where(own_head & (iota((LANES, LANES), 1) < heads), 1.0, 0.0)
        raw = dot(side_ref[q, :, LANES:], own_head.astype(BF16))
        step = jax.nn.softplus(raw + head_ref[0:1, :])
        summed = jnp.dot(
            ones,
            step * head_ref[1:2, :],
            preferred_element_type=F32,
            precision=lax.Precision.HIGHEST,
        )
        source = summed - jnp.log(step)
        source_t = source.T
        left = jnp.exp(summed[tok_rows - 1 :, :] - source)
        high = left.astype(BF16)
        low = (left - high.astype(F32)).astype(BF16)
        tail.held[b] = dot(jnp.concatenate([high, low], axis=1), spread).astype(BF16)
        tail.send(b)

        both = side_ref[q, :, :LANES]
        keys_t = both.astype(F32).T.astype(BF16)[:nstate, :]
        scores = dot(both[:, nstate:], keys_t)
        for pair in range(heads // 2):
            lanes = slice(pair * LANES, (pair + 1) * LANES)
            wide = []
            for h in (2 * pair, 2 * pair + 1):
                wide.append(jnp.broadcast_to(summed[:, h : h + 1], (tok_rows, tok_rows)))
                gaps = wide[-1] - source_t[h : h + 1, :]
                decay = jnp.exp(jnp.where(lower, gaps, -jnp.inf))
                at = (h % 2) * tok_rows
                weights.held[b, pair, :, at : at + tok_rows] = (scores * decay).astype(BF16)
            both_wide = jnp.exp(jnp.where(first, wide[0], wide[1]))
            kept.held[b, :, lanes] = both_wide.astype(BF16)
            last.held[b, :, lanes] = both_wide[tok_rows - 8 :, :]
        weights.send(b)
        kept.send(b)
        last.send(b)


def scan_kernel(
    cfg,
    info_ref,
    ids_ref,
    chan_ref,
    side,
    placed,
    far,
    *refs,
):
    experts, cap, tok_rows, nstate, chn, heads = cfg
    out_near, out_far, inner_ref, made_ref = refs[-4:]
    blocks = ids_ref.shape[0]
    taps = 4
    inner_ref[:8, :] = jnp.zeros((8, chn), F32)

    for q in range(blocks):
        b = info_ref[1 + q]
        at = pl.ds(8 + b * tok_rows, tok_rows)
        if q < 2:
            inner_ref[at, :] = placed.whole()[q].astype(F32)
        else:
            place = slot_rows(ids_ref[b], experts, cap).T.astype(BF16)
            inner_ref[at, :] = dot(place, flat_rows(far.whole()[:, q - 2]))

    first = iota((tok_rows, LANES), 1) < HEAD_DIM
    state = jnp.zeros((nstate, chn), F32)
    side_ref = side.whole()
    for b in range(blocks):
        q = info_ref[1 + blocks + b]
        weights, kept, tail, last = refs[4 * b : 4 * b + 4]
        total = chan_ref[taps : taps + 1, :]
        for j in range(taps):
            start = 8 + b * tok_rows - (taps - 1) + j
            total = total + chan_ref[j : j + 1, :] * inner_ref[start : start + tok_rows, :]
        signal = jax.nn.silu(total)

        both = side_ref[q, :, :LANES]
        keys_t = both.astype(F32).T.astype(BF16)[:nstate, :]
        rest = chan_ref[taps + 1 : taps + 2, :] * signal
        if b > 0:
            carried = dot(both[:, nstate:], state.astype(BF16))
            rest = rest + carried * kept.whole()[0].astype(F32)
        if b < blocks - 1:
            added = dot(keys_t, (signal * tail.whole()[0].astype(F32)).astype(BF16))
            state = last.whole()[0, 7:8, :] * state + added

        for pair in range(heads // 2):
            lanes = slice(pair * LANES, (pair + 1) * LANES)
            values = signal[:, lanes]
            values = jnp.concatenate(
                [jnp.where(first, values, 0.0), jnp.where(first, 0.0, values)], axis=0
            ).astype(BF16)
            local = dot(weights.whole()[0, pair], values)
            made_ref[b * tok_rows : (b + 1) * tok_rows, lanes] = (rest[:, lanes] + local).astype(BF16)

    for q in range(blocks - 1, -1, -1):
        b = info_ref[1 + q]
        place = slot_rows(ids_ref[b], experts, cap).astype(BF16)
        start = pl.multiple_of(b * tok_rows, tok_rows)
        leaving = dot(place, made_ref[pl.ds(start, tok_rows), :]).astype(BF16)
        for e in range(experts):
            piece = leaving[e * cap : (e + 1) * cap, :]
            if q < 2:
                out_near.held[e, q] = piece
            else:
                out_far.held[e, q - 2] = piece
        if q == 2:
            out_far.send(0)
    out_near.send(0)


def per_device(
    tokens,
    route,
    w_inner,
    w_state,
    w_step,
    step_bias,
    decay_log,
    skip_gain,
    conv_weight,
    conv_bias,
    w_out,
):
    tok_rows, width = tokens.shape[1], tokens.shape[2]
    experts = lax.axis_size("expert")
    shards = lax.axis_size("context")
    cap = 2 * tok_rows // experts
    slots = experts * cap
    chans = w_inner.shape[3]
    heads = w_step.shape[2]
    nstate = w_state.shape[2] // 2
    chips = shards // 2
    far_count = shards - 2

    here = lax.axis_index("context").astype(jnp.int32)
    blocks = jnp.arange(shards, dtype=jnp.int32)
    order = 2 * ((here // 2 - blocks // 2) % chips) + ((here % 2) ^ (blocks % 2))
    groups = 2 * ((blocks // 2 - here // 2) % chips) + ((here % 2) ^ (blocks % 2))
    block_at = 2 * ((here // 2 - blocks // 2) % chips) + ((here % 2) ^ (blocks % 2))
    info = jnp.concatenate([here[None], block_at, order, groups])
    ids = route.reshape(shards, 1, tok_rows)
    swap = [(c, c ^ 1) for c in range(shards)]

    def hop(k):
        return [(c, ((c // 2 + k) % chips) * 2 + c % 2) for c in range(shards)]

    def permute(value, pairs):
        return lax.ppermute(value, "context", pairs)

    def spread(value):
        made = [value, permute(value, swap)]
        for k in range(1, chips):
            arrived = permute(value, hop(k))
            made += [arrived, permute(arrived, swap)]
        return made

    def exchange(value):
        return lax.all_to_all(value, "expert", split_axis=0, concat_axis=0, tiled=True)

    w_flat = w_inner[0].reshape(width, 2 * chans)

    once = [Ellipsis]
    outgoing = call(
        functools.partial(dispatch_kernel, experts, cap),
        info, [full(ids), full(tokens[0])], [(shape(slots, width), once)],
        flops=2 * slots * tok_rows * width,
    )[0]
    own = exchange(outgoing.reshape(experts, cap, width)).reshape(slots, width)
    steps = spread(tie(w_step[0], outgoing).T)
    own = tie(own, w_flat, *steps)
    swapped = permute(own, swap)
    everything = (slice(None),) * 3

    def inner_cuts(place, extra):
        at = (slice(None), place, slice(None))
        cuts = [at + (pl.ds(lo, 256),) for lo in range(0, chans, 256)]
        return cuts + [everything + (pl.ds(chans, LANES),)] * extra

    near_shape = shape(experts, 2, cap, chans + LANES)
    own_part = call(
        functools.partial(own_kernel, experts, cap, 256),
        info,
        [kept_in_vmem(own), columns(w_flat, chans, chans, 256), full(w_state[0])]
        + [full(part) for part in steps],
        [(near_shape, inner_cuts(0, 1))],
        flops=2 * slots * width * (chans + 2 * LANES),
    )[0]
    near = call(
        functools.partial(project_kernel, [1], experts, cap, 256),
        info,
        [kept_in_vmem(swapped), columns(w_flat, chans, chans, 256)],
        [(near_shape, inner_cuts(1, 0))],
        alias=own_part,
        flops=2 * slots * width * chans,
    )[0]
    distant = []
    for k in range(1, chips):
        arrived = tie(permute(own, hop(k)), near)
        distant += [arrived, permute(arrived, swap)]
    far = call(
        functools.partial(project_kernel, range(far_count), experts, cap, 256),
        info,
        [kept_in_vmem(rows) for rows in distant] + [columns(w_flat, chans, chans, 256)],
        [(shape(experts, far_count, cap, chans), inner_cuts(slice(None), 0))],
        flops=2 * far_count * slots * width * chans,
    )[0]
    near_back = exchange(near)
    far_back = exchange(far)

    lanes = everything + (pl.ds(chans, LANES),)
    side = call(
        functools.partial(side_kernel, experts, cap),
        info,
        [(near_back, (experts, 2, cap, LANES), [(lanes, Ellipsis)])],
        [(shape(tok_rows, 2 * LANES), once)],
        small=[ids],
        after=[far],
        flops=2 * slots * tok_rows * 2 * LANES,
    )[0]
    sides = jnp.stack(spread(side))

    def padded_heads(row):
        return jnp.pad(row, (0, LANES - heads))[None, :]

    head_rows = jnp.concatenate(
        [padded_heads(step_bias), padded_heads(-jnp.exp(decay_log)), jnp.zeros((6, LANES), F32)]
    )
    chan_rows = jnp.concatenate(
        [conv_weight, conv_bias[None, :], jnp.repeat(skip_gain, HEAD_DIM)[None, :]]
    )
    chan_rows = jnp.pad(chan_rows, ((0, 2), (0, 0)))
    def gates(rows):
        return call(
            functools.partial(gate_kernel, 256),
            info,
            [full(part) for part in rows] + [columns(w_flat, 0, chans, 256)],
            [(shape(slots, chans), once)] * len(rows),
            after=[far],
            flops=2 * len(rows) * slots * width * chans,
        )

    gate_far = gates(distant)
    gate_near = gates([own, swapped])
    cfg = (experts, cap, tok_rows, nstate, chans, heads)
    each = list(range(shards))
    weights, kept, tail, last, placed = call(
        functools.partial(factors_kernel, cfg),
        info, [full(near_back), full(sides)],
        [
            (shape(shards, heads // 2, tok_rows, 2 * tok_rows), each),
            (shape(shards, tok_rows, chans), each),
            (shape(shards, tok_rows, chans), each),
            (jax.ShapeDtypeStruct((shards, 8, chans), F32), each),
            (shape(2, tok_rows, chans), once),
        ],
        small=[ids, head_rows],
        flops=2 * tok_rows * chans * (2 * slots + shards * 512),
        exps=shards * tok_rows * tok_rows * heads,
    )
    in_turn = [
        (array, (1, *array.shape[1:]), [(pl.ds(b, 1), Ellipsis)])
        for b in range(shards)
        for array in (weights, kept, tail, last)
    ]
    near_out, far_out = call(
        functools.partial(scan_kernel, cfg),
        info,
        [full(sides), full(placed), full(far_back)] + in_turn,
        [
            (shape(experts, 2, cap, chans), None),
            (shape(experts, far_count, cap, chans), None),
        ],
        small=[ids, chan_rows],
        after=[gate_far[0], gate_near[0]],
        scratch=[
            pltpu.VMEM((8 + shards * tok_rows, chans), F32),
            pltpu.VMEM((shards * tok_rows, chans), BF16),
        ],
        flops=2 * shards * tok_rows * chans * (2 * slots + 2 * nstate + 2 * tok_rows),
    )
    far_ret = exchange(far_out)
    near_ret = exchange(near_out)

    def output(scanned, at, after=()):
        gate = (gate_near + gate_far)[at]
        return call(
            functools.partial(output_kernel, 512),
            info,
            [place_of(scanned, at % 2 if at < 2 else at - 2), full(gate), columns(w_out[0], 0, width, 512)],
            [(shape(slots, width), None)],
            after=after,
            flops=2 * slots * width * chans,
        )[0]

    hopped = []
    others = [permute(output(far_ret, 2 * k + 1), swap) for k in range(1, chips)]
    for k in range(1, chips):
        pair = output(far_ret, 2 * k).astype(F32) + others[k - 1].astype(F32)
        hopped.append(permute(pair.astype(BF16), hop(chips - k)))
    part_swap = permute(output(near_ret, 1), swap)
    part_own = output(near_ret, 0, hopped)
    summed = part_own.astype(F32) + part_swap.astype(F32)
    for part in hopped:
        summed = summed + part.astype(F32)
    returned = exchange(summed.astype(BF16).reshape(experts, cap, width)).reshape(slots, width)
    result = call(
        functools.partial(collect_kernel, experts, cap),
        info, [kept_in_vmem(returned)], [(shape(tok_rows, width), once)],
        small=[ids],
        flops=2 * slots * tok_rows * width,
    )[0]
    return result[None]


def solution(mesh):
    in_specs = (
        P("expert", "context", None),
        P("expert", None, None),
        P("expert", None, None, "context"),
        P("expert", None, None),
        P("expert", None, "context"),
        P("context"),
        P("context"),
        P("context"),
        P(None, "context"),
        P("context"),
        P("expert", "context", None),
    )
    out_specs = P("expert", "context", None)
    return jax.shard_map(
        per_device, mesh=mesh, in_specs=in_specs, out_specs=out_specs, check_vma=False
    )
```

profile of v0, /device:TPU:0, one launch (start us, length us, event | category | flops | bytes accessed | tf_op | source)
XLA Modules:
  0.0 235.9 jit_solution(16055228786817427943)
XLA Ops:
  0.1 3.0 %shard_map.109.refs_1_ = bf16[256,2048]{1,0:T(8,128)(2,1)} custom-call(s32[13]{0:T(128)S(1)} %pad_add_fusion.refs_0_, s32[4,1,128]{2,1,0:T(1,128)} %bitcast.27, bf16[128,2048]{1,0:T(8,128)(2,1)} %bitcast.49), custom_call_target="tpu_custom_call" | custom-call | flops 134217728 | bytes 1573888 | tf_op jit(solution)/shard_map/pallas_call | solution.py:180
  3.1 7.3 %all-to-all-start = ((bf16[8,32,2048]{2,1,0:T(8,128)(2,1)}), bf16[8,32,2048]{2,1,0:T(8,128)(2,1)S(1)}, u32[]{:S(2)}, u32[]{:S(2)}) async-start(bf16[8,32,2048]{2,1,0:T(8,128)(2,1)} %bitcast.42), calls=%async_computation | async-start | bytes 2097152 | tf_op jit(solution)/shard_map/all_to_all | solution.py:460
  15.3 10.2 %copy.18 = bf16[256,8,2,1024]{3,1,2,0:T(8,128)(2,1)} copy(bf16[256,8,2,1024]{3,2,1,0:T(2,128)(2,1)} %bitcast.43) | data formatting | bytes 16777216
  25.5 10.7 %all-to-all-done = bf16[8,32,2048]{2,1,0:T(8,128)(2,1)S(1)} async-done(((bf16[8,32,2048]{2,1,0:T(8,128)(2,1)}), bf16[8,32,2048]{2,1,0:T(8,128)(2,1)S(1)}, u32[]{:S(2)}, u32[]{:S(2)}) %all-to-all-start) | async-done | bytes 1048608 | tf_op jit(solution)/shard_map/all_to_all | solution.py:460
  37.8 7.1 %shard_map.112.refs_3_ = bf16[8,2,32,1152]{3,2,1,0:T(8,128)(2,1)} custom-call(s32[13]{0:T(128)S(1)} %pad_add_fusion.refs_0_, bf16[256,2048]{1,0:T(8,128)(2,1)S(1)} %shard_map.111.refs_1_, bf16[2048,2048]{1,0:T(8,128)(2,1)} %bitcast.33, bf16[2048,128]{1,0:T(8,128)(2,1)} %bitcast.50, bf16[16,2048]{1,0:T(8,128)(2,1)} %bitcast.48, bf16[16,2048]{1,0:T(8,128)(2,1)} %copy-done.10, ...), custom_call_target="tpu_custom_call" | custom-call | flops 1342177280 | bytes 11403264 | tf_op jit(solution)/shard_map/pallas_call | solution.py:180
  45.0 5.3 %shard_map.113.refs_1_ = bf16[8,2,32,1152]{3,2,1,0:T(8,128)(2,1)} custom-call(s32[13]{0:T(128)S(1)} %pad_add_fusion.refs_0_, bf16[256,2048]{1,0:T(8,128)(2,1)S(1)} %collective-permute-done.3.refs_1_.refs_2_, bf16[2048,2048]{1,0:T(8,128)(2,1)} %bitcast.34, bf16[8,2,32,1152]{3,2,1,0:T(8,128)(2,1)} %shard_map.112.refs_3_), custom_call_target="tpu_custom_call", output_to_operand_aliasing={{}: (3, {})} | custom-call | flops 1073741824 | bytes 10616832 | tf_op jit(solution)/shard_map/pallas_call | solution.py:180
  50.3 4.3 %all-to-all-start.1 = ((bf16[8,2,32,1152]{3,2,1,0:T(8,128)(2,1)}), bf16[8,2,32,1152]{3,2,1,0:T(8,128)(2,1)}, u32[]{:S(2)}, u32[]{:S(2)}) async-start(bf16[8,2,32,1152]{3,2,1,0:T(8,128)(2,1)} %shard_map.113.refs_1_), calls=%async_computation.1 | async-start | bytes 2359296 | tf_op jit(solution)/shard_map/all_to_all | solution.py:460
  54.6 7.2 %collective-permute-done.4.refs_0_ = bf16[256,2048]{1,0:T(8,128)(2,1)S(1)} collective-permute-done((bf16[256,2048]{1,0:T(8,128)(2,1)S(1)}, bf16[256,2048]{1,0:T(8,128)(2,1)S(1)}, u32[]{:S(2)}, u32[]{:S(2)}) %collective-permute-start.4) | collective-permute-done | bytes 1048608 | tf_op jit(solution)/shard_map/ppermute | solution.py:450
  64.5 5.4 %shard_map.115.refs_3_.refs_4_ = bf16[8,2,32,1024]{3,2,1,0:T(8,128)(2,1)} custom-call(s32[13]{0:T(128)S(1)} %pad_add_fusion.refs_0_, bf16[256,2048]{1,0:T(8,128)(2,1)S(1)} %shard_map.114.refs_1_, bf16[256,2048]{1,0:T(8,128)(2,1)S(1)} %collective-permute-done.5.refs_2_, bf16[2048,2048]{1,0:T(8,128)(2,1)} %bitcast.35), custom_call_target="tpu_custom_call" | custom-call | flops 2147483648 | bytes 11534336 | tf_op jit(solution)/shard_map/pallas_call | solution.py:180
  70.1 13.7 %all-to-all-done.1.refs_2_.refs_3_ = bf16[8,2,32,1152]{3,2,1,0:T(8,128)(2,1)} async-done(((bf16[8,2,32,1152]{3,2,1,0:T(8,128)(2,1)}), bf16[8,2,32,1152]{3,2,1,0:T(8,128)(2,1)}, u32[]{:S(2)}, u32[]{:S(2)}) %all-to-all-start.1) | async-done | bytes 1179680 | tf_op jit(solution)/shard_map/all_to_all | solution.py:460
  83.8 3.7 %all-to-all-start.2 = ((bf16[8,2,32,1024]{3,2,1,0:T(8,128)(2,1)}), bf16[8,2,32,1024]{3,2,1,0:T(8,128)(2,1)S(1)}, u32[]{:S(2)}, u32[]{:S(2)}) async-start(bf16[8,2,32,1024]{3,2,1,0:T(8,128)(2,1)} %shard_map.115.refs_3_.refs_4_), calls=%async_computation.2 | async-start | bytes 2097152 | tf_op jit(solution)/shard_map/all_to_all | solution.py:460
  90.8 7.1 %shard_map.119 = (bf16[256,1024]{1,0:T(8,128)(2,1)}, bf16[256,1024]{1,0:T(8,128)(2,1)}) custom-call(s32[13]{0:T(128)S(1)} %pad_add_fusion.refs_0_, bf16[256,2048]{1,0:T(8,128)(2,1)} %copy-done, bf16[256,2048]{1,0:T(8,128)(2,1)} %copy-done.2, bf16[2048,2048]{1,0:T(8,128)(2,1)} %bitcast.36, bf16[8,2,32,1024]{3,2,1,0:T(8,128)(2,1)} %shard_map.115.refs_3_.refs_4_), custom_call_target="tpu_custom_call" | custom-call | flops 2147483648 | bytes 11534336 | tf_op jit(solution)/shard_map/pallas_call | solution.py:180
  98.6 7.2 %shard_map.118 = (bf16[256,1024]{1,0:T(8,128)(2,1)}, bf16[256,1024]{1,0:T(8,128)(2,1)}) custom-call(s32[13]{0:T(128)S(1)} %pad_add_fusion.refs_0_, bf16[256,2048]{1,0:T(8,128)(2,1)} %copy-done.1, bf16[256,2048]{1,0:T(8,128)(2,1)} %copy-done.3, bf16[2048,2048]{1,0:T(8,128)(2,1)} %bitcast.37, bf16[8,2,32,1024]{3,2,1,0:T(8,128)(2,1)} %shard_map.115.refs_3_.refs_4_), custom_call_target="tpu_custom_call" | custom-call | flops 2147483648 | bytes 11534336 | tf_op jit(solution)/shard_map/pallas_call | solution.py:180
  106.6 6.8 %shard_map.117 = (bf16[4,8,128,256]{3,2,1,0:T(8,128)(2,1)}, bf16[4,128,1024]{2,1,0:T(8,128)(2,1)}, bf16[4,128,1024]{2,1,0:T(8,128)(2,1)}, f32[4,8,1024]{2,1,0:T(8,128)}, bf16[2,128,1024]{2,1,0:T(8,128)(2,1)}) custom-call(s32[13]{0:T(128)S(1)} %pad_add_fusion.refs_0_, s32[4,1,128]{2,1,0:T(1,128)S(1)} %bitcast.29, f32[8,128]{1,0:T(8,128)S(1)} %maximum_maximum_fusion.refs_2_, ...), custom_call_target="tpu_custom_call" | custom-call | flops 671088640 | bytes 6225920 | tf_op jit(solution)/shard_map/pallas_call | solution.py:180
  114.4 11.1 %shard_map.120 = (bf16[8,2,32,1024]{3,2,1,0:T(8,128)(2,1)}, bf16[8,2,32,1024]{3,2,1,0:T(8,128)(2,1)S(1)}) custom-call(s32[13]{0:T(128)S(1)} %pad_add_fusion.refs_0_, s32[4,1,128]{2,1,0:T(1,128)S(1)} %bitcast.30, f32[8,1024]{1,0:T(8,128)S(1)} %select_maximum_fusion.refs_2_, bf16[4,128,256]{2,1,0:T(8,128)(2,1)} %pad_maximum_fusion.refs_4_.refs_3_, ...), custom_call_target="tpu_custom_call" | custom-call | flops 939524096 | bytes 20971520 | tf_op jit(solution)/shard_map/pallas_call | solution.py:180
  125.5 31.7 %all_to_all.30.refs_1_ = bf16[8,2,32,1024]{3,2,1,0:T(8,128)(2,1)} all-to-all(bf16[8,2,32,1024]{3,2,1,0:T(8,128)(2,1)S(1)} %get-tuple-element.24), channel_id=1, replica_groups=mesh['expert'=8,'context'=4] {'expert'}, dimensions={0} | all-to-all | bytes 2097152 | tf_op jit(solution)/shard_map/all_to_all | solution.py:460
  157.2 3.6 %all-to-all-start.3 = ((bf16[8,2,32,1024]{3,2,1,0:T(8,128)(2,1)}), bf16[8,2,32,1024]{3,2,1,0:T(8,128)(2,1)S(1)}, u32[]{:S(2)}, u32[]{:S(2)}) async-start(bf16[8,2,32,1024]{3,2,1,0:T(8,128)(2,1)} %get-tuple-element.23), calls=%async_computation.3 | async-start | bytes 2097152 | tf_op jit(solution)/shard_map/all_to_all | solution.py:460
  160.9 4.2 %shard_map.122 = bf16[256,2048]{1,0:T(8,128)(2,1)S(1)} custom-call(s32[13]{0:T(128)S(1)} %pad_add_fusion.refs_0_, bf16[8,2,32,1024]{3,2,1,0:T(8,128)(2,1)} %all_to_all.30.refs_1_, bf16[256,1024]{1,0:T(8,128)(2,1)} %get-tuple-element.25.refs_2_, bf16[1024,2048]{1,0:T(8,128)(2,1)} %bitcast.38), custom_call_target="tpu_custom_call" | custom-call | flops 1073741824 | bytes 6815744 | tf_op jit(solution)/shard_map/pallas_call | solution.py:180
  165.2 4.2 %shard_map.121 = bf16[256,2048]{1,0:T(8,128)(2,1)S(1)} custom-call(s32[13]{0:T(128)S(1)} %pad_add_fusion.refs_0_, bf16[8,2,32,1024]{3,2,1,0:T(8,128)(2,1)} %all_to_all.30.refs_1_, bf16[256,1024]{1,0:T(8,128)(2,1)} %get-tuple-element.21.refs_22_.refs_2_, bf16[1024,2048]{1,0:T(8,128)(2,1)} %bitcast.39), custom_call_target="tpu_custom_call" | custom-call | flops 1073741824 | bytes 6815744 | tf_op jit(solution)/shard_map/pallas_call | solution.py:180
  171.4 15.0 %all-to-all-done.3.refs_1_ = bf16[8,2,32,1024]{3,2,1,0:T(8,128)(2,1)S(1)} async-done(((bf16[8,2,32,1024]{3,2,1,0:T(8,128)(2,1)}), bf16[8,2,32,1024]{3,2,1,0:T(8,128)(2,1)S(1)}, u32[]{:S(2)}, u32[]{:S(2)}) %all-to-all-start.3) | async-done | bytes 1048608 | tf_op jit(solution)/shard_map/all_to_all | solution.py:460
  187.5 4.2 %shard_map.124 = bf16[256,2048]{1,0:T(8,128)(2,1)S(1)} custom-call(s32[13]{0:T(128)S(1)} %pad_add_fusion.refs_0_, bf16[8,2,32,1024]{3,2,1,0:T(8,128)(2,1)} %copy-done.5, bf16[256,1024]{1,0:T(8,128)(2,1)} %get-tuple-element.26.refs_2_, bf16[1024,2048]{1,0:T(8,128)(2,1)} %bitcast.40), custom_call_target="tpu_custom_call" | custom-call | flops 1073741824 | bytes 6815744 | tf_op jit(solution)/shard_map/pallas_call | solution.py:180
  191.8 3.7 %collective-permute-done.10.refs_4_ = bf16[256,2048]{1,0:T(8,128)(2,1)S(1)} collective-permute-done((bf16[256,2048]{1,0:T(8,128)(2,1)S(1)}, bf16[256,2048]{1,0:T(8,128)(2,1)S(1)}, u32[]{:S(2)}, u32[]{:S(2)}) %collective-permute-start.10) | collective-permute-done | bytes 1048608 | tf_op jit(solution)/shard_map/ppermute | solution.py:450
  196.5 4.2 %shard_map.123 = bf16[256,2048]{1,0:T(8,128)(2,1)S(1)} custom-call(s32[13]{0:T(128)S(1)} %pad_add_fusion.refs_0_, bf16[8,2,32,1024]{3,2,1,0:T(8,128)(2,1)} %copy-done.5, bf16[256,1024]{1,0:T(8,128)(2,1)} %get-tuple-element.22.refs_23_.refs_2_, bf16[1024,2048]{1,0:T(8,128)(2,1)} %bitcast.41, bf16[256,2048]{1,0:T(8,128)(2,1)} %copy-done.7), custom_call_target="tpu_custom_call" | custom-call | flops 1073741824 | bytes 6815744 | tf_op jit(solution)/shard_map/pallas_call | solution.py:180
  202.5 31.4 %all_to_all.31 = bf16[8,32,2048]{2,1,0:T(8,128)(2,1)S(1)} all-to-all(bf16[8,32,2048]{2,1,0:T(8,128)(2,1)S(1)} %bitcast.44), channel_id=1, replica_groups=mesh['expert'=8,'context'=4] {'expert'}, dimensions={0} | all-to-all | bytes 2097152 | tf_op jit(solution)/shard_map/all_to_all | solution.py:460
  (81 shorter events, 22.4 us)
Async XLA Ops:
  3.1 33.1 %all-to-all-start = ((bf16[8,32,2048]{2,1,0:T(8,128)(2,1)}), bf16[8,32,2048]{2,1,0:T(8,128)(2,1)S(1)}, u32[]{:S(2)}, u32[]{:S(2)}) async-start(bf16[8,32,2048]{2,1,0:T(8,128)(2,1)} %bitcast.42), calls=%async_computation | async-start | bytes 2097152 | tf_op jit(solution)/shard_map/all_to_all | solution.py:460
  10.9 14.5 %copy-start.8 = (bf16[2048,16]{0,1:T(8,128)(2,1)}, bf16[2048,16]{0,1:T(8,128)(2,1)S(1)}, u32[]{:S(2)}) copy-start(bf16[2048,16]{0,1:T(8,128)(2,1)S(1)} %copy.17) | copy-start | bytes 196612
  10.9 4.3 %collective-permute-start.1 = (bf16[16,2048]{1,0:T(8,128)(2,1)S(1)}, bf16[16,2048]{1,0:T(8,128)(2,1)S(1)}, u32[]{:S(2)}, u32[]{:S(2)}) collective-permute-start(bf16[16,2048]{1,0:T(8,128)(2,1)S(1)} %bitcast.45), channel_id=1, source_target_pairs={{0,2},{1,3},{2,0},{3,1},{4,6},{5,7},{6,4},{7,5},{8,10},{9,11},{10,... | collective-permute-start | bytes 196616 | tf_op jit(solution)/shard_map/ppermute | solution.py:450
  12.5 13.0 %collective-permute-start = (bf16[16,2048]{1,0:T(8,128)(2,1)S(1)}, bf16[16,2048]{1,0:T(8,128)(2,1)S(1)}, u32[]{:S(2)}, u32[]{:S(2)}) collective-permute-start(bf16[16,2048]{1,0:T(8,128)(2,1)S(1)} %bitcast.46), channel_id=1, source_target_pairs={{0,1},{1,0},{2,3},{3,2},{4,5},{5,4},{6,7},{7,6},{8,9},{9,8},{10,11... | collective-permute-start | bytes 196616 | tf_op jit(solution)/shard_map/ppermute | solution.py:450
  15.2 10.2 %collective-permute-start.2 = (bf16[16,2048]{1,0:T(8,128)(2,1)S(1)}, bf16[16,2048]{1,0:T(8,128)(2,1)S(1)}, u32[]{:S(2)}, u32[]{:S(2)}) collective-permute-start(bf16[16,2048]{1,0:T(8,128)(2,1)S(1)} %collective-permute-done.1.refs_4_.refs_6_), channel_id=1, source_target_pairs={{0,1},{1,0},{2,3},{3,2},{4,5},{5,4},{6,7},{7,6},{8,9},{9,8},{10,11... | collective-permute-start | bytes 196616 | tf_op jit(solution)/shard_map/ppermute | solution.py:450
  25.5 10.7 %copy-start.10 = (bf16[16,2048]{1,0:T(8,128)(2,1)}, bf16[16,2048]{1,0:T(8,128)(2,1)S(1)}, u32[]{:S(2)}) copy-start(bf16[16,2048]{1,0:T(8,128)(2,1)S(1)} %collective-permute-done.refs_3_.refs_5_) | copy-start | bytes 196612
  36.2 8.8 %collective-permute-start.3 = (bf16[256,2048]{1,0:T(8,128)(2,1)S(1)}, bf16[256,2048]{1,0:T(8,128)(2,1)S(1)}, u32[]{:S(2)}, u32[]{:S(2)}) collective-permute-start(bf16[256,2048]{1,0:T(8,128)(2,1)S(1)} %shard_map.111.refs_1_), channel_id=1, source_target_pairs={{0,1},{1,0},{2,3},{3,2},{4,5},{5,4},{6,7},{7,6},{8,9},{9,8},{10,11... | collective-permute-start | bytes 3145736 | tf_op jit(solution)/shard_map/ppermute | solution.py:450
  36.3 25.6 %collective-permute-start.4 = (bf16[256,2048]{1,0:T(8,128)(2,1)S(1)}, bf16[256,2048]{1,0:T(8,128)(2,1)S(1)}, u32[]{:S(2)}, u32[]{:S(2)}) collective-permute-start(bf16[256,2048]{1,0:T(8,128)(2,1)S(1)} %shard_map.111.refs_1_), channel_id=1, source_target_pairs={{0,2},{1,3},{2,0},{3,1},{4,6},{5,7},{6,4},{7,5},{8,10},{9,11},{10,... | collective-permute-start | bytes 3145736 | tf_op jit(solution)/shard_map/ppermute | solution.py:450
  50.3 33.5 %all-to-all-start.1 = ((bf16[8,2,32,1152]{3,2,1,0:T(8,128)(2,1)}), bf16[8,2,32,1152]{3,2,1,0:T(8,128)(2,1)}, u32[]{:S(2)}, u32[]{:S(2)}) async-start(bf16[8,2,32,1152]{3,2,1,0:T(8,128)(2,1)} %shard_map.113.refs_1_), calls=%async_computation.1 | async-start | bytes 2359296 | tf_op jit(solution)/shard_map/all_to_all | solution.py:460
  61.9 2.7 %collective-permute-start.5 = (bf16[256,2048]{1,0:T(8,128)(2,1)S(1)}, bf16[256,2048]{1,0:T(8,128)(2,1)S(1)}, u32[]{:S(2)}, u32[]{:S(2)}) collective-permute-start(bf16[256,2048]{1,0:T(8,128)(2,1)S(1)} %shard_map.114.refs_1_), channel_id=1, source_target_pairs={{0,1},{1,0},{2,3},{3,2},{4,5},{5,4},{6,7},{7,6},{8,9},{9,8},{10,11... | collective-permute-start | bytes 3145736 | tf_op jit(solution)/shard_map/ppermute | solution.py:450
  70.0 17.6 %copy-start.16 = (f32[16]{0:T(128)S(1)}, f32[16]{0:T(128)}, u32[]{:S(2)}) copy-start(f32[16]{0:T(128)} %param.18) | copy-start | bytes 196
  70.0 17.8 %copy-start.18 = (f32[16]{0:T(128)S(1)}, f32[16]{0:T(128)}, u32[]{:S(2)}) copy-start(f32[16]{0:T(128)} %param.17) | copy-start | bytes 196
  70.0 17.8 %copy-start.17 = (f32[16]{0:T(128)S(1)}, f32[16]{0:T(128)}, u32[]{:S(2)}) copy-start(f32[16]{0:T(128)} %param.16) | copy-start | bytes 196
  70.0 17.8 %copy-start.14 = (f32[4,1024]{1,0:T(4,128)S(1)}, f32[4,1024]{1,0:T(4,128)}, u32[]{:S(2)}) copy-start(f32[4,1024]{1,0:T(4,128)} %param.19) | copy-start | bytes 49156
  70.1 17.8 %copy-start.15 = (f32[1024]{0:T(1024)S(1)}, f32[1024]{0:T(1024)}, u32[]{:S(2)}) copy-start(f32[1024]{0:T(1024)} %param.20) | copy-start | bytes 12292
  70.1 17.9 %copy-start.4 = (s32[1,512,1]{1,2,0:T(1,128)S(1)}, s32[1,512,1]{1,2,0:T(1,128)}, u32[]{:S(2)}) copy-start(s32[1,512,1]{1,2,0:T(1,128)} %param.12) | copy-start | bytes 6148
  83.8 29.6 %all-to-all-start.2 = ((bf16[8,2,32,1024]{3,2,1,0:T(8,128)(2,1)}), bf16[8,2,32,1024]{3,2,1,0:T(8,128)(2,1)S(1)}, u32[]{:S(2)}, u32[]{:S(2)}) async-start(bf16[8,2,32,1024]{3,2,1,0:T(8,128)(2,1)} %shard_map.115.refs_3_.refs_4_), calls=%async_computation.2 | async-start | bytes 2097152 | tf_op jit(solution)/shard_map/all_to_all | solution.py:460
  90.2 7.8 %collective-permute-start.7 = (bf16[128,256]{1,0:T(8,128)(2,1)}, bf16[128,256]{1,0:T(8,128)(2,1)S(1)}, u32[]{:S(2)}, u32[]{:S(2)}) collective-permute-start(bf16[128,256]{1,0:T(8,128)(2,1)} %shard_map.116), channel_id=1, source_target_pairs={{0,2},{1,3},{2,0},{3,1},{4,6},{5,7},{6,4},{7,5},{8,10},{9,11},{10,... | collective-permute-start | bytes 196616 | tf_op jit(solution)/shard_map/ppermute | solution.py:450
  98.0 7.8 %collective-permute-start.6 = (bf16[128,256]{1,0:T(8,128)(2,1)S(1)}, bf16[128,256]{1,0:T(8,128)(2,1)S(1)}, u32[]{:S(2)}, u32[]{:S(2)}) collective-permute-start(bf16[128,256]{1,0:T(8,128)(2,1)S(1)} %copy-done.12), channel_id=1, source_target_pairs={{0,1},{1,0},{2,3},{3,2},{4,5},{5,4},{6,7},{7,6},{8,9},{9,8},{10,11... | collective-permute-start | bytes 196616 | tf_op jit(solution)/shard_map/ppermute | solution.py:450
  98.1 7.7 %collective-permute-start.8 = (bf16[128,256]{1,0:T(8,128)(2,1)S(1)}, bf16[128,256]{1,0:T(8,128)(2,1)S(1)}, u32[]{:S(2)}, u32[]{:S(2)}) collective-permute-start(bf16[128,256]{1,0:T(8,128)(2,1)S(1)} %collective-permute-done.7), channel_id=1, source_target_pairs={{0,1},{1,0},{2,3},{3,2},{4,5},{5,4},{6,7},{7,6},{8,9},{9,8},{10,11... | collective-permute-start | bytes 196616 | tf_op jit(solution)/shard_map/ppermute | solution.py:450
  157.2 29.2 %all-to-all-start.3 = ((bf16[8,2,32,1024]{3,2,1,0:T(8,128)(2,1)}), bf16[8,2,32,1024]{3,2,1,0:T(8,128)(2,1)S(1)}, u32[]{:S(2)}, u32[]{:S(2)}) async-start(bf16[8,2,32,1024]{3,2,1,0:T(8,128)(2,1)} %get-tuple-element.23), calls=%async_computation.3 | async-start | bytes 2097152 | tf_op jit(solution)/shard_map/all_to_all | solution.py:460
  165.1 4.3 %collective-permute-start.9 = (bf16[256,2048]{1,0:T(8,128)(2,1)S(1)}, bf16[256,2048]{1,0:T(8,128)(2,1)S(1)}, u32[]{:S(2)}, u32[]{:S(2)}) collective-permute-start(bf16[256,2048]{1,0:T(8,128)(2,1)S(1)} %shard_map.122), channel_id=1, source_target_pairs={{0,1},{1,0},{2,3},{3,2},{4,5},{5,4},{6,7},{7,6},{8,9},{9,8},{10,11... | collective-permute-start | bytes 3145736 | tf_op jit(solution)/shard_map/ppermute | solution.py:450
  169.9 25.6 %collective-permute-start.10 = (bf16[256,2048]{1,0:T(8,128)(2,1)S(1)}, bf16[256,2048]{1,0:T(8,128)(2,1)S(1)}, u32[]{:S(2)}, u32[]{:S(2)}) collective-permute-start(bf16[256,2048]{1,0:T(8,128)(2,1)S(1)} %add_convert_fusion.1), channel_id=1, source_target_pairs={{0,2},{1,3},{2,0},{3,1},{4,6},{5,7},{6,4},{7,5},{8,10},{9,11},{10,... | collective-permute-start | bytes 3145736 | tf_op jit(solution)/shard_map/ppermute | solution.py:450
  191.7 9.0 %collective-permute-start.11 = (bf16[256,2048]{1,0:T(8,128)(2,1)S(1)}, bf16[256,2048]{1,0:T(8,128)(2,1)S(1)}, u32[]{:S(2)}, u32[]{:S(2)}) collective-permute-start(bf16[256,2048]{1,0:T(8,128)(2,1)S(1)} %shard_map.124), channel_id=1, source_target_pairs={{0,1},{1,0},{2,3},{3,2},{4,5},{5,4},{6,7},{7,6},{8,9},{9,8},{10,11... | collective-permute-start | bytes 3145736 | tf_op jit(solution)/shard_map/ppermute | solution.py:450
  (11 other events, 69.8 us)
where the time goes:
time: 237 us; the launch traced here: 236 us
  Pallas kernels  74.3 us (31%)
  blocking collectives  63.2 us (27%)
  waiting for transfers between devices  55.9 us (24%)
  starting transfers between devices  25 us (11%)
  local copies, waits for them, and re-layouts  14 us (6%)
  other arithmetic  3.02 us (1%)
    pallas_call x14, Pallas kernels, call(): pl.pallas_call(body, out_shape=[(pltpu.HBM if pieces else pltpu.VMEM)(o.s...  74.3 us
    all_to_all x2, blocking collectives, exchange(): lax.all_to_all(value, 'expert', split_axis=0, concat_axis=0, tiled=True)  63.2 us
    all_to_all x4, waiting for transfers between devices, exchange(): lax.all_to_all(value, 'expert', split_axis=0, concat_axis=0, tiled=True)  39.5 us
    all_to_all x4, starting transfers between devices, exchange(): lax.all_to_all(value, 'expert', split_axis=0, concat_axis=0, tiled=True)  18.9 us
    ppermute x12, waiting for transfers between devices, permute(): return lax.ppermute(value, 'context', pairs)  16.4 us
    unnamed x40, local copies, waits for them, and re-layouts  13.5 us
    ppermute x12, starting transfers between devices, permute(): return lax.ppermute(value, 'context', pairs)  6.04 us
  transfers between devices with their start and end apart: 16, of which 7 were waited for; matrix products, arithmetic and copies ran while one was open for 5% of the time, Pallas kernels for 25%

commit v1 on v0

--- a/solution.py
+++ b/solution.py
@@ -28,19 +28,20 @@
     return pieces.reshape(count * rows, lanes)
 
 
-def slot_rows(ids, experts, cap):
+def slot_rows(ids, experts, cap, me=0):
     tok_rows = ids.shape[1]
     onehot = jnp.where(iota((experts, tok_rows), 0) == ids, 1.0, 0.0)
     upto = jnp.where(iota((tok_rows, tok_rows), 0) <= iota((tok_rows, tok_rows), 1), 1.0, 0.0)
     before = dot(onehot.astype(BF16), upto.astype(BF16))
     rank = jnp.sum(onehot * before, axis=0, keepdims=True) - 1.0
-    slot = ids * cap + rank.astype(jnp.int32)
+    slot = (ids ^ me) * cap + rank.astype(jnp.int32)
     return jnp.where(iota((experts * cap, tok_rows), 0) == slot, 1.0, 0.0)
 
 
 VMEM = pl.BlockSpec(memory_space=pltpu.VMEM)
 SMEM = pl.BlockSpec(memory_space=pltpu.SMEM)
 HBM = pl.BlockSpec(memory_space=pltpu.HBM)
+ANY = pl.BlockSpec(memory_space=pl.ANY)
 
 
 class Stream:
@@ -108,17 +109,8 @@
     return (array, array.shape, [(t, t) for t in range(array.shape[0])])
 
 
-def columns(array, start, count, tile):
-    cuts = [
-        ((slice(None), pl.ds(start + lo, tile)), (slice(None), pl.ds(lo, tile)))
-        for lo in range(0, count, tile)
-    ]
-    return (array, (array.shape[0], count), cuts)
-
-
-def place_of(array, at):
-    held = (array.shape[0], *array.shape[2:])
-    return (array, held, [((slice(None), at), Ellipsis)])
+def columns(array, start, count):
+    return (array, (array.shape[0], count), [((slice(None), pl.ds(start, count)), Ellipsis)])
 
 
 def call(
@@ -176,14 +168,15 @@
             result.finish()
 
     arrays = [in_hbm(a) if pieces else in_vmem(a) for a, _, pieces in big]
-    arrays += [in_hbm(array) for array in after] + ([in_hbm(alias)] if alias is not None else [])
+    arrays += list(after) + ([in_hbm(alias)] if alias is not None else [])
     return pl.pallas_call(
         body,
         out_shape=[(pltpu.HBM if pieces else pltpu.VMEM)(o.shape, o.dtype) for o, pieces in outs],
         in_specs=[SMEM]
         + [VMEM] * len(small)
         + [HBM if pieces else VMEM for _, _, pieces in big]
-        + [HBM] * (len(after) + (alias is not None)),
+        + [ANY] * len(after)
+        + [HBM] * (alias is not None),
         out_specs=[HBM if pieces else VMEM for _, pieces in outs],
         scratch_shapes=held + list(scratch),
         input_output_aliases={len(small) + len(arrays): 0} if alias is not None else {},
@@ -196,15 +189,40 @@
     return jax.ShapeDtypeStruct(dims, BF16)
 
 
-def tie(value, *after):
+def tie(values, *after, hbm=False):
+    count = len(values)
+    space, spec, pin = (pltpu.HBM, HBM, in_hbm) if hbm else (pltpu.VMEM, VMEM, in_vmem)
     return pl.pallas_call(
         lambda *refs: None,
-        out_shape=pltpu.VMEM(value.shape, value.dtype),
-        in_specs=[VMEM] + [HBM] * len(after),
+        out_shape=[space(value.shape, value.dtype) for value in values],
+        in_specs=[spec] * count + [ANY] * len(after),
+        out_specs=[spec] * count,
+        input_output_aliases={i: i for i in range(count)},
+        compiler_params=pltpu.CompilerParams(vmem_limit_bytes=4 << 20),
+    )(*(pin(value) for value in values), *after)
+
+
+def staged(array, start, count, after):
+    def body(source, _, target, sem):
+        copy = pltpu.make_async_copy(source.at[:, pl.ds(start, count)], target, sem)
+        copy.start()
+        copy.wait()
+
+    return pl.pallas_call(
+        body,
+        out_shape=pltpu.VMEM((array.shape[0], count), array.dtype),
+        in_specs=[HBM, ANY],
         out_specs=VMEM,
-        input_output_aliases={0: 0},
+        scratch_shapes=[pltpu.SemaphoreType.DMA],
         compiler_params=pltpu.CompilerParams(vmem_limit_bytes=4 << 20),
-    )(in_vmem(value), *(in_hbm(array) for array in after))
+        cost_estimate=pl.CostEstimate(
+            flops=0, bytes_accessed=4 * array.shape[0] * count, transcendentals=0
+        ),
+    )(in_hbm(array), after)
+
+
+def peer_rows(ref, me):
+    return flat_rows(jnp.stack([ref[r ^ me] for r in range(ref.shape[0])]))
 
 
 def dispatch_kernel(experts, cap, info_ref, ids, tokens, out):
@@ -230,10 +248,11 @@
 
 def project_rows(places, experts, cap, rows, weight, out, tile):
     chans = weight.held.shape[1]
+    rows = [flat_rows(block.whole()[...]) for block in rows]
     for lo in range(0, chans, tile):
-        part = weight.piece(lo // tile)[:, lo : lo + tile]
+        part = weight.whole()[:, lo : lo + tile]
         for at, block in zip(places, rows):
-            store_rows(out, at, lo, dot(block.whole()[...], part), experts, cap)
+            store_rows(out, at, lo, dot(block, part), experts, cap)
         out.send(lo // tile)
 
 
@@ -247,7 +266,7 @@
     steps, out = refs[:-1], refs[-1]
     chans = weight.held.shape[1]
     project_rows([0], experts, cap, [rows], weight, out, tile)
-    first = rows.whole()[...]
+    first = flat_rows(rows.whole()[...])
     store_rows(out, 0, chans, dot(first, states.whole()[...]), experts, cap)
     steps = [ref.whole()[...].astype(F32) for ref in steps]
     spare = LANES - sum(part.shape[0] for part in steps)
@@ -263,23 +282,49 @@
     project_rows(places, experts, cap, rows, weight, out, tile)
 
 
-def gate_kernel(tile, info_ref, *refs):
-    count = len(refs) // 2
-    rows, weight, outs = refs[:count], refs[count], refs[count + 1 :]
+def peers_kernel(places, experts, cap, tile, info_ref, *refs):
+    weight, outs = refs[places], refs[places + 1 :]
+    me = info_ref[info_ref.shape[0] - 1]
+    rows = [peer_rows(ref.whole(), me) for ref in refs[:places]]
     for lo in range(0, weight.held.shape[1], tile):
-        for block, out in zip(rows, outs):
-            made = dot(block.whole()[...], weight.piece(lo // tile)[:, lo : lo + tile])
-            out.held[:, lo : lo + tile] = made.astype(BF16)
+        part = weight.whole()[:, lo : lo + tile]
+        for at in range(places):
+            made = dot(rows[at], part).astype(BF16)
+            for r in range(experts):
+                outs[r].held[at, :, lo : lo + tile] = made[r * cap : (r + 1) * cap, :]
     for out in outs:
         out.send(0)
 
 
-def output_kernel(tile, info_ref, scanned, gate, weight, out):
+def gate_kernel(tile, by_peer, info_ref, *refs):
+    count = len(refs) // 2
+    weight, outs = refs[count], refs[count + 1 :]
+    if by_peer:
+        rows = [peer_rows(ref.whole(), info_ref[info_ref.shape[0] - 1]) for ref in refs[:count]]
+    else:
+        rows = [flat_rows(ref.whole()[...]) for ref in refs[:count]]
+    for lo in range(0, weight.held.shape[1], tile):
+        part = weight.whole()[:, lo : lo + tile]
+        for block, out in zip(rows, outs):
+            out.held[:, lo : lo + tile] = dot(block, part).astype(BF16)
+    for out in outs:
+        out.send(0)
+
+
+def output_kernel(at, experts, cap, tile, info_ref, *refs):
+    scanned, gate, weight, out = refs[:-3], refs[-3], refs[-2].held, refs[-1].held
+    if len(scanned) > 1:
+        me = info_ref[info_ref.shape[0] - 1]
+        rows = flat_rows(jnp.stack([ref.held[at] for ref in scanned]))
+    else:
+        me = 0
+        rows = flat_rows(scanned[0].held[:, at])
     gates = jax.nn.silu(gate.whole()[...].astype(F32))
-    gated = (flat_rows(scanned.whole()[...]).astype(F32) * gates).astype(BF16)
-    for lo in range(0, weight.held.shape[1], tile):
-        part = weight.piece(lo // tile)[:, lo : lo + tile]
-        out.held[:, lo : lo + tile] = dot(gated, part).astype(BF16)
+    gated = (rows.astype(F32) * gates).astype(BF16)
+    for lo in range(0, weight.shape[1], tile):
+        made = dot(gated, weight[:, lo : lo + tile]).astype(BF16)
+        for r in range(experts):
+            out[r ^ me, :, lo : lo + tile] = made[r * cap : (r + 1) * cap, :]
 
 
 def factors_kernel(cfg, info_ref, ids_ref, head_ref, near, side, weights, kept, tail, last, placed):
@@ -345,11 +390,13 @@
     chan_ref,
     side,
     placed,
-    far,
     *refs,
 ):
     experts, cap, tok_rows, nstate, chn, heads = cfg
-    out_near, out_far, inner_ref, made_ref = refs[-4:]
+    far, refs = refs[:experts], refs[experts:]
+    weights, kept, tail, last = refs[:4]
+    out_near, (out_far, inner_ref, made_ref) = refs[4 : 4 + experts], refs[4 + experts :]
+    me = info_ref[info_ref.shape[0] - 1]
     blocks = ids_ref.shape[0]
     taps = 4
     inner_ref[:8, :] = jnp.zeros((8, chn), F32)
@@ -360,15 +407,15 @@
         if q < 2:
             inner_ref[at, :] = placed.whole()[q].astype(F32)
         else:
-            place = slot_rows(ids_ref[b], experts, cap).T.astype(BF16)
-            inner_ref[at, :] = dot(place, flat_rows(far.whole()[:, q - 2]))
+            place = slot_rows(ids_ref[b], experts, cap, me).T.astype(BF16)
+            rows = jnp.stack([far[r].whole()[q - 2] for r in range(experts)])
+            inner_ref[at, :] = dot(place, flat_rows(rows))
 
     first = iota((tok_rows, LANES), 1) < HEAD_DIM
     state = jnp.zeros((nstate, chn), F32)
     side_ref = side.whole()
     for b in range(blocks):
         q = info_ref[1 + blocks + b]
-        weights, kept, tail, last = refs[4 * b : 4 * b + 4]
         total = chan_ref[taps : taps + 1, :]
         for j in range(taps):
             start = 8 + b * tok_rows - (taps - 1) + j
@@ -380,10 +427,10 @@
         rest = chan_ref[taps + 1 : taps + 2, :] * signal
         if b > 0:
             carried = dot(both[:, nstate:], state.astype(BF16))
-            rest = rest + carried * kept.whole()[0].astype(F32)
+            rest = rest + carried * kept.held[b].astype(F32)
         if b < blocks - 1:
-            added = dot(keys_t, (signal * tail.whole()[0].astype(F32)).astype(BF16))
-            state = last.whole()[0, 7:8, :] * state + added
+            added = dot(keys_t, (signal * tail.held[b].astype(F32)).astype(BF16))
+            state = last.held[b, 7:8, :] * state + added
 
         for pair in range(heads // 2):
             lanes = slice(pair * LANES, (pair + 1) * LANES)
@@ -391,23 +438,20 @@
             values = jnp.concatenate(
                 [jnp.where(first, values, 0.0), jnp.where(first, 0.0, values)], axis=0
             ).astype(BF16)
-            local = dot(weights.whole()[0, pair], values)
+            local = dot(weights.held[b, pair], values)
             made_ref[b * tok_rows : (b + 1) * tok_rows, lanes] = (rest[:, lanes] + local).astype(BF16)
 
     for q in range(blocks - 1, -1, -1):
         b = info_ref[1 + q]
-        place = slot_rows(ids_ref[b], experts, cap).astype(BF16)
+        place = slot_rows(ids_ref[b], experts, cap, me if q < 2 else 0).astype(BF16)
         start = pl.multiple_of(b * tok_rows, tok_rows)
         leaving = dot(place, made_ref[pl.ds(start, tok_rows), :]).astype(BF16)
         for e in range(experts):
             piece = leaving[e * cap : (e + 1) * cap, :]
             if q < 2:
-                out_near.held[e, q] = piece
+                out_near[e].held[q] = piece
             else:
                 out_far.held[e, q - 2] = piece
-        if q == 2:
-            out_far.send(0)
-    out_near.send(0)
 
 
 def per_device(
@@ -439,7 +483,8 @@
     order = 2 * ((here // 2 - blocks // 2) % chips) + ((here % 2) ^ (blocks % 2))
     groups = 2 * ((blocks // 2 - here // 2) % chips) + ((here % 2) ^ (blocks % 2))
     block_at = 2 * ((here // 2 - blocks // 2) % chips) + ((here % 2) ^ (blocks % 2))
-    info = jnp.concatenate([here[None], block_at, order, groups])
+    me = lax.axis_index("expert").astype(jnp.int32)
+    info = jnp.concatenate([here[None], block_at, order, groups, me[None]])
     ids = route.reshape(shards, 1, tok_rows)
     swap = [(c, c ^ 1) for c in range(shards)]
 
@@ -459,6 +504,13 @@
     def exchange(value):
         return lax.all_to_all(value, "expert", split_axis=0, concat_axis=0, tiled=True)
 
+    def exchange_peers(pieces):
+        sent = [
+            lax.ppermute(pieces[r], "expert", [(e, e ^ r) for e in range(experts)])
+            for r in range(experts - 1, 0, -1)
+        ]
+        return [pieces[0]] + sent[::-1]
+
     w_flat = w_inner[0].reshape(width, 2 * chans)
 
     once = [Ellipsis]
@@ -467,9 +519,10 @@
         info, [full(ids), full(tokens[0])], [(shape(slots, width), once)],
         flops=2 * slots * tok_rows * width,
     )[0]
-    own = exchange(outgoing.reshape(experts, cap, width)).reshape(slots, width)
-    steps = spread(tie(w_step[0], outgoing).T)
-    own = tie(own, w_flat, *steps)
+    own = exchange(outgoing.reshape(experts, cap, width))
+    steps = spread(tie([w_step[0]], outgoing)[0].T)
+    own = tie([own], w_flat, *steps)[0]
+    w_in = staged(w_flat, chans, chans, own)
     swapped = permute(own, swap)
     everything = (slice(None),) * 3
 
@@ -482,7 +535,7 @@
     own_part = call(
         functools.partial(own_kernel, experts, cap, 256),
         info,
-        [kept_in_vmem(own), columns(w_flat, chans, chans, 256), full(w_state[0])]
+        [kept_in_vmem(own), kept_in_vmem(w_in), full(w_state[0])]
         + [full(part) for part in steps],
         [(near_shape, inner_cuts(0, 1))],
         flops=2 * slots * width * (chans + 2 * LANES),
@@ -490,24 +543,39 @@
     near = call(
         functools.partial(project_kernel, [1], experts, cap, 256),
         info,
-        [kept_in_vmem(swapped), columns(w_flat, chans, chans, 256)],
+        [kept_in_vmem(swapped), kept_in_vmem(w_in)],
         [(near_shape, inner_cuts(1, 0))],
         alias=own_part,
         flops=2 * slots * width * chans,
     )[0]
     distant = []
     for k in range(1, chips):
-        arrived = tie(permute(own, hop(k)), near)
+        arrived = tie([permute(own, hop(k))], near, hbm=True)[0]
         distant += [arrived, permute(arrived, swap)]
     far = call(
-        functools.partial(project_kernel, range(far_count), experts, cap, 256),
+        functools.partial(peers_kernel, far_count, experts, cap, 256),
         info,
-        [kept_in_vmem(rows) for rows in distant] + [columns(w_flat, chans, chans, 256)],
-        [(shape(experts, far_count, cap, chans), inner_cuts(slice(None), 0))],
+        [full(rows) for rows in distant] + [columns(w_flat, chans, chans)],
+        [(shape(far_count, cap, chans), once)] * experts,
         flops=2 * far_count * slots * width * chans,
-    )[0]
+    )
     near_back = exchange(near)
-    far_back = exchange(far)
+    far_back = exchange_peers(far)
+
+    def gates(rows, by_peer):
+        return call(
+            functools.partial(gate_kernel, 256, by_peer),
+            info,
+            [kept_in_vmem(part) if by_peer else full(part) for part in rows]
+            + [columns(w_flat, 0, chans)],
+            [(shape(slots, chans), once)] * len(rows),
+            after=[near],
+            flops=2 * len(rows) * slots * width * chans,
+        )
+
+    gate_near = gates([own, swapped], True)
+    gate_far = gates(distant, False)
+    out_weight = staged(w_out[0], 0, width, near_back)
 
     lanes = everything + (pl.ds(chans, LANES),)
     side = call(
@@ -516,7 +584,7 @@
         [(near_back, (experts, 2, cap, LANES), [(lanes, Ellipsis)])],
         [(shape(tok_rows, 2 * LANES), once)],
         small=[ids],
-        after=[far],
+        after=[far[0], gate_near[0], gate_far[0]],
         flops=2 * slots * tok_rows * 2 * LANES,
     )[0]
     sides = jnp.stack(spread(side))
@@ -531,49 +599,32 @@
         [conv_weight, conv_bias[None, :], jnp.repeat(skip_gain, HEAD_DIM)[None, :]]
     )
     chan_rows = jnp.pad(chan_rows, ((0, 2), (0, 0)))
-    def gates(rows):
-        return call(
-            functools.partial(gate_kernel, 256),
-            info,
-            [full(part) for part in rows] + [columns(w_flat, 0, chans, 256)],
-            [(shape(slots, chans), once)] * len(rows),
-            after=[far],
-            flops=2 * len(rows) * slots * width * chans,
-        )
-
-    gate_far = gates(distant)
-    gate_near = gates([own, swapped])
     cfg = (experts, cap, tok_rows, nstate, chans, heads)
     each = list(range(shards))
     weights, kept, tail, last, placed = call(
         functools.partial(factors_kernel, cfg),
-        info, [full(near_back), full(sides)],
+        info, [full(near_back), kept_in_vmem(sides)],
         [
-            (shape(shards, heads // 2, tok_rows, 2 * tok_rows), each),
-            (shape(shards, tok_rows, chans), each),
-            (shape(shards, tok_rows, chans), each),
-            (jax.ShapeDtypeStruct((shards, 8, chans), F32), each),
-            (shape(2, tok_rows, chans), once),
+            (shape(shards, heads // 2, tok_rows, 2 * tok_rows), None),
+            (shape(shards, tok_rows, chans), None),
+            (shape(shards, tok_rows, chans), None),
+            (jax.ShapeDtypeStruct((shards, 8, chans), F32), None),
+            (shape(2, tok_rows, chans), None),
         ],
         small=[ids, head_rows],
         flops=2 * tok_rows * chans * (2 * slots + shards * 512),
         exps=shards * tok_rows * tok_rows * heads,
     )
-    in_turn = [
-        (array, (1, *array.shape[1:]), [(pl.ds(b, 1), Ellipsis)])
-        for b in range(shards)
-        for array in (weights, kept, tail, last)
-    ]
-    near_out, far_out = call(
+    *near_out, far_out = call(
         functools.partial(scan_kernel, cfg),
         info,
-        [full(sides), full(placed), full(far_back)] + in_turn,
-        [
-            (shape(experts, 2, cap, chans), None),
-            (shape(experts, far_count, cap, chans), None),
-        ],
+        [kept_in_vmem(sides), kept_in_vmem(placed)]
+        + [full(piece) for piece in far_back]
+        + [kept_in_vmem(array) for array in (weights, kept, tail, last)],
+        [(shape(2, cap, chans), None)] * experts
+        + [(shape(experts, far_count, cap, chans), None)],
         small=[ids, chan_rows],
-        after=[gate_far[0], gate_near[0]],
+        after=[gate_far[0], gate_near[0], out_weight],
         scratch=[
             pltpu.VMEM((8 + shards * tok_rows, chans), F32),
             pltpu.VMEM((shards * tok_rows, chans), BF16),
@@ -581,30 +632,29 @@
         flops=2 * shards * tok_rows * chans * (2 * slots + 2 * nstate + 2 * tok_rows),
     )
     far_ret = exchange(far_out)
-    near_ret = exchange(near_out)
-
-    def output(scanned, at, after=()):
-        gate = (gate_near + gate_far)[at]
+    near_ret = exchange_peers(tie(near_out, far_ret))
+
+    def output(scanned, gate, at, after=()):
         return call(
-            functools.partial(output_kernel, 512),
+            functools.partial(output_kernel, at, experts, cap, 512),
             info,
-            [place_of(scanned, at % 2 if at < 2 else at - 2), full(gate), columns(w_out[0], 0, width, 512)],
-            [(shape(slots, width), None)],
+            [kept_in_vmem(part) for part in scanned] + [full(gate), kept_in_vmem(out_weight)],
+            [(shape(experts, cap, width), None)],
             after=after,
             flops=2 * slots * width * chans,
         )[0]
 
     hopped = []
-    others = [permute(output(far_ret, 2 * k + 1), swap) for k in range(1, chips)]
+    others = [permute(output([far_ret], gate_far[2 * k - 1], 2 * k - 1), swap) for k in range(1, chips)]
     for k in range(1, chips):
-        pair = output(far_ret, 2 * k).astype(F32) + others[k - 1].astype(F32)
+        pair = output([far_ret], gate_far[2 * k - 2], 2 * k - 2).astype(F32) + others[k - 1].astype(F32)
         hopped.append(permute(pair.astype(BF16), hop(chips - k)))
-    part_swap = permute(output(near_ret, 1), swap)
-    part_own = output(near_ret, 0, hopped)
+    part_swap = permute(output(near_ret, gate_near[1], 1), swap)
+    part_own = output(near_ret, gate_near[0], 0, hopped)
     summed = part_own.astype(F32) + part_swap.astype(F32)
     for part in hopped:
         summed = summed + part.astype(F32)
-    returned = exchange(summed.astype(BF16).reshape(experts, cap, width)).reshape(slots, width)
+    returned = exchange(summed.astype(BF16)).reshape(slots, width)
     result = call(
         functools.partial(collect_kernel, experts, cap),
         info, [kept_in_vmem(returned)], [(shape(tok_rows, width), once)],

time: 237 us -> 239 us (level)
  starting transfers between devices: 25 us -> 39.9 us
  waiting for transfers between devices: 55.9 us -> 47.2 us
  Pallas kernels: 74.3 us -> 66.8 us
  local copies, waits for them, and re-layouts: 14 us -> 21 us
  blocking collectives: 63.2 us -> 60.1 us
    all_to_all x4 -> x2, waiting for transfers between devices: 39.5 us -> 10.7 us  [exchange(): lax.all_to_all(value, 'expert', split_axis=0, concat_axis=0, tiled=True)]
    ppermute x0 -> x14, starting transfers between devices: none -> 22.2 us  [exchange_peers(): lax.ppermute(pieces[r], 'expert', [(e, e ^ r) for e in range(experts)])]
    ppermute x0 -> x14, waiting for transfers between devices: none -> 13.3 us  [exchange_peers(): lax.ppermute(pieces[r], 'expert', [(e, e ^ r) for e in range(experts)])]
    pallas_call x14, Pallas kernels: 74.3 us -> 62.4 us  [call(): pl.pallas_call(body, out_shape=[(pltpu.HBM if pieces else pltpu.VMEM)(o.s...]
    all_to_all x4 -> x2, starting transfers between devices: 18.9 us -> 11.3 us  [exchange(): lax.all_to_all(value, 'expert', split_axis=0, concat_axis=0, tiled=True)]
    ppermute x12, waiting for transfers between devices: 16.4 us -> 23.3 us  [permute(): return lax.ppermute(value, 'context', pairs)]
    unnamed x40 -> x66, local copies, waits for them, and re-layouts: 13.5 us -> 20 us
    pallas_call x3 -> x6, Pallas kernels: 0.01 us -> 4.46 us  [the longest x2 4.45 us: staged(): pl.pallas_call(body, out_shape=pltpu.VMEM((array.shape[0], count), array....]
  transfers between devices with their start and end apart: 16 -> 28, of which waited for: 7 -> 10; matrix products, arithmetic and copies ran while one was open for 5% -> 5% of each run, Pallas kernels for 25% -> 21%
where the time goes in v1:
time: 239 us; the launch traced here: 238 us
  Pallas kernels  66.8 us (28%)
  blocking collectives  60.1 us (25%)
  waiting for transfers between devices  47.2 us (20%)
  starting transfers between devices  39.9 us (17%)
  local copies, waits for them, and re-layouts  21 us (9%)
    pallas_call x14, Pallas kernels, call(): pl.pallas_call(body, out_shape=[(pltpu.HBM if pieces else pltpu.VMEM)(o.s...  62.4 us
    all_to_all x2, blocking collectives, exchange(): lax.all_to_all(value, 'expert', split_axis=0, concat_axis=0, tiled=True)  60.1 us
    ppermute x12, waiting for transfers between devices, permute(): return lax.ppermute(value, 'context', pairs)  23.3 us
    ppermute x14, starting transfers between devices, exchange_peers(): lax.ppermute(pieces[r], 'expert', [(e, e ^ r) for e in range(experts)])  22.2 us
    unnamed x66, local copies, waits for them, and re-layouts  20 us
    ppermute x14, waiting for transfers between devices, exchange_peers(): lax.ppermute(pieces[r], 'expert', [(e, e ^ r) for e in range(experts)])  13.3 us
    all_to_all x2, starting transfers between devices, exchange(): lax.all_to_all(value, 'expert', split_axis=0, concat_axis=0, tiled=True)  11.3 us
    all_to_all x2, waiting for transfers between devices, exchange(): lax.all_to_all(value, 'expert', split_axis=0, concat_axis=0, tiled=True)  10.7 us
  transfers between devices with their start and end apart: 28, of which 10 were waited for; matrix products, arithmetic and copies ran while one was open for 5% of the time, Pallas kernels for 21%

profile of v1, /device:TPU:0, one launch (start us, length us, event | category | flops | bytes accessed | tf_op | source)
XLA Modules:
  0.0 237.6 jit_solution(3583613731419180801)
XLA Ops:
  0.1 3.0 %shard_map.109.refs_1_ = bf16[256,2048]{1,0:T(8,128)(2,1)} custom-call(s32[14]{0:T(128)S(1)} %concatenate.9.refs_0_, s32[4,1,128]{2,1,0:T(1,128)} %bitcast.35, bf16[128,2048]{1,0:T(8,128)(2,1)} %bitcast.43), custom_call_target="tpu_custom_call" | custom-call | flops 134217728 | bytes 1573888 | tf_op jit(solution)/shard_map/pallas_call | solution.py:172
  3.1 7.4 %all-to-all-start = ((bf16[8,32,2048]{2,1,0:T(8,128)(2,1)}), bf16[8,32,2048]{2,1,0:T(8,128)(2,1)S(1)}, u32[]{:S(2)}, u32[]{:S(2)}) async-start(bf16[8,32,2048]{2,1,0:T(8,128)(2,1)} %bitcast.28), calls=%async_computation | async-start | bytes 2097152 | tf_op jit(solution)/shard_map/all_to_all | solution.py:505
  15.4 10.2 %copy.26 = bf16[256,8,2,1024]{3,1,2,0:T(8,128)(2,1)} copy(bf16[256,8,2,1024]{3,2,1,0:T(2,128)(2,1)} %bitcast.40) | data formatting | bytes 16777216
  25.6 10.7 %all-to-all-done.refs_0_ = bf16[8,32,2048]{2,1,0:T(8,128)(2,1)S(1)} async-done(((bf16[8,32,2048]{2,1,0:T(8,128)(2,1)}), bf16[8,32,2048]{2,1,0:T(8,128)(2,1)S(1)}, u32[]{:S(2)}, u32[]{:S(2)}) %all-to-all-start) | async-done | bytes 1048608 | tf_op jit(solution)/shard_map/all_to_all | solution.py:505
  36.3 3.4 %copy-done = bf16[256,8,2,1024]{3,1,2,0:T(8,128)(2,1)S(1)} copy-done((bf16[256,8,2,1024]{3,1,2,0:T(8,128)(2,1)S(1)}, bf16[256,8,2,1024]{3,1,2,0:T(8,128)(2,1)}, u32[]{:S(2)}) %copy-start) | copy-done | bytes 8388632
  43.5 5.9 %shard_map.113.refs_3_ = bf16[8,2,32,1152]{3,2,1,0:T(8,128)(2,1)} custom-call(s32[14]{0:T(128)S(1)} %concatenate.9.refs_0_, bf16[8,32,2048]{2,1,0:T(8,128)(2,1)S(1)} %shard_map.111._.refs_1_, bf16[2048,1024]{1,0:T(8,128)(2,1)S(1)} %shard_map.112.refs_2_, bf16[2048,128]{1,0:T(8,128)(2,1)} %bitcast.42, bf16[16,2048]{1,0:T(8,128)(2,1)} %bitcast.34, ...), custom_call_target="tpu_custom_call" | custom-call | flops 1342177280 | bytes 7208960 | tf_op jit(solution)/shard_map/pallas_call | solution.py:172
  49.4 4.0 %shard_map.114.refs_1_.refs_4_ = bf16[8,2,32,1152]{3,2,1,0:T(8,128)(2,1)} custom-call(s32[14]{0:T(128)S(1)} %concatenate.9.refs_0_, bf16[8,32,2048]{2,1,0:T(8,128)(2,1)S(1)} %collective-permute-done.3.refs_1_.refs_2_, bf16[2048,1024]{1,0:T(8,128)(2,1)S(1)} %shard_map.112.refs_2_, ...), custom_call_target="tpu_custom_call", output_to_operand_aliasing={{}: (3, {})} | custom-call | flops 1073741824 | bytes 6422528 | tf_op jit(solution)/shard_map/pallas_call | solution.py:172
  54.4 3.9 %all-to-all-start.1 = ((bf16[8,2,32,1152]{3,2,1,0:T(8,128)(2,1)}), bf16[8,2,32,1152]{3,2,1,0:T(8,128)(2,1)S(1)}, u32[]{:S(2)}, u32[]{:S(2)}) async-start(bf16[8,2,32,1152]{3,2,1,0:T(8,128)(2,1)} %shard_map.114.refs_1_.refs_4_), calls=%async_computation.1 | async-start | bytes 2359296 | tf_op jit(solution)/shard_map/all_to_all | solution.py:505
  58.3 7.1 %collective-permute-done.4.refs_0_ = bf16[8,32,2048]{2,1,0:T(8,128)(2,1)} collective-permute-done((bf16[8,32,2048]{2,1,0:T(8,128)(2,1)S(1)}, bf16[8,32,2048]{2,1,0:T(8,128)(2,1)}, u32[]{:S(2)}, u32[]{:S(2)}) %collective-permute-start.4) | collective-permute-done | bytes 1048608 | tf_op jit(solution)/shard_map/ppermute | solution.py:495
  66.1 6.1 %shard_map.117 = (bf16[256,1024]{1,0:T(8,128)(2,1)}, bf16[256,1024]{1,0:T(8,128)(2,1)}) custom-call(s32[14]{0:T(128)S(1)} %concatenate.9.refs_0_, bf16[8,32,2048]{2,1,0:T(8,128)(2,1)S(1)} %shard_map.111._.refs_1_, bf16[8,32,2048]{2,1,0:T(8,128)(2,1)S(1)} %copy-done.8, bf16[2048,2048]{1,0:T(8,128)(2,1)} %bitcast.24, bf16[8,2,32,1152]{3,2,1,0:T(8,128)(2,1)S(1)} %copy-done.1), custom_call_target="tpu_custom_call" | custom-call | flops 2147483648 | bytes 11534336 | tf_op jit(solution)/shard_map/pallas_call | solution.py:172
  73.2 6.8 %shard_map.116 = (bf16[2,32,1024]{2,1,0:T(8,128)(2,1)}, bf16[2,32,1024]{2,1,0:T(8,128)(2,1)}, bf16[2,32,1024]{2,1,0:T(8,128)(2,1)}, bf16[2,32,1024]{2,1,0:T(8,12...) custom-call(s32[14]{0:T(128)S(1)} %concatenate.9.refs_0_, ...), custom_call_target="tpu_custom_call" | custom-call | flops 2147483648 | bytes 11534336 | tf_op jit(solution)/shard_map/pallas_call | solution.py:172
  82.9 6.7 %shard_map.118 = (bf16[256,1024]{1,0:T(8,128)(2,1)}, bf16[256,1024]{1,0:T(8,128)(2,1)}) custom-call(s32[14]{0:T(128)S(1)} %concatenate.9.refs_0_, bf16[8,32,2048]{2,1,0:T(8,128)(2,1)} %shard_map.115.refs_1_, bf16[8,32,2048]{2,1,0:T(8,128)(2,1)} %copy-done.15, bf16[2048,2048]{1,0:T(8,128)(2,1)} %bitcast.26, bf16[8,2,32,1152]{3,2,1,0:T(8,128)(2,1)S(1)} %copy-done.1), custom_call_target="tpu_custom_call" | custom-call | flops 2147483648 | bytes 11534336 | tf_op jit(solution)/shard_map/pallas_call | solution.py:172
  103.1 2.9 %collective-permute-start.13 = (bf16[2,32,1024]{2,1,0:T(8,128)(2,1)S(1)}, bf16[2,32,1024]{2,1,0:T(8,128)(2,1)S(1)}, u32[]{:S(2)}, u32[]{:S(2)}) collective-permute-start(bf16[2,32,1024]{2,1,0:T(8,128)(2,1)S(1)} %copy-done.30), channel_id=1, source_target_pairs={{0,20},{4,16},{8,28},{12,24},{16,4},{20,0},{24,12},{28,8},{1,21},{... | collective-permute-start | bytes 393224 | tf_op jit(solution)/shard_map/ppermute | solution.py:509
  107.2 3.5 %collective-permute-start.15 = (bf16[2,32,1024]{2,1,0:T(8,128)(2,1)S(1)}, bf16[2,32,1024]{2,1,0:T(8,128)(2,1)S(1)}, u32[]{:S(2)}, u32[]{:S(2)}) collective-permute-start(bf16[2,32,1024]{2,1,0:T(8,128)(2,1)S(1)} %copy-done.28), channel_id=1, source_target_pairs={{0,28},{4,24},{8,20},{12,16},{16,12},{20,8},{24,4},{28,0},{1,29},{... | collective-permute-start | bytes 393224 | tf_op jit(solution)/shard_map/ppermute | solution.py:509
  111.4 4.9 %shard_map.120 = (bf16[4,8,128,256]{3,2,1,0:T(8,128)(2,1)S(1)}, bf16[4,128,1024]{2,1,0:T(8,128)(2,1)S(1)}, bf16[4,128,1024]{2,1,0:T(8,128)(2,1)S(1)}, f32[4,8,1024]{2,1,0:T(8,128)S(1)}, bf16[2,128,1024]{2,1,0:T(8,128)(2,1)S(1)}) custom-call(s32[14]{0:T(128)S(1)} %concatenate.9.refs_0_, s32[4,1,128]{2,1,0:T(1,128)S(1)} %bitcast.37, ...), custom_call_target="tpu_custom_call" | custom-call | flops 671088640 | bytes 6225920 | tf_op jit(solution)/shard_map/pallas_call | solution.py:172
  117.3 2.9 %collective-permute-done.13.refs_10_ = bf16[2,32,1024]{2,1,0:T(8,128)(2,1)S(1)} collective-permute-done((bf16[2,32,1024]{2,1,0:T(8,128)(2,1)S(1)}, bf16[2,32,1024]{2,1,0:T(8,128)(2,1)S(1)}, u32[]{:S(2)}, u32[]{:S(2)}) %collective-permute-start.13) | collective-permute-done | bytes 131104 | tf_op jit(solution)/shard_map/ppermute | solution.py:509
  121.5 9.3 %shard_map.122 = (bf16[2,32,1024]{2,1,0:T(8,128)(2,1)S(1)}, bf16[2,32,1024]{2,1,0:T(8,128)(2,1)S(1)}, bf16[2,32,1024]{2,1,0:T(8,128)(2,1)S(1)}, bf16[2,32,1024]{...) custom-call(s32[14]{0:T(128)S(1)} %concatenate.9.refs_0_, ...), custom_call_target="tpu_custom_call" | custom-call | flops 939524096 | bytes 8192000 | tf_op jit(solution)/shard_map/pallas_call | solution.py:172
  130.8 33.5 %all_to_all.20.refs_8_.refs_1_ = bf16[8,2,32,1024]{3,2,1,0:T(8,128)(2,1)S(1)} all-to-all(bf16[8,2,32,1024]{3,2,1,0:T(8,128)(2,1)S(1)} %get-tuple-element.62), channel_id=1, replica_groups=mesh['expert'=8,'context'=4] {'expert'}, dimensions={0} | all-to-all | bytes 2097152 | tf_op jit(solution)/shard_map/all_to_all | solution.py:505
  164.3 2.9 %shard_map.125 = bf16[8,32,2048]{2,1,0:T(8,128)(2,1)S(1)} custom-call(s32[14]{0:T(128)S(1)} %concatenate.9.refs_0_, bf16[8,2,32,1024]{3,2,1,0:T(8,128)(2,1)S(1)} %all_to_all.20.refs_8_.refs_1_, bf16[256,1024]{1,0:T(8,128)(2,1)} %get-tuple-element.71.refs_2_, bf16[1024,2048]{1,0:T(8,128)(2,1)S(1)} %shard_map.121.refs_19_.refs_3_.refs_10_), custom_call_target="tpu_custom_call" | custom-call | flops 1073741824 | bytes 6815744 | tf_op jit(solution)/shard_map/pallas_call | solution.py:172
  183.5 8.4 %collective-permute-done.20.refs_6_ = bf16[2,32,1024]{2,1,0:T(8,128)(2,1)S(1)} collective-permute-done((bf16[2,32,1024]{2,1,0:T(8,128)(2,1)S(1)}, bf16[2,32,1024]{2,1,0:T(8,128)(2,1)S(1)}, u32[]{:S(2)}, u32[]{:S(2)}) %collective-permute-start.20) | collective-permute-done | bytes 131104 | tf_op jit(solution)/shard_map/ppermute | solution.py:509
  191.9 2.9 %shard_map.127 = bf16[8,32,2048]{2,1,0:T(8,128)(2,1)S(1)} custom-call(s32[14]{0:T(128)S(1)} %concatenate.9.refs_0_, bf16[2,32,1024]{2,1,0:T(8,128)(2,1)S(1)} %get-tuple-element.63.refs_1_, bf16[2,32,1024]{2,1,0:T(8,128)(2,1)S(1)} %collective-permute-done.16.refs_2_, bf16[2,32,1024]{2,1,0:T(8,128)(2,1)S(1)} %collective-permute-done.17.refs_3_, ...), custom_call_target="tpu_custom_call" | custom-call | flops 1073741824 | bytes 6815744 | tf_op jit(solution)/shard_map/pallas_call | solution.py:172
  194.9 10.6 %collective-permute-done.24.refs_11_ = bf16[8,32,2048]{2,1,0:T(8,128)(2,1)S(1)} collective-permute-done((bf16[8,32,2048]{2,1,0:T(8,128)(2,1)S(1)}, bf16[8,32,2048]{2,1,0:T(8,128)(2,1)S(1)}, u32[]{:S(2)}, u32[]{:S(2)}) %collective-permute-start.24) | collective-permute-done | bytes 1048608 | tf_op jit(solution)/shard_map/ppermute | solution.py:495
  205.5 2.9 %shard_map.126 = bf16[8,32,2048]{2,1,0:T(8,128)(2,1)S(1)} custom-call(s32[14]{0:T(128)S(1)} %concatenate.9.refs_0_, bf16[2,32,1024]{2,1,0:T(8,128)(2,1)S(1)} %get-tuple-element.63.refs_1_, bf16[2,32,1024]{2,1,0:T(8,128)(2,1)S(1)} %collective-permute-done.16.refs_2_, bf16[2,32,1024]{2,1,0:T(8,128)(2,1)S(1)} %collective-permute-done.17.refs_3_, ...), custom_call_target="tpu_custom_call" | custom-call | flops 1073741824 | bytes 6815744 | tf_op jit(solution)/shard_map/pallas_call | solution.py:172
  209.0 26.6 %all_to_all.21 = bf16[8,32,2048]{2,1,0:T(8,128)(2,1)S(1)} all-to-all(bf16[8,32,2048]{2,1,0:T(8,128)(2,1)S(1)} %add_convert_fusion), channel_id=1, replica_groups=mesh['expert'=8,'context'=4] {'expert'}, dimensions={0} | all-to-all | bytes 2097152 | tf_op jit(solution)/shard_map/all_to_all | solution.py:505
  (134 shorter events, 50.4 us)
Async XLA Ops:
  3.1 33.2 %all-to-all-start = ((bf16[8,32,2048]{2,1,0:T(8,128)(2,1)}), bf16[8,32,2048]{2,1,0:T(8,128)(2,1)S(1)}, u32[]{:S(2)}, u32[]{:S(2)}) async-start(bf16[8,32,2048]{2,1,0:T(8,128)(2,1)} %bitcast.28), calls=%async_computation | async-start | bytes 2097152 | tf_op jit(solution)/shard_map/all_to_all | solution.py:505
  12.6 13.0 %collective-permute-start = (bf16[16,2048]{1,0:T(8,128)(2,1)S(1)}, bf16[16,2048]{1,0:T(8,128)(2,1)S(1)}, u32[]{:S(2)}, u32[]{:S(2)}) collective-permute-start(bf16[16,2048]{1,0:T(8,128)(2,1)S(1)} %bitcast.32), channel_id=1, source_target_pairs={{0,1},{1,0},{2,3},{3,2},{4,5},{5,4},{6,7},{7,6},{8,9},{9,8},{10,11... | collective-permute-start | bytes 196616 | tf_op jit(solution)/shard_map/ppermute | solution.py:495
  15.4 10.2 %collective-permute-start.2 = (bf16[16,2048]{1,0:T(8,128)(2,1)S(1)}, bf16[16,2048]{1,0:T(8,128)(2,1)S(1)}, u32[]{:S(2)}, u32[]{:S(2)}) collective-permute-start(bf16[16,2048]{1,0:T(8,128)(2,1)S(1)} %collective-permute-done.1.refs_4_.refs_6_), channel_id=1, source_target_pairs={{0,1},{1,0},{2,3},{3,2},{4,5},{5,4},{6,7},{7,6},{8,9},{9,8},{10,11... | collective-permute-start | bytes 196616 | tf_op jit(solution)/shard_map/ppermute | solution.py:495
  39.7 9.6 %collective-permute-start.3 = (bf16[8,32,2048]{2,1,0:T(8,128)(2,1)S(1)}, bf16[8,32,2048]{2,1,0:T(8,128)(2,1)S(1)}, u32[]{:S(2)}, u32[]{:S(2)}) collective-permute-start(bf16[8,32,2048]{2,1,0:T(8,128)(2,1)S(1)} %shard_map.111._.refs_1_), channel_id=1, source_target_pairs={{0,1},{1,0},{2,3},{3,2},{4,5},{5,4},{6,7},{7,6},{8,9},{9,8},{10,11... | collective-permute-start | bytes 3145736 | tf_op jit(solution)/shard_map/ppermute | solution.py:495
  39.7 25.7 %collective-permute-start.4 = (bf16[8,32,2048]{2,1,0:T(8,128)(2,1)S(1)}, bf16[8,32,2048]{2,1,0:T(8,128)(2,1)}, u32[]{:S(2)}, u32[]{:S(2)}) collective-permute-start(bf16[8,32,2048]{2,1,0:T(8,128)(2,1)S(1)} %shard_map.111._.refs_1_), channel_id=1, source_target_pairs={{0,2},{1,3},{2,0},{3,1},{4,6},{5,7},{6,4},{7,5},{8,10},{9,11},{10,... | collective-permute-start | bytes 3145736 | tf_op jit(solution)/shard_map/ppermute | solution.py:495
  54.4 35.3 %all-to-all-start.1 = ((bf16[8,2,32,1152]{3,2,1,0:T(8,128)(2,1)}), bf16[8,2,32,1152]{3,2,1,0:T(8,128)(2,1)S(1)}, u32[]{:S(2)}, u32[]{:S(2)}) async-start(bf16[8,2,32,1152]{3,2,1,0:T(8,128)(2,1)} %shard_map.114.refs_1_.refs_4_), calls=%async_computation.1 | async-start | bytes 2359296 | tf_op jit(solution)/shard_map/all_to_all | solution.py:505
  80.0 23.2 %collective-permute-start.10 = (bf16[2,32,1024]{2,1,0:T(8,128)(2,1)}, bf16[2,32,1024]{2,1,0:T(8,128)(2,1)}, u32[]{:S(2)}, u32[]{:S(2)}) collective-permute-start(bf16[2,32,1024]{2,1,0:T(8,128)(2,1)} %get-tuple-element.44), channel_id=1, source_target_pairs={{0,8},{4,12},{8,0},{12,4},{16,24},{20,28},{24,16},{28,20},{1,9},{5... | collective-permute-start | bytes 393224 | tf_op jit(solution)/shard_map/ppermute | solution.py:509
  80.1 26.0 %collective-permute-start.11 = (bf16[2,32,1024]{2,1,0:T(8,128)(2,1)}, bf16[2,32,1024]{2,1,0:T(8,128)(2,1)}, u32[]{:S(2)}, u32[]{:S(2)}) collective-permute-start(bf16[2,32,1024]{2,1,0:T(8,128)(2,1)} %get-tuple-element.45), channel_id=1, source_target_pairs={{0,12},{4,8},{8,4},{12,0},{16,28},{20,24},{24,20},{28,16},{1,13},{... | collective-permute-start | bytes 393224 | tf_op jit(solution)/shard_map/ppermute | solution.py:509
  95.9 11.3 %collective-permute-start.6 = (bf16[128,256]{1,0:T(8,128)(2,1)}, bf16[128,256]{1,0:T(8,128)(2,1)S(1)}, u32[]{:S(2)}, u32[]{:S(2)}) collective-permute-start(bf16[128,256]{1,0:T(8,128)(2,1)} %shard_map.119), channel_id=1, source_target_pairs={{0,1},{1,0},{2,3},{3,2},{4,5},{5,4},{6,7},{7,6},{8,9},{9,8},{10,11... | collective-permute-start | bytes 196616 | tf_op jit(solution)/shard_map/ppermute | solution.py:495
  98.6 12.1 %collective-permute-start.8 = (bf16[128,256]{1,0:T(8,128)(2,1)S(1)}, bf16[128,256]{1,0:T(8,128)(2,1)S(1)}, u32[]{:S(2)}, u32[]{:S(2)}) collective-permute-start(bf16[128,256]{1,0:T(8,128)(2,1)S(1)} %collective-permute-done.7), channel_id=1, source_target_pairs={{0,1},{1,0},{2,3},{3,2},{4,5},{5,4},{6,7},{7,6},{8,9},{9,8},{10,11... | collective-permute-start | bytes 196616 | tf_op jit(solution)/shard_map/ppermute | solution.py:495
  99.4 17.9 %collective-permute-start.12 = (bf16[2,32,1024]{2,1,0:T(8,128)(2,1)}, bf16[2,32,1024]{2,1,0:T(8,128)(2,1)S(1)}, u32[]{:S(2)}, u32[]{:S(2)}) collective-permute-start(bf16[2,32,1024]{2,1,0:T(8,128)(2,1)} %get-tuple-element.46), channel_id=1, source_target_pairs={{0,16},{4,20},{8,24},{12,28},{16,0},{20,4},{24,8},{28,12},{1,17},{... | collective-permute-start | bytes 393224 | tf_op jit(solution)/shard_map/ppermute | solution.py:509
  103.1 17.1 %collective-permute-start.13 = (bf16[2,32,1024]{2,1,0:T(8,128)(2,1)S(1)}, bf16[2,32,1024]{2,1,0:T(8,128)(2,1)S(1)}, u32[]{:S(2)}, u32[]{:S(2)}) collective-permute-start(bf16[2,32,1024]{2,1,0:T(8,128)(2,1)S(1)} %copy-done.30), channel_id=1, source_target_pairs={{0,20},{4,16},{8,28},{12,24},{16,4},{20,0},{24,12},{28,8},{1,21},{... | collective-permute-start | bytes 393224 | tf_op jit(solution)/shard_map/ppermute | solution.py:509
  106.1 14.2 %collective-permute-start.14 = (bf16[2,32,1024]{2,1,0:T(8,128)(2,1)S(1)}, bf16[2,32,1024]{2,1,0:T(8,128)(2,1)S(1)}, u32[]{:S(2)}, u32[]{:S(2)}) collective-permute-start(bf16[2,32,1024]{2,1,0:T(8,128)(2,1)S(1)} %copy-done.29), channel_id=1, source_target_pairs={{0,24},{4,28},{8,16},{12,20},{16,8},{20,12},{24,0},{28,4},{1,25},{... | collective-permute-start | bytes 393224 | tf_op jit(solution)/shard_map/ppermute | solution.py:509
  107.2 13.0 %collective-permute-start.15 = (bf16[2,32,1024]{2,1,0:T(8,128)(2,1)S(1)}, bf16[2,32,1024]{2,1,0:T(8,128)(2,1)S(1)}, u32[]{:S(2)}, u32[]{:S(2)}) collective-permute-start(bf16[2,32,1024]{2,1,0:T(8,128)(2,1)S(1)} %copy-done.28), channel_id=1, source_target_pairs={{0,28},{4,24},{8,20},{12,16},{16,12},{20,8},{24,4},{28,0},{1,29},{... | collective-permute-start | bytes 393224 | tf_op jit(solution)/shard_map/ppermute | solution.py:509
  110.7 10.1 %collective-permute-start.9 = (bf16[2,32,1024]{2,1,0:T(8,128)(2,1)S(1)}, bf16[2,32,1024]{2,1,0:T(8,128)(2,1)S(1)}, u32[]{:S(2)}, u32[]{:S(2)}) collective-permute-start(bf16[2,32,1024]{2,1,0:T(8,128)(2,1)S(1)} %copy-done.27), channel_id=1, source_target_pairs={{0,4},{4,0},{8,12},{12,8},{16,20},{20,16},{24,28},{28,24},{1,5},{5... | collective-permute-start | bytes 393224 | tf_op jit(solution)/shard_map/ppermute | solution.py:509
  167.2 12.2 %collective-permute-start.23 = (bf16[8,32,2048]{2,1,0:T(8,128)(2,1)S(1)}, bf16[8,32,2048]{2,1,0:T(8,128)(2,1)S(1)}, u32[]{:S(2)}, u32[]{:S(2)}) collective-permute-start(bf16[8,32,2048]{2,1,0:T(8,128)(2,1)S(1)} %shard_map.125), channel_id=1, source_target_pairs={{0,1},{1,0},{2,3},{3,2},{4,5},{5,4},{6,7},{7,6},{8,9},{9,8},{10,11... | collective-permute-start | bytes 3145736 | tf_op jit(solution)/shard_map/ppermute | solution.py:495
  168.8 9.2 %collective-permute-start.17 = (bf16[2,32,1024]{2,1,0:T(8,128)(2,1)S(1)}, bf16[2,32,1024]{2,1,0:T(8,128)(2,1)S(1)}, u32[]{:S(2)}, u32[]{:S(2)}) collective-permute-start(bf16[2,32,1024]{2,1,0:T(8,128)(2,1)S(1)} %get-tuple-element.65), channel_id=1, source_target_pairs={{0,8},{4,12},{8,0},{12,4},{16,24},{20,28},{24,16},{28,20},{1,9},{5... | collective-permute-start | bytes 393224 | tf_op jit(solution)/shard_map/ppermute | solution.py:509
  168.8 13.0 %collective-permute-start.18 = (bf16[2,32,1024]{2,1,0:T(8,128)(2,1)S(1)}, bf16[2,32,1024]{2,1,0:T(8,128)(2,1)S(1)}, u32[]{:S(2)}, u32[]{:S(2)}) collective-permute-start(bf16[2,32,1024]{2,1,0:T(8,128)(2,1)S(1)} %get-tuple-element.66), channel_id=1, source_target_pairs={{0,12},{4,8},{8,4},{12,0},{16,28},{20,24},{24,20},{28,16},{1,13},{... | collective-permute-start | bytes 393224 | tf_op jit(solution)/shard_map/ppermute | solution.py:509
  170.9 12.6 %collective-permute-start.19 = (bf16[2,32,1024]{2,1,0:T(8,128)(2,1)S(1)}, bf16[2,32,1024]{2,1,0:T(8,128)(2,1)S(1)}, u32[]{:S(2)}, u32[]{:S(2)}) collective-permute-start(bf16[2,32,1024]{2,1,0:T(8,128)(2,1)S(1)} %get-tuple-element.67), channel_id=1, source_target_pairs={{0,16},{4,20},{8,24},{12,28},{16,0},{20,4},{24,8},{28,12},{1,17},{... | collective-permute-start | bytes 393224 | tf_op jit(solution)/shard_map/ppermute | solution.py:509
  174.9 17.0 %collective-permute-start.20 = (bf16[2,32,1024]{2,1,0:T(8,128)(2,1)S(1)}, bf16[2,32,1024]{2,1,0:T(8,128)(2,1)S(1)}, u32[]{:S(2)}, u32[]{:S(2)}) collective-permute-start(bf16[2,32,1024]{2,1,0:T(8,128)(2,1)S(1)} %get-tuple-element.68), channel_id=1, source_target_pairs={{0,20},{4,16},{8,28},{12,24},{16,4},{20,0},{24,12},{28,8},{1,21},{... | collective-permute-start | bytes 393224 | tf_op jit(solution)/shard_map/ppermute | solution.py:509
  178.0 13.9 %collective-permute-start.21 = (bf16[2,32,1024]{2,1,0:T(8,128)(2,1)S(1)}, bf16[2,32,1024]{2,1,0:T(8,128)(2,1)S(1)}, u32[]{:S(2)}, u32[]{:S(2)}) collective-permute-start(bf16[2,32,1024]{2,1,0:T(8,128)(2,1)S(1)} %get-tuple-element.69), channel_id=1, source_target_pairs={{0,24},{4,28},{8,16},{12,20},{16,8},{20,12},{24,0},{28,4},{1,25},{... | collective-permute-start | bytes 393224 | tf_op jit(solution)/shard_map/ppermute | solution.py:509
  179.4 12.4 %collective-permute-start.22 = (bf16[2,32,1024]{2,1,0:T(8,128)(2,1)S(1)}, bf16[2,32,1024]{2,1,0:T(8,128)(2,1)S(1)}, u32[]{:S(2)}, u32[]{:S(2)}) collective-permute-start(bf16[2,32,1024]{2,1,0:T(8,128)(2,1)S(1)} %get-tuple-element.70), channel_id=1, source_target_pairs={{0,28},{4,24},{8,20},{12,16},{16,12},{20,8},{24,4},{28,0},{1,29},{... | collective-permute-start | bytes 393224 | tf_op jit(solution)/shard_map/ppermute | solution.py:509
  181.9 23.6 %collective-permute-start.24 = (bf16[8,32,2048]{2,1,0:T(8,128)(2,1)S(1)}, bf16[8,32,2048]{2,1,0:T(8,128)(2,1)S(1)}, u32[]{:S(2)}, u32[]{:S(2)}) collective-permute-start(bf16[8,32,2048]{2,1,0:T(8,128)(2,1)S(1)} %add_convert_fusion.1), channel_id=1, source_target_pairs={{0,2},{1,3},{2,0},{3,1},{4,6},{5,7},{6,4},{7,5},{8,10},{9,11},{10,... | collective-permute-start | bytes 3145736 | tf_op jit(solution)/shard_map/ppermute | solution.py:495
  194.8 13.6 %collective-permute-start.25 = (bf16[8,32,2048]{2,1,0:T(8,128)(2,1)S(1)}, bf16[8,32,2048]{2,1,0:T(8,128)(2,1)S(1)}, u32[]{:S(2)}, u32[]{:S(2)}) collective-permute-start(bf16[8,32,2048]{2,1,0:T(8,128)(2,1)S(1)} %shard_map.127), channel_id=1, source_target_pairs={{0,1},{1,0},{2,3},{3,2},{4,5},{5,4},{6,7},{7,6},{8,9},{9,8},{10,11... | collective-permute-start | bytes 3145736 | tf_op jit(solution)/shard_map/ppermute | solution.py:495
  (36 other events, 252.8 us)

commit v2 on v1

--- a/solution.py
+++ b/solution.py
@@ -41,7 +41,6 @@
 VMEM = pl.BlockSpec(memory_space=pltpu.VMEM)
 SMEM = pl.BlockSpec(memory_space=pltpu.SMEM)
 HBM = pl.BlockSpec(memory_space=pltpu.HBM)
-ANY = pl.BlockSpec(memory_space=pl.ANY)
 
 
 class Stream:
@@ -114,7 +113,7 @@
 
 
 def call(
-    kernel, info, big, outs, small=(), after=(), alias=None, scratch=(), flops=0, exps=0, limit=32
+    kernel, info, big, outs, small=(), after=(), after_vmem=(), passed=(), scratch=(), flops=0, exps=0, limit=32
 ):
     moved = sum(2 * a.size for a, _, _ in big) + sum(2 * o.size for o, _ in outs)
     held = []
@@ -126,7 +125,7 @@
             held.append(pltpu.VMEM(out.shape, out.dtype))
     fetches = sum(len(pieces or ()) for _, _, pieces in big)
     sends = sum(len(pieces or ()) for _, pieces in outs)
-    held += [pltpu.SemaphoreType.DMA((max(count, 1),)) for count in (fetches, sends)]
+    held += [pltpu.SemaphoreType.DMA((max(count, 1),)) for count in (fetches, sends, len(passed))]
 
     def body(*refs):
         refs = list(refs)
@@ -138,11 +137,12 @@
 
         info_ref = take(1)[0]
         small_refs, big_refs = take(len(small)), take(len(big))
-        take(len(after) + (alias is not None))
-        out_refs = take(len(outs))
+        take(len(after) + len(after_vmem))
+        pass_refs = take(len(passed))
+        out_refs, passed_refs = take(len(outs)), take(len(passed))
         held_refs = [take(1)[0] if pieces else ref for ref, (_, _, pieces) in zip(big_refs, big)]
         made_refs = [take(1)[0] if pieces else ref for ref, (_, pieces) in zip(out_refs, outs)]
-        fetch_sems, send_sems = take(2)
+        fetch_sems, send_sems, pass_sems = take(3)
         copies, spans = [], []
         for source, target, (_, _, pieces) in zip(big_refs, held_refs, big):
             spans.append((len(copies), len(pieces or ())))
@@ -150,6 +150,12 @@
                 sem = fetch_sems.at[len(copies)]
                 copies.append(pltpu.make_async_copy(source.at[there], target.at[here], sem))
         stream = Stream(copies, 3)
+        passing = [
+            pltpu.make_async_copy(source, target, pass_sems.at[i])
+            for i, (source, target) in enumerate(zip(pass_refs, passed_refs))
+        ]
+        for copy in passing:
+            copy.start()
         operands = [
             Operand(ref, stream if count else None, at, count)
             for ref, (at, count) in zip(held_refs, spans)
@@ -166,20 +172,24 @@
             stream.need(i)
         for result in results:
             result.finish()
+        for copy in passing:
+            copy.wait()
 
     arrays = [in_hbm(a) if pieces else in_vmem(a) for a, _, pieces in big]
-    arrays += list(after) + ([in_hbm(alias)] if alias is not None else [])
+    arrays += [in_hbm(array) for array in after] + [in_vmem(array) for array in after_vmem]
+    arrays += [in_hbm(array) for array in passed]
     return pl.pallas_call(
         body,
-        out_shape=[(pltpu.HBM if pieces else pltpu.VMEM)(o.shape, o.dtype) for o, pieces in outs],
+        out_shape=[(pltpu.HBM if pieces else pltpu.VMEM)(o.shape, o.dtype) for o, pieces in outs]
+        + [pltpu.VMEM(array.shape, array.dtype) for array in passed],
         in_specs=[SMEM]
         + [VMEM] * len(small)
         + [HBM if pieces else VMEM for _, _, pieces in big]
-        + [ANY] * len(after)
-        + [HBM] * (alias is not None),
-        out_specs=[HBM if pieces else VMEM for _, pieces in outs],
+        + [HBM] * len(after)
+        + [VMEM] * len(after_vmem)
+        + [HBM] * len(passed),
+        out_specs=[HBM if pieces else VMEM for _, pieces in outs] + [VMEM] * len(passed),
         scratch_shapes=held + list(scratch),
-        input_output_aliases={len(small) + len(arrays): 0} if alias is not None else {},
         compiler_params=pltpu.CompilerParams(vmem_limit_bytes=limit << 20),
         cost_estimate=pl.CostEstimate(flops=flops, bytes_accessed=moved, transcendentals=exps),
     )(info, *small, *arrays)
@@ -189,17 +199,21 @@
     return jax.ShapeDtypeStruct(dims, BF16)
 
 
-def tie(values, *after, hbm=False):
+def tie(values, after=(), after_vmem=(), hbm=False):
     count = len(values)
     space, spec, pin = (pltpu.HBM, HBM, in_hbm) if hbm else (pltpu.VMEM, VMEM, in_vmem)
     return pl.pallas_call(
         lambda *refs: None,
         out_shape=[space(value.shape, value.dtype) for value in values],
-        in_specs=[spec] * count + [ANY] * len(after),
+        in_specs=[spec] * count + [HBM] * len(after) + [VMEM] * len(after_vmem),
         out_specs=[spec] * count,
         input_output_aliases={i: i for i in range(count)},
         compiler_params=pltpu.CompilerParams(vmem_limit_bytes=4 << 20),
-    )(*(pin(value) for value in values), *after)
+    )(
+        *(pin(value) for value in values),
+        *(in_hbm(array) for array in after),
+        *(in_vmem(array) for array in after_vmem),
+    )
 
 
 def staged(array, start, count, after):
@@ -211,14 +225,14 @@
     return pl.pallas_call(
         body,
         out_shape=pltpu.VMEM((array.shape[0], count), array.dtype),
-        in_specs=[HBM, ANY],
+        in_specs=[HBM, VMEM],
         out_specs=VMEM,
         scratch_shapes=[pltpu.SemaphoreType.DMA],
         compiler_params=pltpu.CompilerParams(vmem_limit_bytes=4 << 20),
         cost_estimate=pl.CostEstimate(
             flops=0, bytes_accessed=4 * array.shape[0] * count, transcendentals=0
         ),
-    )(in_hbm(array), after)
+    )(in_hbm(array), in_vmem(after))
 
 
 def peer_rows(ref, me):
@@ -246,54 +260,31 @@
     out.send(0)
 
 
-def project_rows(places, experts, cap, rows, weight, out, tile):
+def project_kernel(places, experts, cap, tile, info_ref, *refs):
+    rows, weight, sides, out = refs[:places], refs[places], refs[places + 1 : -1], refs[-1]
     chans = weight.held.shape[1]
-    rows = [flat_rows(block.whole()[...]) for block in rows]
+
+    def store(at, lo, made):
+        made = made.astype(BF16)
+        for e in range(experts):
+            out.held[e, at, :, lo : lo + made.shape[1]] = made[e * cap : (e + 1) * cap, :]
+
     for lo in range(0, chans, tile):
-        part = weight.whole()[:, lo : lo + tile]
-        for at, block in zip(places, rows):
-            store_rows(out, at, lo, dot(block, part), experts, cap)
-        out.send(lo // tile)
-
-
-def store_rows(out, at, lo, made, experts, cap):
-    made = made.astype(BF16)
-    for e in range(experts):
-        out.held[e, at, :, lo : lo + made.shape[1]] = made[e * cap : (e + 1) * cap, :]
-
-
-def own_kernel(experts, cap, tile, info_ref, rows, weight, states, *refs):
-    steps, out = refs[:-1], refs[-1]
-    chans = weight.held.shape[1]
-    project_rows([0], experts, cap, [rows], weight, out, tile)
-    first = flat_rows(rows.whole()[...])
-    store_rows(out, 0, chans, dot(first, states.whole()[...]), experts, cap)
-    steps = [ref.whole()[...].astype(F32) for ref in steps]
-    spare = LANES - sum(part.shape[0] for part in steps)
-    steps.append(jnp.zeros((spare, steps[0].shape[1]), F32))
-    steps = jnp.concatenate(steps, axis=0).astype(BF16)
-    made = lax.dot_general(first, steps, (((1,), (1,)), ((), ())), preferred_element_type=F32)
-    store_rows(out, 1, chans, made, experts, cap)
-    out.send(chans // tile)
-
-
-def project_kernel(places, experts, cap, tile, info_ref, *refs):
-    rows, weight, out = refs[: len(places)], refs[-2], refs[-1]
-    project_rows(places, experts, cap, rows, weight, out, tile)
-
-
-def peers_kernel(places, experts, cap, tile, info_ref, *refs):
-    weight, outs = refs[places], refs[places + 1 :]
-    me = info_ref[info_ref.shape[0] - 1]
-    rows = [peer_rows(ref.whole(), me) for ref in refs[:places]]
-    for lo in range(0, weight.held.shape[1], tile):
-        part = weight.whole()[:, lo : lo + tile]
         for at in range(places):
-            made = dot(rows[at], part).astype(BF16)
-            for r in range(experts):
-                outs[r].held[at, :, lo : lo + tile] = made[r * cap : (r + 1) * cap, :]
-    for out in outs:
-        out.send(0)
+            block = flat_rows(rows[at].whole()[...])
+            store(at, lo, dot(block, weight.whole()[:, lo : lo + tile]))
+    if sides:
+        first = flat_rows(rows[0].whole()[...])
+        store(0, chans, dot(first, sides[0].whole()[...]))
+        steps = [ref.whole()[...].astype(F32) for ref in sides[1:]]
+        spare = LANES - sum(part.shape[0] for part in steps)
+        steps.append(jnp.zeros((spare, steps[0].shape[1]), F32))
+        steps = jnp.concatenate(steps, axis=0).astype(BF16)
+        made = lax.dot_general(
+            first, steps, (((1,), (1,)), ((), ())), preferred_element_type=F32
+        )
+        store(1, chans, made)
+    out.send(0)
 
 
 def gate_kernel(tile, by_peer, info_ref, *refs):
@@ -327,22 +318,52 @@
             out[r ^ me, :, lo : lo + tile] = made[r * cap : (r + 1) * cap, :]
 
 
-def factors_kernel(cfg, info_ref, ids_ref, head_ref, near, side, weights, kept, tail, last, placed):
+def scan_kernel(
+    cfg,
+    info_ref,
+    ids_ref,
+    head_ref,
+    chan_ref,
+    near,
+    side,
+    far,
+    *refs,
+):
     experts, cap, tok_rows, nstate, chn, heads = cfg
     blocks = ids_ref.shape[0]
+    taps = 4
+    out_near, (out_far, inner_ref, made_ref) = refs[:experts], refs[experts:]
+    me = info_ref[info_ref.shape[0] - 1]
+    near_ref, far_ref, side_ref = near.whole(), far.whole(), side.whole()
+    inner_ref[:8, :] = jnp.zeros((8, chn), F32)
+
+    for q in range(blocks):
+        b = info_ref[1 + q]
+        place = slot_rows(ids_ref[b], experts, cap).T.astype(BF16)
+        rows = flat_rows(near_ref[:, q, :, :chn] if q < 2 else far_ref[:, q - 2])
+        inner_ref[pl.ds(8 + b * tok_rows, tok_rows), :] = dot(place, rows)
+
     lower = iota((tok_rows, tok_rows), 0) >= iota((tok_rows, tok_rows), 1)
     ones = jnp.where(lower, 1.0, 0.0)
     first = iota((tok_rows, LANES), 1) < HEAD_DIM
     spread = jnp.where(
         iota((2 * LANES, chn), 0) % LANES == iota((2 * LANES, chn), 1) // HEAD_DIM, 1.0, 0.0
     ).astype(BF16)
-    for q in range(2):
-        place = slot_rows(ids_ref[info_ref[1 + q]], experts, cap).T.astype(BF16)
-        placed.held[q] = dot(place, flat_rows(near.whole()[:, q, :, :chn])).astype(BF16)
-    placed.send(0)
-    side_ref = side.whole()
+
+    def widen(values):
+        high = values.astype(BF16)
+        low = (values - high.astype(F32)).astype(BF16)
+        return dot(jnp.concatenate([high, low], axis=1), spread)
+
+    state = jnp.zeros((nstate, chn), F32)
     for b in range(blocks):
         q = info_ref[1 + blocks + b]
+        total = chan_ref[taps : taps + 1, :]
+        for j in range(taps):
+            start = 8 + b * tok_rows - (taps - 1) + j
+            total = total + chan_ref[j : j + 1, :] * inner_ref[start : start + tok_rows, :]
+        signal = jax.nn.silu(total)
+
         own_head = iota((LANES, LANES), 0) == iota((LANES, LANES), 1) + info_ref[
             1 + 2 * blocks + b
         ] * heads
@@ -357,80 +378,18 @@
         )
         source = summed - jnp.log(step)
         source_t = source.T
-        left = jnp.exp(summed[tok_rows - 1 :, :] - source)
-        high = left.astype(BF16)
-        low = (left - high.astype(F32)).astype(BF16)
-        tail.held[b] = dot(jnp.concatenate([high, low], axis=1), spread).astype(BF16)
-        tail.send(b)
+        kept = widen(jnp.exp(summed))
+        tail = widen(jnp.exp(summed[tok_rows - 1 :, :] - source))
 
         both = side_ref[q, :, :LANES]
         keys_t = both.astype(F32).T.astype(BF16)[:nstate, :]
-        scores = dot(both[:, nstate:], keys_t)
-        for pair in range(heads // 2):
-            lanes = slice(pair * LANES, (pair + 1) * LANES)
-            wide = []
-            for h in (2 * pair, 2 * pair + 1):
-                wide.append(jnp.broadcast_to(summed[:, h : h + 1], (tok_rows, tok_rows)))
-                gaps = wide[-1] - source_t[h : h + 1, :]
-                decay = jnp.exp(jnp.where(lower, gaps, -jnp.inf))
-                at = (h % 2) * tok_rows
-                weights.held[b, pair, :, at : at + tok_rows] = (scores * decay).astype(BF16)
-            both_wide = jnp.exp(jnp.where(first, wide[0], wide[1]))
-            kept.held[b, :, lanes] = both_wide.astype(BF16)
-            last.held[b, :, lanes] = both_wide[tok_rows - 8 :, :]
-        weights.send(b)
-        kept.send(b)
-        last.send(b)
-
-
-def scan_kernel(
-    cfg,
-    info_ref,
-    ids_ref,
-    chan_ref,
-    side,
-    placed,
-    *refs,
-):
-    experts, cap, tok_rows, nstate, chn, heads = cfg
-    far, refs = refs[:experts], refs[experts:]
-    weights, kept, tail, last = refs[:4]
-    out_near, (out_far, inner_ref, made_ref) = refs[4 : 4 + experts], refs[4 + experts :]
-    me = info_ref[info_ref.shape[0] - 1]
-    blocks = ids_ref.shape[0]
-    taps = 4
-    inner_ref[:8, :] = jnp.zeros((8, chn), F32)
-
-    for q in range(blocks):
-        b = info_ref[1 + q]
-        at = pl.ds(8 + b * tok_rows, tok_rows)
-        if q < 2:
-            inner_ref[at, :] = placed.whole()[q].astype(F32)
-        else:
-            place = slot_rows(ids_ref[b], experts, cap, me).T.astype(BF16)
-            rows = jnp.stack([far[r].whole()[q - 2] for r in range(experts)])
-            inner_ref[at, :] = dot(place, flat_rows(rows))
-
-    first = iota((tok_rows, LANES), 1) < HEAD_DIM
-    state = jnp.zeros((nstate, chn), F32)
-    side_ref = side.whole()
-    for b in range(blocks):
-        q = info_ref[1 + blocks + b]
-        total = chan_ref[taps : taps + 1, :]
-        for j in range(taps):
-            start = 8 + b * tok_rows - (taps - 1) + j
-            total = total + chan_ref[j : j + 1, :] * inner_ref[start : start + tok_rows, :]
-        signal = jax.nn.silu(total)
-
-        both = side_ref[q, :, :LANES]
-        keys_t = both.astype(F32).T.astype(BF16)[:nstate, :]
+        queries = both[:, nstate:]
+        scores = dot(queries, keys_t)
         rest = chan_ref[taps + 1 : taps + 2, :] * signal
         if b > 0:
-            carried = dot(both[:, nstate:], state.astype(BF16))
-            rest = rest + carried * kept.held[b].astype(F32)
+            rest = rest + dot(queries, state.astype(BF16)) * kept
         if b < blocks - 1:
-            added = dot(keys_t, (signal * tail.held[b].astype(F32)).astype(BF16))
-            state = last.held[b, 7:8, :] * state + added
+            state = kept[tok_rows - 1 :, :] * state + dot(keys_t, (signal * tail).astype(BF16))
 
         for pair in range(heads // 2):
             lanes = slice(pair * LANES, (pair + 1) * LANES)
@@ -438,10 +397,15 @@
             values = jnp.concatenate(
                 [jnp.where(first, values, 0.0), jnp.where(first, 0.0, values)], axis=0
             ).astype(BF16)
-            local = dot(weights.held[b, pair], values)
+            weights = []
+            for h in (2 * pair, 2 * pair + 1):
+                gaps = summed[:, h : h + 1] - source_t[h : h + 1, :]
+                decay = jnp.exp(jnp.where(lower, gaps, -jnp.inf))
+                weights.append((scores * decay).astype(BF16))
+            local = dot(jnp.concatenate(weights, axis=1), values)
             made_ref[b * tok_rows : (b + 1) * tok_rows, lanes] = (rest[:, lanes] + local).astype(BF16)
 
-    for q in range(blocks - 1, -1, -1):
+    for q in range(blocks):
         b = info_ref[1 + q]
         place = slot_rows(ids_ref[b], experts, cap, me if q < 2 else 0).astype(BF16)
         start = pl.multiple_of(b * tok_rows, tok_rows)
@@ -520,47 +484,30 @@
         flops=2 * slots * tok_rows * width,
     )[0]
     own = exchange(outgoing.reshape(experts, cap, width))
-    steps = spread(tie([w_step[0]], outgoing)[0].T)
-    own = tie([own], w_flat, *steps)[0]
+    steps = spread(tie([w_step[0]], [outgoing])[0].T)
+    own = tie([own], [w_flat], steps)[0]
     w_in = staged(w_flat, chans, chans, own)
     swapped = permute(own, swap)
-    everything = (slice(None),) * 3
-
-    def inner_cuts(place, extra):
-        at = (slice(None), place, slice(None))
-        cuts = [at + (pl.ds(lo, 256),) for lo in range(0, chans, 256)]
-        return cuts + [everything + (pl.ds(chans, LANES),)] * extra
-
-    near_shape = shape(experts, 2, cap, chans + LANES)
-    own_part = call(
-        functools.partial(own_kernel, experts, cap, 256),
+    near = call(
+        functools.partial(project_kernel, 2, experts, cap, 256),
         info,
-        [kept_in_vmem(own), kept_in_vmem(w_in), full(w_state[0])]
-        + [full(part) for part in steps],
-        [(near_shape, inner_cuts(0, 1))],
-        flops=2 * slots * width * (chans + 2 * LANES),
-    )[0]
-    near = call(
-        functools.partial(project_kernel, [1], experts, cap, 256),
-        info,
-        [kept_in_vmem(swapped), kept_in_vmem(w_in)],
-        [(near_shape, inner_cuts(1, 0))],
-        alias=own_part,
-        flops=2 * slots * width * chans,
+        [kept_in_vmem(array) for array in (own, swapped, w_in, w_state[0], *steps)],
+        [(shape(experts, 2, cap, chans + LANES), once)],
+        flops=4 * slots * width * (chans + LANES),
     )[0]
     distant = []
     for k in range(1, chips):
-        arrived = tie([permute(own, hop(k))], near, hbm=True)[0]
+        arrived = tie([permute(own, hop(k))], [near], hbm=True)[0]
         distant += [arrived, permute(arrived, swap)]
     far = call(
-        functools.partial(peers_kernel, far_count, experts, cap, 256),
+        functools.partial(project_kernel, far_count, experts, cap, 256),
         info,
         [full(rows) for rows in distant] + [columns(w_flat, chans, chans)],
-        [(shape(far_count, cap, chans), once)] * experts,
+        [(shape(experts, far_count, cap, chans), once)],
         flops=2 * far_count * slots * width * chans,
-    )
+    )[0]
     near_back = exchange(near)
-    far_back = exchange_peers(far)
+    far_back = exchange(far)
 
     def gates(rows, by_peer):
         return call(
@@ -575,16 +522,15 @@
 
     gate_near = gates([own, swapped], True)
     gate_far = gates(distant, False)
-    out_weight = staged(w_out[0], 0, width, near_back)
-
-    lanes = everything + (pl.ds(chans, LANES),)
+
+    lanes = (slice(None),) * 3 + (pl.ds(chans, LANES),)
     side = call(
         functools.partial(side_kernel, experts, cap),
         info,
         [(near_back, (experts, 2, cap, LANES), [(lanes, Ellipsis)])],
         [(shape(tok_rows, 2 * LANES), once)],
         small=[ids],
-        after=[far[0], gate_near[0], gate_far[0]],
+        after=[far, gate_near[0], gate_far[0]],
         flops=2 * slots * tok_rows * 2 * LANES,
     )[0]
     sides = jnp.stack(spread(side))
@@ -601,54 +547,44 @@
     chan_rows = jnp.pad(chan_rows, ((0, 2), (0, 0)))
     cfg = (experts, cap, tok_rows, nstate, chans, heads)
     each = list(range(shards))
-    weights, kept, tail, last, placed = call(
-        functools.partial(factors_kernel, cfg),
-        info, [full(near_back), kept_in_vmem(sides)],
-        [
-            (shape(shards, heads // 2, tok_rows, 2 * tok_rows), None),
-            (shape(shards, tok_rows, chans), None),
-            (shape(shards, tok_rows, chans), None),
-            (jax.ShapeDtypeStruct((shards, 8, chans), F32), None),
-            (shape(2, tok_rows, chans), None),
-        ],
-        small=[ids, head_rows],
-        flops=2 * tok_rows * chans * (2 * slots + shards * 512),
-        exps=shards * tok_rows * tok_rows * heads,
-    )
-    *near_out, far_out = call(
+    made = call(
         functools.partial(scan_kernel, cfg),
         info,
-        [kept_in_vmem(sides), kept_in_vmem(placed)]
-        + [full(piece) for piece in far_back]
-        + [kept_in_vmem(array) for array in (weights, kept, tail, last)],
+        [full(near_back), kept_in_vmem(sides), kept_in_vmem(far_back)],
         [(shape(2, cap, chans), None)] * experts
         + [(shape(experts, far_count, cap, chans), None)],
-        small=[ids, chan_rows],
-        after=[gate_far[0], gate_near[0], out_weight],
+        small=[ids, head_rows, chan_rows],
+        passed=[w_out[0], *gate_near, *gate_far],
         scratch=[
             pltpu.VMEM((8 + shards * tok_rows, chans), F32),
             pltpu.VMEM((shards * tok_rows, chans), BF16),
         ],
-        flops=2 * shards * tok_rows * chans * (2 * slots + 2 * nstate + 2 * tok_rows),
+        flops=2 * shards * tok_rows * chans * (2 * slots + 2 * nstate + 2 * tok_rows + 768),
+        exps=shards * tok_rows * tok_rows * heads,
     )
+    near_out, far_out, out_weight = made[:experts], made[experts], made[experts + 1]
+    gate_near, gate_far = made[experts + 2 : experts + 4], made[experts + 4 :]
     far_ret = exchange(far_out)
-    near_ret = exchange_peers(tie(near_out, far_ret))
-
     def output(scanned, gate, at, after=()):
         return call(
             functools.partial(output_kernel, at, experts, cap, 512),
             info,
-            [kept_in_vmem(part) for part in scanned] + [full(gate), kept_in_vmem(out_weight)],
+            [kept_in_vmem(part) for part in scanned] + [kept_in_vmem(gate), kept_in_vmem(out_weight)],
             [(shape(experts, cap, width), None)],
-            after=after,
+            after_vmem=after,
             flops=2 * slots * width * chans,
         )[0]
 
-    hopped = []
     others = [permute(output([far_ret], gate_far[2 * k - 1], 2 * k - 1), swap) for k in range(1, chips)]
+    pairs = []
     for k in range(1, chips):
         pair = output([far_ret], gate_far[2 * k - 2], 2 * k - 2).astype(F32) + others[k - 1].astype(F32)
-        hopped.append(permute(pair.astype(BF16), hop(chips - k)))
+        pairs.append(pair.astype(BF16))
+    hopped = [permute(pair, hop(chips - k)) for k, pair in enumerate(pairs, 1)]
+    near_out = tie(near_out, after_vmem=[far_ret])
+    cut = experts // 2
+    near_out = tie(near_out[:cut], after_vmem=pairs) + near_out[cut:]
+    near_ret = exchange_peers(near_out)
     part_swap = permute(output(near_ret, gate_near[1], 1), swap)
     part_own = output(near_ret, gate_near[0], 0, hopped)
     summed = part_own.astype(F32) + part_swap.astype(F32)

time: 239 us -> 231 us (0.967)
  waiting for transfers between devices: 47.2 us -> 75.2 us
  Pallas kernels: 66.8 us -> 52.9 us
  starting transfers between devices: 39.9 us -> 28.9 us
  local copies, waits for them, and re-layouts: 21 us -> 12.1 us
    ppermute x12, waiting for transfers between devices: 23.3 us -> 40.6 us  [permute(): return lax.ppermute(value, 'context', pairs)]
    ppermute x14 -> x7, starting transfers between devices: 22.2 us -> 9.24 us  [exchange_peers(): lax.ppermute(pieces[r], 'expert', [(e, e ^ r) for e in range(experts)])]
    pallas_call x14 -> x12, Pallas kernels: 62.4 us -> 50.7 us  [call(): pl.pallas_call(body, out_shape=[(pltpu.HBM if pieces else pltpu.VMEM)(o.s...]
    all_to_all x2 -> x3, waiting for transfers between devices: 10.7 us -> 19.3 us  [exchange(): lax.all_to_all(value, 'expert', split_axis=0, concat_axis=0, tiled=True)]
    unnamed x66 -> x20, local copies, waits for them, and re-layouts: 20 us -> 11.5 us
    all_to_all x2 -> x3, starting transfers between devices: 11.3 us -> 15.3 us  [exchange(): lax.all_to_all(value, 'expert', split_axis=0, concat_axis=0, tiled=True)]
    ppermute x14 -> x7, waiting for transfers between devices: 13.3 us -> 15.3 us  [exchange_peers(): lax.ppermute(pieces[r], 'expert', [(e, e ^ r) for e in range(experts)])]
  transfers between devices with their start and end apart: 28 -> 22, of which waited for: 10 -> 13; matrix products, arithmetic and copies ran while one was open for 5% -> 5% of each run, Pallas kernels for 21% -> 15%
where the time goes in v2:
time: 231 us
  waiting for transfers between devices  75.2 us (33%)
  blocking collectives  59.3 us (26%)
  Pallas kernels  52.9 us (23%)
  starting transfers between devices  28.9 us (13%)
  local copies, waits for them, and re-layouts  12.1 us (5%)
    all_to_all x2, blocking collectives, exchange(): lax.all_to_all(value, 'expert', split_axis=0, concat_axis=0, tiled=True)  59.3 us
    pallas_call x12, Pallas kernels, call(): pl.pallas_call(body, out_shape=[(pltpu.HBM if pieces else pltpu.VMEM)(o.s...  50.7 us
    ppermute x12, waiting for transfers between devices, permute(): return lax.ppermute(value, 'context', pairs)  40.6 us
    all_to_all x3, waiting for transfers between devices, exchange(): lax.all_to_all(value, 'expert', split_axis=0, concat_axis=0, tiled=True)  19.3 us
    ppermute x7, waiting for transfers between devices, exchange_peers(): lax.ppermute(pieces[r], 'expert', [(e, e ^ r) for e in range(experts)])  15.3 us
    all_to_all x3, starting transfers between devices, exchange(): lax.all_to_all(value, 'expert', split_axis=0, concat_axis=0, tiled=True)  15.3 us
    unnamed x20, local copies, waits for them, and re-layouts  11.5 us
    ppermute x7, starting transfers between devices, exchange_peers(): lax.ppermute(pieces[r], 'expert', [(e, e ^ r) for e in range(experts)])  9.24 us
  transfers between devices with their start and end apart: 22, of which 13 were waited for; matrix products, arithmetic and copies ran while one was open for 5% of the time, Pallas kernels for 15%

profile of v2, /device:TPU:0, one launch (start us, length us, event | category | flops | bytes accessed | tf_op | source)
XLA Modules:
  0.0 230.9 jit_solution(18245120590821400649)
XLA Ops:
  0.1 3.1 %shard_map.109.refs_1_ = bf16[256,2048]{1,0:T(8,128)(2,1)} custom-call(s32[14]{0:T(128)S(1)} %concatenate.9.refs_0_, s32[4,1,128]{2,1,0:T(1,128)} %bitcast.29, bf16[128,2048]{1,0:T(8,128)(2,1)} %bitcast.42), custom_call_target="tpu_custom_call" | custom-call | flops 134217728 | bytes 1573888 | tf_op jit(solution)/shard_map/pallas_call | solution.py:181
  3.2 7.3 %all-to-all-start = ((bf16[8,32,2048]{2,1,0:T(8,128)(2,1)}), bf16[8,32,2048]{2,1,0:T(8,128)(2,1)S(1)}, u32[]{:S(2)}, u32[]{:S(2)}) async-start(bf16[8,32,2048]{2,1,0:T(8,128)(2,1)} %bitcast.39), calls=%async_computation | async-start | bytes 2097152 | tf_op jit(solution)/shard_map/all_to_all | solution.py:469
  12.5 2.8 %collective-permute-done.1.refs_4_.refs_7_ = bf16[16,2048]{1,0:T(8,128)(2,1)S(1)} collective-permute-done((bf16[16,2048]{1,0:T(8,128)(2,1)S(1)}, bf16[16,2048]{1,0:T(8,128)(2,1)S(1)}, u32[]{:S(2)}, u32[]{:S(2)}) %collective-permute-start.1) | collective-permute-done | bytes 65568 | tf_op jit(solution)/shard_map/ppermute | solution.py:459
  15.3 10.2 %copy.29 = bf16[256,8,2,1024]{3,1,2,0:T(8,128)(2,1)} copy(bf16[256,8,2,1024]{3,2,1,0:T(2,128)(2,1)} %bitcast.40) | data formatting | bytes 16777216
  25.5 10.8 %all-to-all-done.refs_0_ = bf16[8,32,2048]{2,1,0:T(8,128)(2,1)S(1)} async-done(((bf16[8,32,2048]{2,1,0:T(8,128)(2,1)}), bf16[8,32,2048]{2,1,0:T(8,128)(2,1)S(1)}, u32[]{:S(2)}, u32[]{:S(2)}) %all-to-all-start) | async-done | bytes 1048608 | tf_op jit(solution)/shard_map/all_to_all | solution.py:469
  39.9 4.5 %shard_map.113.refs_1_.refs_4_ = bf16[8,2,32,1152]{3,2,1,0:T(8,128)(2,1)} custom-call(s32[14]{0:T(128)S(1)} %concatenate.9.refs_0_, bf16[8,32,2048]{2,1,0:T(8,128)(2,1)S(1)} %shard_map.111._.refs_1_, bf16[8,32,2048]{2,1,0:T(8,128)(2,1)S(1)} %collective-permute-done.3.refs_2_, bf16[2048,1024]{1,0:T(8,128)(2,1)S(1)} %shard_map.112.refs_3_, ...), custom_call_target="tpu_custom_call" | custom-call | flops 2415919104 | bytes 8257536 | tf_op jit(solution)/shard_map/pallas_call | solution.py:181
  44.4 4.3 %all-to-all-start.1 = ((bf16[8,2,32,1152]{3,2,1,0:T(8,128)(2,1)}), bf16[8,2,32,1152]{3,2,1,0:T(8,128)(2,1)}, u32[]{:S(2)}, u32[]{:S(2)}) async-start(bf16[8,2,32,1152]{3,2,1,0:T(8,128)(2,1)} %shard_map.113.refs_1_.refs_4_), calls=%async_computation.1 | async-start | bytes 2359296 | tf_op jit(solution)/shard_map/all_to_all | solution.py:469
  48.7 13.2 %collective-permute-done.4.refs_0_ = bf16[8,32,2048]{2,1,0:T(8,128)(2,1)} collective-permute-done((bf16[8,32,2048]{2,1,0:T(8,128)(2,1)S(1)}, bf16[8,32,2048]{2,1,0:T(8,128)(2,1)}, u32[]{:S(2)}, u32[]{:S(2)}) %collective-permute-start.4) | collective-permute-done | bytes 1048608 | tf_op jit(solution)/shard_map/ppermute | solution.py:459
  61.9 2.9 %collective-permute-done.5.refs_2_ = bf16[8,32,2048]{2,1,0:T(8,128)(2,1)S(1)} collective-permute-done((bf16[8,32,2048]{2,1,0:T(8,128)(2,1)}, bf16[8,32,2048]{2,1,0:T(8,128)(2,1)S(1)}, u32[]{:S(2)}, u32[]{:S(2)}) %collective-permute-start.5) | collective-permute-done | bytes 1048608 | tf_op jit(solution)/shard_map/ppermute | solution.py:459
  65.8 7.4 %shard_map.115.refs_3_ = bf16[8,2,32,1024]{3,2,1,0:T(8,128)(2,1)} custom-call(s32[14]{0:T(128)S(1)} %concatenate.9.refs_0_, bf16[8,32,2048]{2,1,0:T(8,128)(2,1)} %shard_map.114.refs_1_, bf16[8,32,2048]{2,1,0:T(8,128)(2,1)} %copy-done.2, bf16[2048,2048]{1,0:T(8,128)(2,1)} %bitcast.36), custom_call_target="tpu_custom_call" | custom-call | flops 2147483648 | bytes 11534336 | tf_op jit(solution)/shard_map/pallas_call | solution.py:181
  73.3 4.7 %all-to-all-done.1.refs_2_.refs_4_ = bf16[8,2,32,1152]{3,2,1,0:T(8,128)(2,1)} async-done(((bf16[8,2,32,1152]{3,2,1,0:T(8,128)(2,1)}), bf16[8,2,32,1152]{3,2,1,0:T(8,128)(2,1)}, u32[]{:S(2)}, u32[]{:S(2)}) %all-to-all-start.1) | async-done | bytes 1179680 | tf_op jit(solution)/shard_map/all_to_all | solution.py:469
  78.0 3.7 %all-to-all-start.2 = ((bf16[8,2,32,1024]{3,2,1,0:T(8,128)(2,1)}), bf16[8,2,32,1024]{3,2,1,0:T(8,128)(2,1)S(1)}, u32[]{:S(2)}, u32[]{:S(2)}) async-start(bf16[8,2,32,1024]{3,2,1,0:T(8,128)(2,1)} %shard_map.115.refs_3_), calls=%async_computation.2 | async-start | bytes 2097152 | tf_op jit(solution)/shard_map/all_to_all | solution.py:469
  81.8 6.1 %shard_map.116 = (bf16[256,1024]{1,0:T(8,128)(2,1)}, bf16[256,1024]{1,0:T(8,128)(2,1)}) custom-call(s32[14]{0:T(128)S(1)} %concatenate.9.refs_0_, bf16[8,32,2048]{2,1,0:T(8,128)(2,1)S(1)} %shard_map.111._.refs_1_, bf16[8,32,2048]{2,1,0:T(8,128)(2,1)S(1)} %collective-permute-done.3.refs_2_, bf16[2048,2048]{1,0:T(8,128)(2,1)} %bitcast.37, ...), custom_call_target="tpu_custom_call" | custom-call | flops 2147483648 | bytes 11534336 | tf_op jit(solution)/shard_map/pallas_call | solution.py:181
  87.9 6.8 %shard_map.117 = (bf16[256,1024]{1,0:T(8,128)(2,1)}, bf16[256,1024]{1,0:T(8,128)(2,1)}) custom-call(s32[14]{0:T(128)S(1)} %concatenate.9.refs_0_, bf16[8,32,2048]{2,1,0:T(8,128)(2,1)} %shard_map.114.refs_1_, bf16[8,32,2048]{2,1,0:T(8,128)(2,1)} %copy-done.2, bf16[2048,2048]{1,0:T(8,128)(2,1)} %bitcast.38, bf16[8,2,32,1152]{3,2,1,0:T(8,128)(2,1)} %shard_map.113.refs_1_.refs_4_), custom_call_target="tpu_custom_call" | custom-call | flops 2147483648 | bytes 11534336 | tf_op jit(solution)/shard_map/pallas_call | solution.py:181
  97.9 3.7 %collective-permute-done.7 = bf16[128,256]{1,0:T(8,128)(2,1)S(1)} collective-permute-done((bf16[128,256]{1,0:T(8,128)(2,1)}, bf16[128,256]{1,0:T(8,128)(2,1)S(1)}, u32[]{:S(2)}, u32[]{:S(2)}) %collective-permute-start.7) | collective-permute-done | bytes 65568 | tf_op jit(solution)/shard_map/ppermute | solution.py:459
  103.7 3.9 %all-to-all-done.2.refs_6_ = bf16[8,2,32,1024]{3,2,1,0:T(8,128)(2,1)S(1)} async-done(((bf16[8,2,32,1024]{3,2,1,0:T(8,128)(2,1)}), bf16[8,2,32,1024]{3,2,1,0:T(8,128)(2,1)S(1)}, u32[]{:S(2)}, u32[]{:S(2)}) %all-to-all-start.2) | async-done | bytes 1048608 | tf_op jit(solution)/shard_map/all_to_all | solution.py:469
  107.6 11.3 %shard_map.119 = (bf16[2,32,1024]{2,1,0:T(8,128)(2,1)S(1)}, bf16[2,32,1024]{2,1,0:T(8,128)(2,1)S(1)}, bf16[2,32,1024]{2,1,0:T(8,128)(2,1)S(1)}, bf16[2,32,1024]{...) custom-call(s32[14]{0:T(128)S(1)} %concatenate.9.refs_0_, ...), custom_call_target="tpu_custom_call" | custom-call | flops 1744830464 | bytes 4587520 | tf_op jit(solution)/shard_map/pallas_call | solution.py:181
  118.9 29.3 %all_to_all.25.refs_8_.refs_1_ = bf16[8,2,32,1024]{3,2,1,0:T(8,128)(2,1)S(1)} all-to-all(bf16[8,2,32,1024]{3,2,1,0:T(8,128)(2,1)S(1)} %get-tuple-element.47), channel_id=1, replica_groups=mesh['expert'=8,'context'=4] {'expert'}, dimensions={0} | all-to-all | bytes 2097152 | tf_op jit(solution)/shard_map/all_to_all | solution.py:469
  151.3 2.7 %collective-permute-start.14 = (bf16[2,32,1024]{2,1,0:T(8,128)(2,1)S(1)}, bf16[2,32,1024]{2,1,0:T(8,128)(2,1)S(1)}, u32[]{:S(2)}, u32[]{:S(2)}) collective-permute-start(bf16[2,32,1024]{2,1,0:T(8,128)(2,1)S(1)} %get-tuple-element.60), channel_id=1, source_target_pairs={{0,20},{4,16},{8,28},{12,24},{16,4},{20,0},{24,12},{28,8},{1,21},{... | collective-permute-start | bytes 393224 | tf_op jit(solution)/shard_map/ppermute | solution.py:473
  161.7 7.0 %collective-permute-done.13.refs_5_ = bf16[2,32,1024]{2,1,0:T(8,128)(2,1)S(1)} collective-permute-done((bf16[2,32,1024]{2,1,0:T(8,128)(2,1)S(1)}, bf16[2,32,1024]{2,1,0:T(8,128)(2,1)S(1)}, u32[]{:S(2)}, u32[]{:S(2)}) %collective-permute-start.13) | collective-permute-done | bytes 131104 | tf_op jit(solution)/shard_map/ppermute | solution.py:473
  168.7 2.6 %collective-permute-done.14.refs_6_ = bf16[2,32,1024]{2,1,0:T(8,128)(2,1)S(1)} collective-permute-done((bf16[2,32,1024]{2,1,0:T(8,128)(2,1)S(1)}, bf16[2,32,1024]{2,1,0:T(8,128)(2,1)S(1)}, u32[]{:S(2)}, u32[]{:S(2)}) %collective-permute-start.14) | collective-permute-done | bytes 131104 | tf_op jit(solution)/shard_map/ppermute | solution.py:473
  173.9 3.7 %collective-permute-done.12.refs_4_ = bf16[2,32,1024]{2,1,0:T(8,128)(2,1)S(1)} collective-permute-done((bf16[2,32,1024]{2,1,0:T(8,128)(2,1)S(1)}, bf16[2,32,1024]{2,1,0:T(8,128)(2,1)S(1)}, u32[]{:S(2)}, u32[]{:S(2)}) %collective-permute-start.12) | collective-permute-done | bytes 131104 | tf_op jit(solution)/shard_map/ppermute | solution.py:473
  179.5 16.8 %collective-permute-done.17.refs_11_ = bf16[8,32,2048]{2,1,0:T(8,128)(2,1)S(1)} collective-permute-done((bf16[8,32,2048]{2,1,0:T(8,128)(2,1)S(1)}, bf16[8,32,2048]{2,1,0:T(8,128)(2,1)S(1)}, u32[]{:S(2)}, u32[]{:S(2)}) %collective-permute-start.17) | collective-permute-done | bytes 1048608 | tf_op jit(solution)/shard_map/ppermute | solution.py:459
  198.8 30.0 %all_to_all.26 = bf16[8,32,2048]{2,1,0:T(8,128)(2,1)S(1)} all-to-all(bf16[8,32,2048]{2,1,0:T(8,128)(2,1)S(1)} %add_convert_fusion), channel_id=1, replica_groups=mesh['expert'=8,'context'=4] {'expert'}, dimensions={0} | all-to-all | bytes 2097152 | tf_op jit(solution)/shard_map/all_to_all | solution.py:469
  (74 shorter events, 31.7 us)
Async XLA Ops:
  0.0 10.5 %copy-start.3 = (bf16[1,2048,16]{1,2,0:T(8,128)(2,1)S(1)}, bf16[1,2048,16]{1,2,0:T(8,128)(2,1)}, u32[]{:S(2)}) copy-start(bf16[1,2048,16]{1,2,0:T(8,128)(2,1)} %param.15) | copy-start | bytes 196612
  3.2 33.1 %all-to-all-start = ((bf16[8,32,2048]{2,1,0:T(8,128)(2,1)}), bf16[8,32,2048]{2,1,0:T(8,128)(2,1)S(1)}, u32[]{:S(2)}, u32[]{:S(2)}) async-start(bf16[8,32,2048]{2,1,0:T(8,128)(2,1)} %bitcast.39), calls=%async_computation | async-start | bytes 2097152 | tf_op jit(solution)/shard_map/all_to_all | solution.py:469
  10.9 4.3 %collective-permute-start.1 = (bf16[16,2048]{1,0:T(8,128)(2,1)S(1)}, bf16[16,2048]{1,0:T(8,128)(2,1)S(1)}, u32[]{:S(2)}, u32[]{:S(2)}) collective-permute-start(bf16[16,2048]{1,0:T(8,128)(2,1)S(1)} %bitcast.25), channel_id=1, source_target_pairs={{0,2},{1,3},{2,0},{3,1},{4,6},{5,7},{6,4},{7,5},{8,10},{9,11},{10,... | collective-permute-start | bytes 196616 | tf_op jit(solution)/shard_map/ppermute | solution.py:459
  12.5 13.0 %collective-permute-start = (bf16[16,2048]{1,0:T(8,128)(2,1)S(1)}, bf16[16,2048]{1,0:T(8,128)(2,1)S(1)}, u32[]{:S(2)}, u32[]{:S(2)}) collective-permute-start(bf16[16,2048]{1,0:T(8,128)(2,1)S(1)} %bitcast.26), channel_id=1, source_target_pairs={{0,1},{1,0},{2,3},{3,2},{4,5},{5,4},{6,7},{7,6},{8,9},{9,8},{10,11... | collective-permute-start | bytes 196616 | tf_op jit(solution)/shard_map/ppermute | solution.py:459
  15.3 10.2 %collective-permute-start.2 = (bf16[16,2048]{1,0:T(8,128)(2,1)S(1)}, bf16[16,2048]{1,0:T(8,128)(2,1)S(1)}, u32[]{:S(2)}, u32[]{:S(2)}) collective-permute-start(bf16[16,2048]{1,0:T(8,128)(2,1)S(1)} %collective-permute-done.1.refs_4_.refs_7_), channel_id=1, source_target_pairs={{0,1},{1,0},{2,3},{3,2},{4,5},{5,4},{6,7},{7,6},{8,9},{9,8},{10,11... | collective-permute-start | bytes 196616 | tf_op jit(solution)/shard_map/ppermute | solution.py:459
  36.2 3.7 %collective-permute-start.3 = (bf16[8,32,2048]{2,1,0:T(8,128)(2,1)S(1)}, bf16[8,32,2048]{2,1,0:T(8,128)(2,1)S(1)}, u32[]{:S(2)}, u32[]{:S(2)}) collective-permute-start(bf16[8,32,2048]{2,1,0:T(8,128)(2,1)S(1)} %shard_map.111._.refs_1_), channel_id=1, source_target_pairs={{0,1},{1,0},{2,3},{3,2},{4,5},{5,4},{6,7},{7,6},{8,9},{9,8},{10,11... | collective-permute-start | bytes 3145736 | tf_op jit(solution)/shard_map/ppermute | solution.py:459
  36.2 25.7 %collective-permute-start.4 = (bf16[8,32,2048]{2,1,0:T(8,128)(2,1)S(1)}, bf16[8,32,2048]{2,1,0:T(8,128)(2,1)}, u32[]{:S(2)}, u32[]{:S(2)}) collective-permute-start(bf16[8,32,2048]{2,1,0:T(8,128)(2,1)S(1)} %shard_map.111._.refs_1_), channel_id=1, source_target_pairs={{0,2},{1,3},{2,0},{3,1},{4,6},{5,7},{6,4},{7,5},{8,10},{9,11},{10,... | collective-permute-start | bytes 3145736 | tf_op jit(solution)/shard_map/ppermute | solution.py:459
  44.4 33.5 %all-to-all-start.1 = ((bf16[8,2,32,1152]{3,2,1,0:T(8,128)(2,1)}), bf16[8,2,32,1152]{3,2,1,0:T(8,128)(2,1)}, u32[]{:S(2)}, u32[]{:S(2)}) async-start(bf16[8,2,32,1152]{3,2,1,0:T(8,128)(2,1)} %shard_map.113.refs_1_.refs_4_), calls=%async_computation.1 | async-start | bytes 2359296 | tf_op jit(solution)/shard_map/all_to_all | solution.py:469
  61.9 2.9 %collective-permute-start.5 = (bf16[8,32,2048]{2,1,0:T(8,128)(2,1)}, bf16[8,32,2048]{2,1,0:T(8,128)(2,1)S(1)}, u32[]{:S(2)}, u32[]{:S(2)}) collective-permute-start(bf16[8,32,2048]{2,1,0:T(8,128)(2,1)} %shard_map.114.refs_1_), channel_id=1, source_target_pairs={{0,1},{1,0},{2,3},{3,2},{4,5},{5,4},{6,7},{7,6},{8,9},{9,8},{10,11... | collective-permute-start | bytes 3145736 | tf_op jit(solution)/shard_map/ppermute | solution.py:459
  73.2 8.5 %copy-start.8 = (f32[16]{0:T(128)S(1)}, f32[16]{0:T(128)}, u32[]{:S(2)}) copy-start(f32[16]{0:T(128)} %param.17) | copy-start | bytes 196
  78.0 29.6 %all-to-all-start.2 = ((bf16[8,2,32,1024]{3,2,1,0:T(8,128)(2,1)}), bf16[8,2,32,1024]{3,2,1,0:T(8,128)(2,1)S(1)}, u32[]{:S(2)}, u32[]{:S(2)}) async-start(bf16[8,2,32,1024]{3,2,1,0:T(8,128)(2,1)} %shard_map.115.refs_3_), calls=%async_computation.2 | async-start | bytes 2097152 | tf_op jit(solution)/shard_map/all_to_all | solution.py:469
  97.0 4.5 %collective-permute-start.7 = (bf16[128,256]{1,0:T(8,128)(2,1)}, bf16[128,256]{1,0:T(8,128)(2,1)S(1)}, u32[]{:S(2)}, u32[]{:S(2)}) collective-permute-start(bf16[128,256]{1,0:T(8,128)(2,1)} %shard_map.118), channel_id=1, source_target_pairs={{0,2},{1,3},{2,0},{3,1},{4,6},{5,7},{6,4},{7,5},{8,10},{9,11},{10,... | collective-permute-start | bytes 196616 | tf_op jit(solution)/shard_map/ppermute | solution.py:459
  97.9 3.8 %collective-permute-start.6 = (bf16[128,256]{1,0:T(8,128)(2,1)}, bf16[128,256]{1,0:T(8,128)(2,1)S(1)}, u32[]{:S(2)}, u32[]{:S(2)}) collective-permute-start(bf16[128,256]{1,0:T(8,128)(2,1)} %shard_map.118), channel_id=1, source_target_pairs={{0,1},{1,0},{2,3},{3,2},{4,5},{5,4},{6,7},{7,6},{8,9},{9,8},{10,11... | collective-permute-start | bytes 196616 | tf_op jit(solution)/shard_map/ppermute | solution.py:459
  101.6 1.3 collective-permute-start.8
  150.1 9.7 %collective-permute-start.9 = (bf16[8,32,2048]{2,1,0:T(8,128)(2,1)S(1)}, bf16[8,32,2048]{2,1,0:T(8,128)(2,1)S(1)}, u32[]{:S(2)}, u32[]{:S(2)}) collective-permute-start(bf16[8,32,2048]{2,1,0:T(8,128)(2,1)S(1)} %shard_map.122), channel_id=1, source_target_pairs={{0,1},{1,0},{2,3},{3,2},{4,5},{5,4},{6,7},{7,6},{8,9},{9,8},{10,11... | collective-permute-start | bytes 3145736 | tf_op jit(solution)/shard_map/ppermute | solution.py:459
  150.2 18.5 %collective-permute-start.13 = (bf16[2,32,1024]{2,1,0:T(8,128)(2,1)S(1)}, bf16[2,32,1024]{2,1,0:T(8,128)(2,1)S(1)}, u32[]{:S(2)}, u32[]{:S(2)}) collective-permute-start(bf16[2,32,1024]{2,1,0:T(8,128)(2,1)S(1)} %get-tuple-element.59), channel_id=1, source_target_pairs={{0,16},{4,20},{8,24},{12,28},{16,0},{20,4},{24,8},{28,12},{1,17},{... | collective-permute-start | bytes 393224 | tf_op jit(solution)/shard_map/ppermute | solution.py:473
  151.3 19.9 %collective-permute-start.14 = (bf16[2,32,1024]{2,1,0:T(8,128)(2,1)S(1)}, bf16[2,32,1024]{2,1,0:T(8,128)(2,1)S(1)}, u32[]{:S(2)}, u32[]{:S(2)}) collective-permute-start(bf16[2,32,1024]{2,1,0:T(8,128)(2,1)S(1)} %get-tuple-element.60), channel_id=1, source_target_pairs={{0,20},{4,16},{8,28},{12,24},{16,4},{20,0},{24,12},{28,8},{1,21},{... | collective-permute-start | bytes 393224 | tf_op jit(solution)/shard_map/ppermute | solution.py:473
  154.1 17.2 %collective-permute-start.15 = (bf16[2,32,1024]{2,1,0:T(8,128)(2,1)S(1)}, bf16[2,32,1024]{2,1,0:T(8,128)(2,1)S(1)}, u32[]{:S(2)}, u32[]{:S(2)}) collective-permute-start(bf16[2,32,1024]{2,1,0:T(8,128)(2,1)S(1)} %get-tuple-element.61), channel_id=1, source_target_pairs={{0,24},{4,28},{8,16},{12,20},{16,8},{20,12},{24,0},{28,4},{1,25},{... | collective-permute-start | bytes 393224 | tf_op jit(solution)/shard_map/ppermute | solution.py:473
  155.5 16.3 %collective-permute-start.16 = (bf16[2,32,1024]{2,1,0:T(8,128)(2,1)S(1)}, bf16[2,32,1024]{2,1,0:T(8,128)(2,1)S(1)}, u32[]{:S(2)}, u32[]{:S(2)}) collective-permute-start(bf16[2,32,1024]{2,1,0:T(8,128)(2,1)S(1)} %get-tuple-element.62), channel_id=1, source_target_pairs={{0,28},{4,24},{8,20},{12,16},{16,12},{20,8},{24,4},{28,0},{1,29},{... | collective-permute-start | bytes 393224 | tf_op jit(solution)/shard_map/ppermute | solution.py:473
  160.2 11.6 %collective-permute-start.10 = (bf16[2,32,1024]{2,1,0:T(8,128)(2,1)S(1)}, bf16[2,32,1024]{2,1,0:T(8,128)(2,1)S(1)}, u32[]{:S(2)}, u32[]{:S(2)}) collective-permute-start(bf16[2,32,1024]{2,1,0:T(8,128)(2,1)S(1)} %get-tuple-element.56), channel_id=1, source_target_pairs={{0,4},{4,0},{8,12},{12,8},{16,20},{20,16},{24,28},{28,24},{1,5},{5... | collective-permute-start | bytes 393224 | tf_op jit(solution)/shard_map/ppermute | solution.py:473
  168.7 5.2 %collective-permute-start.11 = (bf16[2,32,1024]{2,1,0:T(8,128)(2,1)S(1)}, bf16[2,32,1024]{2,1,0:T(8,128)(2,1)S(1)}, u32[]{:S(2)}, u32[]{:S(2)}) collective-permute-start(bf16[2,32,1024]{2,1,0:T(8,128)(2,1)S(1)} %get-tuple-element.57), channel_id=1, source_target_pairs={{0,8},{4,12},{8,0},{12,4},{16,24},{20,28},{24,16},{28,20},{1,9},{5... | collective-permute-start | bytes 393224 | tf_op jit(solution)/shard_map/ppermute | solution.py:473
  171.3 6.3 %collective-permute-start.12 = (bf16[2,32,1024]{2,1,0:T(8,128)(2,1)S(1)}, bf16[2,32,1024]{2,1,0:T(8,128)(2,1)S(1)}, u32[]{:S(2)}, u32[]{:S(2)}) collective-permute-start(bf16[2,32,1024]{2,1,0:T(8,128)(2,1)S(1)} %get-tuple-element.58), channel_id=1, source_target_pairs={{0,12},{4,8},{8,4},{12,0},{16,28},{20,24},{24,20},{28,16},{1,13},{... | collective-permute-start | bytes 393224 | tf_op jit(solution)/shard_map/ppermute | solution.py:473
  171.3 25.1 %collective-permute-start.17 = (bf16[8,32,2048]{2,1,0:T(8,128)(2,1)S(1)}, bf16[8,32,2048]{2,1,0:T(8,128)(2,1)S(1)}, u32[]{:S(2)}, u32[]{:S(2)}) collective-permute-start(bf16[8,32,2048]{2,1,0:T(8,128)(2,1)S(1)} %add_convert_fusion.1.refs_4_), channel_id=1, source_target_pairs={{0,2},{1,3},{2,0},{3,1},{4,6},{5,7},{6,4},{7,5},{8,10},{9,11},{10,... | collective-permute-start | bytes 3145736 | tf_op jit(solution)/shard_map/ppermute | solution.py:459
  179.4 18.8 %collective-permute-start.18 = (bf16[8,32,2048]{2,1,0:T(8,128)(2,1)S(1)}, bf16[8,32,2048]{2,1,0:T(8,128)(2,1)S(1)}, u32[]{:S(2)}, u32[]{:S(2)}) collective-permute-start(bf16[8,32,2048]{2,1,0:T(8,128)(2,1)S(1)} %shard_map.125), channel_id=1, source_target_pairs={{0,1},{1,0},{2,3},{3,2},{4,5},{5,4},{6,7},{7,6},{8,9},{9,8},{10,11... | collective-permute-start | bytes 3145736 | tf_op jit(solution)/shard_map/ppermute | solution.py:459
  (7 other events, 36.9 us)

commit v3 on v2

--- a/solution.py
+++ b/solution.py
@@ -28,13 +28,13 @@
     return pieces.reshape(count * rows, lanes)
 
 
-def slot_rows(ids, experts, cap, me=0):
+def slot_rows(ids, experts, cap):
     tok_rows = ids.shape[1]
     onehot = jnp.where(iota((experts, tok_rows), 0) == ids, 1.0, 0.0)
     upto = jnp.where(iota((tok_rows, tok_rows), 0) <= iota((tok_rows, tok_rows), 1), 1.0, 0.0)
     before = dot(onehot.astype(BF16), upto.astype(BF16))
     rank = jnp.sum(onehot * before, axis=0, keepdims=True) - 1.0
-    slot = (ids ^ me) * cap + rank.astype(jnp.int32)
+    slot = ids * cap + rank.astype(jnp.int32)
     return jnp.where(iota((experts * cap, tok_rows), 0) == slot, 1.0, 0.0)
 
 
@@ -235,10 +235,6 @@
     )(in_hbm(array), in_vmem(after))
 
 
-def peer_rows(ref, me):
-    return flat_rows(jnp.stack([ref[r ^ me] for r in range(ref.shape[0])]))
-
-
 def dispatch_kernel(experts, cap, info_ref, ids, tokens, out):
     place = slot_rows(ids.whole()[info_ref[0]], experts, cap).astype(BF16)
     out.held[...] = dot(place, tokens.whole()[...]).astype(BF16)
@@ -287,13 +283,10 @@
     out.send(0)
 
 
-def gate_kernel(tile, by_peer, info_ref, *refs):
+def gate_kernel(tile, info_ref, *refs):
     count = len(refs) // 2
     weight, outs = refs[count], refs[count + 1 :]
-    if by_peer:
-        rows = [peer_rows(ref.whole(), info_ref[info_ref.shape[0] - 1]) for ref in refs[:count]]
-    else:
-        rows = [flat_rows(ref.whole()[...]) for ref in refs[:count]]
+    rows = [flat_rows(ref.whole()[...]) for ref in refs[:count]]
     for lo in range(0, weight.held.shape[1], tile):
         part = weight.whole()[:, lo : lo + tile]
         for block, out in zip(rows, outs):
@@ -302,20 +295,13 @@
         out.send(0)
 
 
-def output_kernel(at, experts, cap, tile, info_ref, *refs):
-    scanned, gate, weight, out = refs[:-3], refs[-3], refs[-2].held, refs[-1].held
-    if len(scanned) > 1:
-        me = info_ref[info_ref.shape[0] - 1]
-        rows = flat_rows(jnp.stack([ref.held[at] for ref in scanned]))
-    else:
-        me = 0
-        rows = flat_rows(scanned[0].held[:, at])
-    gates = jax.nn.silu(gate.whole()[...].astype(F32))
-    gated = (rows.astype(F32) * gates).astype(BF16)
-    for lo in range(0, weight.shape[1], tile):
-        made = dot(gated, weight[:, lo : lo + tile]).astype(BF16)
-        for r in range(experts):
-            out[r ^ me, :, lo : lo + tile] = made[r * cap : (r + 1) * cap, :]
+def output_kernel(at, experts, cap, tile, info_ref, scanned, gate, weight, out):
+    gates = jax.nn.silu(gate.held[...].astype(F32))
+    gated = (flat_rows(scanned.held[:, at]).astype(F32) * gates).astype(BF16)
+    for lo in range(0, weight.held.shape[1], tile):
+        made = dot(gated, weight.held[:, lo : lo + tile]).astype(BF16)
+        for e in range(experts):
+            out.held[e, :, lo : lo + tile] = made[e * cap : (e + 1) * cap, :]
 
 
 def scan_kernel(
@@ -332,15 +318,14 @@
     experts, cap, tok_rows, nstate, chn, heads = cfg
     blocks = ids_ref.shape[0]
     taps = 4
-    out_near, (out_far, inner_ref, made_ref) = refs[:experts], refs[experts:]
-    me = info_ref[info_ref.shape[0] - 1]
-    near_ref, far_ref, side_ref = near.whole(), far.whole(), side.whole()
+    out_near, out_far, inner_ref, made_ref = refs
+    far_ref, side_ref = far.whole(), side.whole()
     inner_ref[:8, :] = jnp.zeros((8, chn), F32)
 
-    for q in range(blocks):
+    for q in (*range(2, blocks), 0, 1):
         b = info_ref[1 + q]
         place = slot_rows(ids_ref[b], experts, cap).T.astype(BF16)
-        rows = flat_rows(near_ref[:, q, :, :chn] if q < 2 else far_ref[:, q - 2])
+        rows = flat_rows(near.whole()[:, q, :, :chn] if q < 2 else far_ref[:, q - 2])
         inner_ref[pl.ds(8 + b * tok_rows, tok_rows), :] = dot(place, rows)
 
     lower = iota((tok_rows, tok_rows), 0) >= iota((tok_rows, tok_rows), 1)
@@ -378,8 +363,9 @@
         )
         source = summed - jnp.log(step)
         source_t = source.T
-        kept = widen(jnp.exp(summed))
-        tail = widen(jnp.exp(summed[tok_rows - 1 :, :] - source))
+        left = jnp.exp(summed[tok_rows - 1 :, :] - source)
+        wide = widen(jnp.concatenate([jnp.exp(summed), left], axis=0))
+        kept, tail = wide[:tok_rows], wide[tok_rows:]
 
         both = side_ref[q, :, :LANES]
         keys_t = both.astype(F32).T.astype(BF16)[:nstate, :]
@@ -407,13 +393,13 @@
 
     for q in range(blocks):
         b = info_ref[1 + q]
-        place = slot_rows(ids_ref[b], experts, cap, me if q < 2 else 0).astype(BF16)
+        place = slot_rows(ids_ref[b], experts, cap).astype(BF16)
         start = pl.multiple_of(b * tok_rows, tok_rows)
         leaving = dot(place, made_ref[pl.ds(start, tok_rows), :]).astype(BF16)
         for e in range(experts):
             piece = leaving[e * cap : (e + 1) * cap, :]
             if q < 2:
-                out_near[e].held[q] = piece
+                out_near.held[e, q] = piece
             else:
                 out_far.held[e, q - 2] = piece
 
@@ -447,8 +433,7 @@
     order = 2 * ((here // 2 - blocks // 2) % chips) + ((here % 2) ^ (blocks % 2))
     groups = 2 * ((blocks // 2 - here // 2) % chips) + ((here % 2) ^ (blocks % 2))
     block_at = 2 * ((here // 2 - blocks // 2) % chips) + ((here % 2) ^ (blocks % 2))
-    me = lax.axis_index("expert").astype(jnp.int32)
-    info = jnp.concatenate([here[None], block_at, order, groups, me[None]])
+    info = jnp.concatenate([here[None], block_at, order, groups])
     ids = route.reshape(shards, 1, tok_rows)
     swap = [(c, c ^ 1) for c in range(shards)]
 
@@ -467,13 +452,6 @@
 
     def exchange(value):
         return lax.all_to_all(value, "expert", split_axis=0, concat_axis=0, tiled=True)
-
-    def exchange_peers(pieces):
-        sent = [
-            lax.ppermute(pieces[r], "expert", [(e, e ^ r) for e in range(experts)])
-            for r in range(experts - 1, 0, -1)
-        ]
-        return [pieces[0]] + sent[::-1]
 
     w_flat = w_inner[0].reshape(width, 2 * chans)
 
@@ -509,19 +487,19 @@
     near_back = exchange(near)
     far_back = exchange(far)
 
-    def gates(rows, by_peer):
+    def gates(rows, fetch):
         return call(
-            functools.partial(gate_kernel, 256, by_peer),
+            functools.partial(gate_kernel, 256),
             info,
-            [kept_in_vmem(part) if by_peer else full(part) for part in rows]
+            [fetch(part) for part in rows]
             + [columns(w_flat, 0, chans)],
             [(shape(slots, chans), once)] * len(rows),
             after=[near],
             flops=2 * len(rows) * slots * width * chans,
         )
 
-    gate_near = gates([own, swapped], True)
-    gate_far = gates(distant, False)
+    gate_near = gates([own, swapped], kept_in_vmem)
+    gate_far = gates(distant, full)
 
     lanes = (slice(None),) * 3 + (pl.ds(chans, LANES),)
     side = call(
@@ -547,14 +525,15 @@
     chan_rows = jnp.pad(chan_rows, ((0, 2), (0, 0)))
     cfg = (experts, cap, tok_rows, nstate, chans, heads)
     each = list(range(shards))
-    made = call(
+    near_out, far_out = call(
         functools.partial(scan_kernel, cfg),
         info,
         [full(near_back), kept_in_vmem(sides), kept_in_vmem(far_back)],
-        [(shape(2, cap, chans), None)] * experts
-        + [(shape(experts, far_count, cap, chans), None)],
+        [
+            (shape(experts, 2, cap, chans), None),
+            (shape(experts, far_count, cap, chans), None),
+        ],
         small=[ids, head_rows, chan_rows],
-        passed=[w_out[0], *gate_near, *gate_far],
         scratch=[
             pltpu.VMEM((8 + shards * tok_rows, chans), F32),
             pltpu.VMEM((shards * tok_rows, chans), BF16),
@@ -562,29 +541,23 @@
         flops=2 * shards * tok_rows * chans * (2 * slots + 2 * nstate + 2 * tok_rows + 768),
         exps=shards * tok_rows * tok_rows * heads,
     )
-    near_out, far_out, out_weight = made[:experts], made[experts], made[experts + 1]
-    gate_near, gate_far = made[experts + 2 : experts + 4], made[experts + 4 :]
     far_ret = exchange(far_out)
+    near_ret = exchange(near_out)
     def output(scanned, gate, at, after=()):
         return call(
             functools.partial(output_kernel, at, experts, cap, 512),
             info,
-            [kept_in_vmem(part) for part in scanned] + [kept_in_vmem(gate), kept_in_vmem(out_weight)],
+            [kept_in_vmem(array) for array in (scanned, gate, w_out[0])],
             [(shape(experts, cap, width), None)],
             after_vmem=after,
             flops=2 * slots * width * chans,
         )[0]
 
-    others = [permute(output([far_ret], gate_far[2 * k - 1], 2 * k - 1), swap) for k in range(1, chips)]
-    pairs = []
+    others = [permute(output(far_ret, gate_far[2 * k - 1], 2 * k - 1), swap) for k in range(1, chips)]
+    hopped = []
     for k in range(1, chips):
-        pair = output([far_ret], gate_far[2 * k - 2], 2 * k - 2).astype(F32) + others[k - 1].astype(F32)
-        pairs.append(pair.astype(BF16))
-    hopped = [permute(pair, hop(chips - k)) for k, pair in enumerate(pairs, 1)]
-    near_out = tie(near_out, after_vmem=[far_ret])
-    cut = experts // 2
-    near_out = tie(near_out[:cut], after_vmem=pairs) + near_out[cut:]
-    near_ret = exchange_peers(near_out)
+        pair = output(far_ret, gate_far[2 * k - 2], 2 * k - 2).astype(F32) + others[k - 1].astype(F32)
+        hopped.append(permute(pair.astype(BF16), hop(chips - k)))
     part_swap = permute(output(near_ret, gate_near[1], 1), swap)
     part_own = output(near_ret, gate_near[0], 0, hopped)
     summed = part_own.astype(F32) + part_swap.astype(F32)

time: 231 us -> 220 us (0.952)
  waiting for transfers between devices: 75.2 us -> 64.6 us
  starting transfers between devices: 28.9 us -> 23.4 us
  local copies, waits for them, and re-layouts: 12.1 us -> 16.4 us
    all_to_all x3 -> x4, waiting for transfers between devices: 19.3 us -> 36.1 us  [exchange(): lax.all_to_all(value, 'expert', split_axis=0, concat_axis=0, tiled=True)]
    ppermute x7 -> x0, waiting for transfers between devices: 15.3 us -> none  [exchange_peers(): lax.ppermute(pieces[r], 'expert', [(e, e ^ r) for e in range(experts)])]
    ppermute x12, waiting for transfers between devices: 40.6 us -> 28.5 us  [permute(): return lax.ppermute(value, 'context', pairs)]
    ppermute x7 -> x0, starting transfers between devices: 9.24 us -> none  [exchange_peers(): lax.ppermute(pieces[r], 'expert', [(e, e ^ r) for e in range(experts)])]
    unnamed x20 -> x32, local copies, waits for them, and re-layouts: 11.5 us -> 15.9 us
    all_to_all x3 -> x4, starting transfers between devices: 15.3 us -> 19.1 us  [exchange(): lax.all_to_all(value, 'expert', split_axis=0, concat_axis=0, tiled=True)]
  transfers between devices with their start and end apart: 22 -> 16, of which waited for: 13 -> 11; matrix products, arithmetic and copies ran while one was open for 5% -> 6% of each run, Pallas kernels for 15% -> 17%
where the time goes in v3:
time: 220 us; the launch traced here: 219 us
  waiting for transfers between devices  64.6 us (29%)
  blocking collectives  60.4 us (27%)
  Pallas kernels  50.7 us (23%)
  starting transfers between devices  23.4 us (11%)
  local copies, waits for them, and re-layouts  16.4 us (7%)
  other arithmetic  2.96 us (1%)
    all_to_all x2, blocking collectives, exchange(): lax.all_to_all(value, 'expert', split_axis=0, concat_axis=0, tiled=True)  60.4 us
    pallas_call x12, Pallas kernels, call(): pl.pallas_call(body, out_shape=[(pltpu.HBM if pieces else pltpu.VMEM)(o.s...  48.5 us
    all_to_all x4, waiting for transfers between devices, exchange(): lax.all_to_all(value, 'expert', split_axis=0, concat_axis=0, tiled=True)  36.1 us
    ppermute x12, waiting for transfers between devices, permute(): return lax.ppermute(value, 'context', pairs)  28.5 us
    all_to_all x4, starting transfers between devices, exchange(): lax.all_to_all(value, 'expert', split_axis=0, concat_axis=0, tiled=True)  19.1 us
    unnamed x32, local copies, waits for them, and re-layouts  15.9 us
  transfers between devices with their start and end apart: 16, of which 11 were waited for; matrix products, arithmetic and copies ran while one was open for 6% of the time, Pallas kernels for 17%

profile of v3, /device:TPU:0, one launch (start us, length us, event | category | flops | bytes accessed | tf_op | source)
XLA Modules:
  0.0 219.0 jit_solution(15385268011597651447)
XLA Ops:
  0.1 3.1 %shard_map.109.refs_1_ = bf16[256,2048]{1,0:T(8,128)(2,1)} custom-call(s32[13]{0:T(128)S(1)} %pad_add_fusion.refs_0_, s32[4,1,128]{2,1,0:T(1,128)} %bitcast.32, bf16[128,2048]{1,0:T(8,128)(2,1)} %bitcast.44), custom_call_target="tpu_custom_call" | custom-call | flops 134217728 | bytes 1573888 | tf_op jit(solution)/shard_map/pallas_call | solution.py:181
  3.2 7.3 %all-to-all-start = ((bf16[8,32,2048]{2,1,0:T(8,128)(2,1)}), bf16[8,32,2048]{2,1,0:T(8,128)(2,1)S(1)}, u32[]{:S(2)}, u32[]{:S(2)}) async-start(bf16[8,32,2048]{2,1,0:T(8,128)(2,1)} %bitcast.42), calls=%async_computation | async-start | bytes 2097152 | tf_op jit(solution)/shard_map/all_to_all | solution.py:454
  12.5 2.8 %collective-permute-done.1.refs_4_.refs_7_ = bf16[16,2048]{1,0:T(8,128)(2,1)S(1)} collective-permute-done((bf16[16,2048]{1,0:T(8,128)(2,1)S(1)}, bf16[16,2048]{1,0:T(8,128)(2,1)S(1)}, u32[]{:S(2)}, u32[]{:S(2)}) %collective-permute-start.1) | collective-permute-done | bytes 65568 | tf_op jit(solution)/shard_map/ppermute | solution.py:444
  15.3 10.2 %copy.17 = bf16[256,8,2,1024]{3,1,2,0:T(8,128)(2,1)} copy(bf16[256,8,2,1024]{3,2,1,0:T(2,128)(2,1)} %bitcast.43) | data formatting | bytes 16777216
  25.5 10.8 %all-to-all-done.refs_0_ = bf16[8,32,2048]{2,1,0:T(8,128)(2,1)S(1)} async-done(((bf16[8,32,2048]{2,1,0:T(8,128)(2,1)}), bf16[8,32,2048]{2,1,0:T(8,128)(2,1)S(1)}, u32[]{:S(2)}, u32[]{:S(2)}) %all-to-all-start) | async-done | bytes 1048608 | tf_op jit(solution)/shard_map/all_to_all | solution.py:454
  37.7 2.2 %shard_map.112.refs_3_ = bf16[2048,1024]{1,0:T(8,128)(2,1)S(1)} custom-call(bf16[2048,2048]{1,0:T(8,128)(2,1)} %bitcast.38, bf16[8,32,2048]{2,1,0:T(8,128)(2,1)S(1)} %shard_map.111._.refs_1_), custom_call_target="tpu_custom_call" | custom-call | bytes 8388608 | tf_op jit(solution)/shard_map/pallas_call | solution.py:225
  39.9 4.5 %shard_map.113.refs_1_.refs_4_ = bf16[8,2,32,1152]{3,2,1,0:T(8,128)(2,1)} custom-call(s32[13]{0:T(128)S(1)} %pad_add_fusion.refs_0_, bf16[8,32,2048]{2,1,0:T(8,128)(2,1)S(1)} %shard_map.111._.refs_1_, bf16[8,32,2048]{2,1,0:T(8,128)(2,1)S(1)} %collective-permute-done.3.refs_2_, bf16[2048,1024]{1,0:T(8,128)(2,1)S(1)} %shard_map.112.refs_3_, ...), custom_call_target="tpu_custom_call" | custom-call | flops 2415919104 | bytes 8257536 | tf_op jit(solution)/shard_map/pallas_call | solution.py:181
  44.4 4.3 %all-to-all-start.1 = ((bf16[8,2,32,1152]{3,2,1,0:T(8,128)(2,1)}), bf16[8,2,32,1152]{3,2,1,0:T(8,128)(2,1)}, u32[]{:S(2)}, u32[]{:S(2)}) async-start(bf16[8,2,32,1152]{3,2,1,0:T(8,128)(2,1)} %shard_map.113.refs_1_.refs_4_), calls=%async_computation.1 | async-start | bytes 2359296 | tf_op jit(solution)/shard_map/all_to_all | solution.py:454
  48.7 13.2 %collective-permute-done.4.refs_0_ = bf16[8,32,2048]{2,1,0:T(8,128)(2,1)} collective-permute-done((bf16[8,32,2048]{2,1,0:T(8,128)(2,1)S(1)}, bf16[8,32,2048]{2,1,0:T(8,128)(2,1)}, u32[]{:S(2)}, u32[]{:S(2)}) %collective-permute-start.4) | collective-permute-done | bytes 1048608 | tf_op jit(solution)/shard_map/ppermute | solution.py:444
  61.9 2.9 %collective-permute-done.5.refs_2_ = bf16[8,32,2048]{2,1,0:T(8,128)(2,1)S(1)} collective-permute-done((bf16[8,32,2048]{2,1,0:T(8,128)(2,1)}, bf16[8,32,2048]{2,1,0:T(8,128)(2,1)S(1)}, u32[]{:S(2)}, u32[]{:S(2)}) %collective-permute-start.5) | collective-permute-done | bytes 1048608 | tf_op jit(solution)/shard_map/ppermute | solution.py:444
  65.8 7.4 %shard_map.115.refs_3_ = bf16[8,2,32,1024]{3,2,1,0:T(8,128)(2,1)} custom-call(s32[13]{0:T(128)S(1)} %pad_add_fusion.refs_0_, bf16[8,32,2048]{2,1,0:T(8,128)(2,1)} %shard_map.114.refs_1_, bf16[8,32,2048]{2,1,0:T(8,128)(2,1)} %copy-done.8, bf16[2048,2048]{1,0:T(8,128)(2,1)} %bitcast.39), custom_call_target="tpu_custom_call" | custom-call | flops 2147483648 | bytes 11534336 | tf_op jit(solution)/shard_map/pallas_call | solution.py:181
  73.3 4.7 %all-to-all-done.1.refs_2_.refs_4_ = bf16[8,2,32,1152]{3,2,1,0:T(8,128)(2,1)} async-done(((bf16[8,2,32,1152]{3,2,1,0:T(8,128)(2,1)}), bf16[8,2,32,1152]{3,2,1,0:T(8,128)(2,1)}, u32[]{:S(2)}, u32[]{:S(2)}) %all-to-all-start.1) | async-done | bytes 1179680 | tf_op jit(solution)/shard_map/all_to_all | solution.py:454
  77.9 3.7 %all-to-all-start.2 = ((bf16[8,2,32,1024]{3,2,1,0:T(8,128)(2,1)}), bf16[8,2,32,1024]{3,2,1,0:T(8,128)(2,1)S(1)}, u32[]{:S(2)}, u32[]{:S(2)}) async-start(bf16[8,2,32,1024]{3,2,1,0:T(8,128)(2,1)} %shard_map.115.refs_3_), calls=%async_computation.2 | async-start | bytes 2097152 | tf_op jit(solution)/shard_map/all_to_all | solution.py:454
  81.8 6.1 %shard_map.116 = (bf16[256,1024]{1,0:T(8,128)(2,1)}, bf16[256,1024]{1,0:T(8,128)(2,1)}) custom-call(s32[13]{0:T(128)S(1)} %pad_add_fusion.refs_0_, bf16[8,32,2048]{2,1,0:T(8,128)(2,1)S(1)} %shard_map.111._.refs_1_, bf16[8,32,2048]{2,1,0:T(8,128)(2,1)S(1)} %collective-permute-done.3.refs_2_, bf16[2048,2048]{1,0:T(8,128)(2,1)} %bitcast.40, ...), custom_call_target="tpu_custom_call" | custom-call | flops 2147483648 | bytes 11534336 | tf_op jit(solution)/shard_map/pallas_call | solution.py:181
  87.9 6.8 %shard_map.117 = (bf16[256,1024]{1,0:T(8,128)(2,1)}, bf16[256,1024]{1,0:T(8,128)(2,1)}) custom-call(s32[13]{0:T(128)S(1)} %pad_add_fusion.refs_0_, bf16[8,32,2048]{2,1,0:T(8,128)(2,1)} %shard_map.114.refs_1_, bf16[8,32,2048]{2,1,0:T(8,128)(2,1)} %copy-done.8, bf16[2048,2048]{1,0:T(8,128)(2,1)} %bitcast.41, bf16[8,2,32,1152]{3,2,1,0:T(8,128)(2,1)} %shard_map.113.refs_1_.refs_4_), custom_call_target="tpu_custom_call" | custom-call | flops 2147483648 | bytes 11534336 | tf_op jit(solution)/shard_map/pallas_call | solution.py:181
  94.7 2.3 %shard_map.118 = bf16[128,256]{1,0:T(8,128)(2,1)} custom-call(s32[13]{0:T(128)S(1)} %pad_add_fusion.refs_0_, s32[4,1,128]{2,1,0:T(1,128)S(1)} %bitcast.33, bf16[8,2,32,1152]{3,2,1,0:T(8,128)(2,1)} %all-to-all-done.1.refs_2_.refs_4_, bf16[8,2,32,1024]{3,2,1,0:T(8,128)(2,1)} %shard_map.115.refs_3_, bf16[256,1024]{1,0:T(8,128)(2,1)} %get-tuple-element.11.refs_4_.refs_2_, ...), custom_call_target="tpu_custom_call" | custom-call | flops 16777216 | bytes 1245184 | tf_op jit(solution)/shard_map/pallas_call | solution.py:181
  97.8 3.7 %collective-permute-done.7 = bf16[128,256]{1,0:T(8,128)(2,1)S(1)} collective-permute-done((bf16[128,256]{1,0:T(8,128)(2,1)}, bf16[128,256]{1,0:T(8,128)(2,1)S(1)}, u32[]{:S(2)}, u32[]{:S(2)}) %collective-permute-start.7) | collective-permute-done | bytes 65568 | tf_op jit(solution)/shard_map/ppermute | solution.py:444
  103.7 3.9 %all-to-all-done.2.refs_6_ = bf16[8,2,32,1024]{3,2,1,0:T(8,128)(2,1)S(1)} async-done(((bf16[8,2,32,1024]{3,2,1,0:T(8,128)(2,1)}), bf16[8,2,32,1024]{3,2,1,0:T(8,128)(2,1)S(1)}, u32[]{:S(2)}, u32[]{:S(2)}) %all-to-all-start.2) | async-done | bytes 1048608 | tf_op jit(solution)/shard_map/all_to_all | solution.py:454
  107.6 9.2 %shard_map.119 = (bf16[8,2,32,1024]{3,2,1,0:T(8,128)(2,1)}, bf16[8,2,32,1024]{3,2,1,0:T(8,128)(2,1)S(1)}) custom-call(s32[13]{0:T(128)S(1)} %pad_add_fusion.refs_0_, s32[4,1,128]{2,1,0:T(1,128)S(1)} %bitcast.34, f32[8,128]{1,0:T(8,128)S(1)} %maximum_maximum_fusion.refs_2_, f32[8,1024]{1,0:T(8,128)S(1)} %select_maximum_fusion.refs_3_, ...), custom_call_target="tpu_custom_call" | custom-call | flops 1744830464 | bytes 4587520 | tf_op jit(solution)/shard_map/pallas_call | solution.py:181
  116.7 29.4 %all_to_all.30.refs_1_ = bf16[8,2,32,1024]{3,2,1,0:T(8,128)(2,1)S(1)} all-to-all(bf16[8,2,32,1024]{3,2,1,0:T(8,128)(2,1)S(1)} %get-tuple-element.14), channel_id=1, replica_groups=mesh['expert'=8,'context'=4] {'expert'}, dimensions={0} | all-to-all | bytes 2097152 | tf_op jit(solution)/shard_map/all_to_all | solution.py:454
  146.2 3.8 %all-to-all-start.3 = ((bf16[8,2,32,1024]{3,2,1,0:T(8,128)(2,1)}), bf16[8,2,32,1024]{3,2,1,0:T(8,128)(2,1)S(1)}, u32[]{:S(2)}, u32[]{:S(2)}) async-start(bf16[8,2,32,1024]{3,2,1,0:T(8,128)(2,1)} %get-tuple-element.13), calls=%async_computation.3 | async-start | bytes 2097152 | tf_op jit(solution)/shard_map/all_to_all | solution.py:454
  158.7 16.8 %all-to-all-done.3.refs_1_ = bf16[8,2,32,1024]{3,2,1,0:T(8,128)(2,1)S(1)} async-done(((bf16[8,2,32,1024]{3,2,1,0:T(8,128)(2,1)}), bf16[8,2,32,1024]{3,2,1,0:T(8,128)(2,1)S(1)}, u32[]{:S(2)}, u32[]{:S(2)}) %all-to-all-start.3) | async-done | bytes 1048608 | tf_op jit(solution)/shard_map/all_to_all | solution.py:454
  179.6 3.9 %collective-permute-done.10.refs_4_ = bf16[8,32,2048]{2,1,0:T(8,128)(2,1)S(1)} collective-permute-done((bf16[8,32,2048]{2,1,0:T(8,128)(2,1)}, bf16[8,32,2048]{2,1,0:T(8,128)(2,1)S(1)}, u32[]{:S(2)}, u32[]{:S(2)}) %collective-permute-start.10) | collective-permute-done | bytes 1048608 | tf_op jit(solution)/shard_map/ppermute | solution.py:444
  186.0 30.9 %all_to_all.31 = bf16[8,32,2048]{2,1,0:T(8,128)(2,1)S(1)} all-to-all(bf16[8,32,2048]{2,1,0:T(8,128)(2,1)S(1)} %add_convert_fusion), channel_id=1, replica_groups=mesh['expert'=8,'context'=4] {'expert'}, dimensions={0} | all-to-all | bytes 2097152 | tf_op jit(solution)/shard_map/all_to_all | solution.py:454
  (72 shorter events, 24.8 us)
Async XLA Ops:
  0.0 10.5 %copy-start.9 = (bf16[1,2048,16]{1,2,0:T(8,128)(2,1)S(1)}, bf16[1,2048,16]{1,2,0:T(8,128)(2,1)}, u32[]{:S(2)}) copy-start(bf16[1,2048,16]{1,2,0:T(8,128)(2,1)} %param.15) | copy-start | bytes 196612
  3.2 33.1 %all-to-all-start = ((bf16[8,32,2048]{2,1,0:T(8,128)(2,1)}), bf16[8,32,2048]{2,1,0:T(8,128)(2,1)S(1)}, u32[]{:S(2)}, u32[]{:S(2)}) async-start(bf16[8,32,2048]{2,1,0:T(8,128)(2,1)} %bitcast.42), calls=%async_computation | async-start | bytes 2097152 | tf_op jit(solution)/shard_map/all_to_all | solution.py:454
  10.9 4.3 %collective-permute-start.1 = (bf16[16,2048]{1,0:T(8,128)(2,1)S(1)}, bf16[16,2048]{1,0:T(8,128)(2,1)S(1)}, u32[]{:S(2)}, u32[]{:S(2)}) collective-permute-start(bf16[16,2048]{1,0:T(8,128)(2,1)S(1)} %bitcast.28), channel_id=1, source_target_pairs={{0,2},{1,3},{2,0},{3,1},{4,6},{5,7},{6,4},{7,5},{8,10},{9,11},{10,... | collective-permute-start | bytes 196616 | tf_op jit(solution)/shard_map/ppermute | solution.py:444
  12.5 13.0 %collective-permute-start = (bf16[16,2048]{1,0:T(8,128)(2,1)S(1)}, bf16[16,2048]{1,0:T(8,128)(2,1)S(1)}, u32[]{:S(2)}, u32[]{:S(2)}) collective-permute-start(bf16[16,2048]{1,0:T(8,128)(2,1)S(1)} %bitcast.29), channel_id=1, source_target_pairs={{0,1},{1,0},{2,3},{3,2},{4,5},{5,4},{6,7},{7,6},{8,9},{9,8},{10,11... | collective-permute-start | bytes 196616 | tf_op jit(solution)/shard_map/ppermute | solution.py:444
  15.3 10.2 %collective-permute-start.2 = (bf16[16,2048]{1,0:T(8,128)(2,1)S(1)}, bf16[16,2048]{1,0:T(8,128)(2,1)S(1)}, u32[]{:S(2)}, u32[]{:S(2)}) collective-permute-start(bf16[16,2048]{1,0:T(8,128)(2,1)S(1)} %collective-permute-done.1.refs_4_.refs_7_), channel_id=1, source_target_pairs={{0,1},{1,0},{2,3},{3,2},{4,5},{5,4},{6,7},{7,6},{8,9},{9,8},{10,11... | collective-permute-start | bytes 196616 | tf_op jit(solution)/shard_map/ppermute | solution.py:444
  36.2 3.7 %collective-permute-start.3 = (bf16[8,32,2048]{2,1,0:T(8,128)(2,1)S(1)}, bf16[8,32,2048]{2,1,0:T(8,128)(2,1)S(1)}, u32[]{:S(2)}, u32[]{:S(2)}) collective-permute-start(bf16[8,32,2048]{2,1,0:T(8,128)(2,1)S(1)} %shard_map.111._.refs_1_), channel_id=1, source_target_pairs={{0,1},{1,0},{2,3},{3,2},{4,5},{5,4},{6,7},{7,6},{8,9},{9,8},{10,11... | collective-permute-start | bytes 3145736 | tf_op jit(solution)/shard_map/ppermute | solution.py:444
  36.2 25.7 %collective-permute-start.4 = (bf16[8,32,2048]{2,1,0:T(8,128)(2,1)S(1)}, bf16[8,32,2048]{2,1,0:T(8,128)(2,1)}, u32[]{:S(2)}, u32[]{:S(2)}) collective-permute-start(bf16[8,32,2048]{2,1,0:T(8,128)(2,1)S(1)} %shard_map.111._.refs_1_), channel_id=1, source_target_pairs={{0,2},{1,3},{2,0},{3,1},{4,6},{5,7},{6,4},{7,5},{8,10},{9,11},{10,... | collective-permute-start | bytes 3145736 | tf_op jit(solution)/shard_map/ppermute | solution.py:444
  44.4 33.5 %all-to-all-start.1 = ((bf16[8,2,32,1152]{3,2,1,0:T(8,128)(2,1)}), bf16[8,2,32,1152]{3,2,1,0:T(8,128)(2,1)}, u32[]{:S(2)}, u32[]{:S(2)}) async-start(bf16[8,2,32,1152]{3,2,1,0:T(8,128)(2,1)} %shard_map.113.refs_1_.refs_4_), calls=%async_computation.1 | async-start | bytes 2359296 | tf_op jit(solution)/shard_map/all_to_all | solution.py:454
  61.9 2.9 %collective-permute-start.5 = (bf16[8,32,2048]{2,1,0:T(8,128)(2,1)}, bf16[8,32,2048]{2,1,0:T(8,128)(2,1)S(1)}, u32[]{:S(2)}, u32[]{:S(2)}) collective-permute-start(bf16[8,32,2048]{2,1,0:T(8,128)(2,1)} %shard_map.114.refs_1_), channel_id=1, source_target_pairs={{0,1},{1,0},{2,3},{3,2},{4,5},{5,4},{6,7},{7,6},{8,9},{9,8},{10,11... | collective-permute-start | bytes 3145736 | tf_op jit(solution)/shard_map/ppermute | solution.py:444
  73.2 8.5 %copy-start.14 = (f32[16]{0:T(128)S(1)}, f32[16]{0:T(128)}, u32[]{:S(2)}) copy-start(f32[16]{0:T(128)} %param.17) | copy-start | bytes 196
  73.2 8.5 %copy-start.13 = (f32[16]{0:T(128)S(1)}, f32[16]{0:T(128)}, u32[]{:S(2)}) copy-start(f32[16]{0:T(128)} %param.16) | copy-start | bytes 196
  77.9 29.6 %all-to-all-start.2 = ((bf16[8,2,32,1024]{3,2,1,0:T(8,128)(2,1)}), bf16[8,2,32,1024]{3,2,1,0:T(8,128)(2,1)S(1)}, u32[]{:S(2)}, u32[]{:S(2)}) async-start(bf16[8,2,32,1024]{3,2,1,0:T(8,128)(2,1)} %shard_map.115.refs_3_), calls=%async_computation.2 | async-start | bytes 2097152 | tf_op jit(solution)/shard_map/all_to_all | solution.py:454
  87.9 6.8 %copy-start.6 = (s32[1,512,1]{1,2,0:T(1,128)S(1)}, s32[1,512,1]{1,2,0:T(1,128)}, u32[]{:S(2)}) copy-start(s32[1,512,1]{1,2,0:T(1,128)} %param.12) | copy-start | bytes 6148
  94.7 6.9 %copy-start.10 = (f32[4,1024]{1,0:T(4,128)S(1)}, f32[4,1024]{1,0:T(4,128)}, u32[]{:S(2)}) copy-start(f32[4,1024]{1,0:T(4,128)} %param.19) | copy-start | bytes 49156
  94.7 6.9 %copy-start.11 = (f32[1024]{0:T(1024)S(1)}, f32[1024]{0:T(1024)}, u32[]{:S(2)}) copy-start(f32[1024]{0:T(1024)} %param.20) | copy-start | bytes 12292
  97.0 4.5 %collective-permute-start.7 = (bf16[128,256]{1,0:T(8,128)(2,1)}, bf16[128,256]{1,0:T(8,128)(2,1)S(1)}, u32[]{:S(2)}, u32[]{:S(2)}) collective-permute-start(bf16[128,256]{1,0:T(8,128)(2,1)} %shard_map.118), channel_id=1, source_target_pairs={{0,2},{1,3},{2,0},{3,1},{4,6},{5,7},{6,4},{7,5},{8,10},{9,11},{10,... | collective-permute-start | bytes 196616 | tf_op jit(solution)/shard_map/ppermute | solution.py:444
  97.8 3.7 %collective-permute-start.6 = (bf16[128,256]{1,0:T(8,128)(2,1)}, bf16[128,256]{1,0:T(8,128)(2,1)S(1)}, u32[]{:S(2)}, u32[]{:S(2)}) collective-permute-start(bf16[128,256]{1,0:T(8,128)(2,1)} %shard_map.118), channel_id=1, source_target_pairs={{0,1},{1,0},{2,3},{3,2},{4,5},{5,4},{6,7},{7,6},{8,9},{9,8},{10,11... | collective-permute-start | bytes 196616 | tf_op jit(solution)/shard_map/ppermute | solution.py:444
  101.6 1.3 collective-permute-start.8
  116.7 33.2 %copy-start.5 = (bf16[256,1024]{1,0:T(8,128)(2,1)S(1)}, bf16[256,1024]{1,0:T(8,128)(2,1)}, u32[]{:S(2)}) copy-start(bf16[256,1024]{1,0:T(8,128)(2,1)} %get-tuple-element.15.refs_2_) | copy-start | bytes 1572868
  146.2 29.3 %all-to-all-start.3 = ((bf16[8,2,32,1024]{3,2,1,0:T(8,128)(2,1)}), bf16[8,2,32,1024]{3,2,1,0:T(8,128)(2,1)S(1)}, u32[]{:S(2)}, u32[]{:S(2)}) async-start(bf16[8,2,32,1024]{3,2,1,0:T(8,128)(2,1)} %get-tuple-element.13), calls=%async_computation.3 | async-start | bytes 2097152 | tf_op jit(solution)/shard_map/all_to_all | solution.py:454
  154.1 2.7 %collective-permute-start.9 = (bf16[8,32,2048]{2,1,0:T(8,128)(2,1)S(1)}, bf16[8,32,2048]{2,1,0:T(8,128)(2,1)S(1)}, u32[]{:S(2)}, u32[]{:S(2)}) collective-permute-start(bf16[8,32,2048]{2,1,0:T(8,128)(2,1)S(1)} %shard_map.121), channel_id=1, source_target_pairs={{0,1},{1,0},{2,3},{3,2},{4,5},{5,4},{6,7},{7,6},{8,9},{9,8},{10,11... | collective-permute-start | bytes 3145736 | tf_op jit(solution)/shard_map/ppermute | solution.py:444
  156.0 19.5 %copy-start.4 = (bf16[256,1024]{1,0:T(8,128)(2,1)S(1)}, bf16[256,1024]{1,0:T(8,128)(2,1)}, u32[]{:S(2)}) copy-start(bf16[256,1024]{1,0:T(8,128)(2,1)} %get-tuple-element.16.refs_2_) | copy-start | bytes 1572868
  158.2 25.4 %collective-permute-start.10 = (bf16[8,32,2048]{2,1,0:T(8,128)(2,1)}, bf16[8,32,2048]{2,1,0:T(8,128)(2,1)S(1)}, u32[]{:S(2)}, u32[]{:S(2)}) collective-permute-start(bf16[8,32,2048]{2,1,0:T(8,128)(2,1)} %add_convert_fusion.1), channel_id=1, source_target_pairs={{0,2},{1,3},{2,0},{3,1},{4,6},{5,7},{6,4},{7,5},{8,10},{9,11},{10,... | collective-permute-start | bytes 3145736 | tf_op jit(solution)/shard_map/ppermute | solution.py:444
  179.5 5.9 %collective-permute-start.11 = (bf16[8,32,2048]{2,1,0:T(8,128)(2,1)S(1)}, bf16[8,32,2048]{2,1,0:T(8,128)(2,1)S(1)}, u32[]{:S(2)}, u32[]{:S(2)}) collective-permute-start(bf16[8,32,2048]{2,1,0:T(8,128)(2,1)S(1)} %shard_map.123), channel_id=1, source_target_pairs={{0,1},{1,0},{2,3},{3,2},{4,5},{5,4},{6,7},{7,6},{8,9},{9,8},{10,11... | collective-permute-start | bytes 3145736 | tf_op jit(solution)/shard_map/ppermute | solution.py:444
  (7 other events, 20.0 us)

commit v4 on v3

--- a/solution.py
+++ b/solution.py
@@ -28,13 +28,13 @@
     return pieces.reshape(count * rows, lanes)
 
 
-def slot_rows(ids, experts, cap):
+def slot_rows(ids, experts, cap, me=0):
     tok_rows = ids.shape[1]
     onehot = jnp.where(iota((experts, tok_rows), 0) == ids, 1.0, 0.0)
     upto = jnp.where(iota((tok_rows, tok_rows), 0) <= iota((tok_rows, tok_rows), 1), 1.0, 0.0)
     before = dot(onehot.astype(BF16), upto.astype(BF16))
     rank = jnp.sum(onehot * before, axis=0, keepdims=True) - 1.0
-    slot = ids * cap + rank.astype(jnp.int32)
+    slot = (ids ^ me) * cap + rank.astype(jnp.int32)
     return jnp.where(iota((experts * cap, tok_rows), 0) == slot, 1.0, 0.0)
 
 
@@ -241,10 +241,21 @@
     out.send(0)
 
 
-def collect_kernel(experts, cap, info_ref, ids_ref, rows, out):
-    place = slot_rows(ids_ref[info_ref[0]], experts, cap).T.astype(BF16)
-    out.held[...] = dot(place, rows.whole()[...]).astype(BF16)
-    out.send(0)
+def sum_kernel(experts, parts, info_ref, *refs):
+    me = info_ref[info_ref.shape[0] - 1]
+    for r in range(experts):
+        total = refs[0].held[r ^ me].astype(F32)
+        for ref in refs[1:parts]:
+            total = total + ref.held[r ^ me].astype(F32)
+        refs[parts + r].held[...] = total.astype(BF16)
+
+
+def collect_kernel(experts, cap, info_ref, ids_ref, *refs):
+    me = info_ref[info_ref.shape[0] - 1]
+    place = slot_rows(ids_ref[info_ref[0]], experts, cap, me).T.astype(BF16)
+    rows = flat_rows(jnp.stack([ref.held[...] for ref in refs[:experts]]))
+    refs[experts].held[...] = dot(place, rows).astype(BF16)
+    refs[experts].send(0)
 
 
 def side_kernel(experts, cap, info_ref, ids_ref, near, out):
@@ -433,7 +444,8 @@
     order = 2 * ((here // 2 - blocks // 2) % chips) + ((here % 2) ^ (blocks % 2))
     groups = 2 * ((blocks // 2 - here // 2) % chips) + ((here % 2) ^ (blocks % 2))
     block_at = 2 * ((here // 2 - blocks // 2) % chips) + ((here % 2) ^ (blocks % 2))
-    info = jnp.concatenate([here[None], block_at, order, groups])
+    me = lax.axis_index("expert").astype(jnp.int32)
+    info = jnp.concatenate([here[None], block_at, order, groups, me[None]])
     ids = route.reshape(shards, 1, tok_rows)
     swap = [(c, c ^ 1) for c in range(shards)]
 
@@ -467,7 +479,7 @@
     w_in = staged(w_flat, chans, chans, own)
     swapped = permute(own, swap)
     near = call(
-        functools.partial(project_kernel, 2, experts, cap, 256),
+        functools.partial(project_kernel, 2, experts, cap, 512),
         info,
         [kept_in_vmem(array) for array in (own, swapped, w_in, w_state[0], *steps)],
         [(shape(experts, 2, cap, chans + LANES), once)],
@@ -560,13 +572,20 @@
         hopped.append(permute(pair.astype(BF16), hop(chips - k)))
     part_swap = permute(output(near_ret, gate_near[1], 1), swap)
     part_own = output(near_ret, gate_near[0], 0, hopped)
-    summed = part_own.astype(F32) + part_swap.astype(F32)
-    for part in hopped:
-        summed = summed + part.astype(F32)
-    returned = exchange(summed.astype(BF16)).reshape(slots, width)
+    summed = call(
+        functools.partial(sum_kernel, experts, 1 + chips),
+        info,
+        [kept_in_vmem(part) for part in (part_own, part_swap, *hopped)],
+        [(shape(cap, width), None)] * experts,
+    )
+    returned = [
+        lax.ppermute(summed[r], "expert", [(e, e ^ r) for e in range(experts)])
+        for r in range(experts - 1, 0, -1)
+    ]
+    returned = [summed[0]] + returned[::-1]
     result = call(
         functools.partial(collect_kernel, experts, cap),
-        info, [kept_in_vmem(returned)], [(shape(tok_rows, width), once)],
+        info, [kept_in_vmem(part) for part in returned], [(shape(tok_rows, width), once)],
         small=[ids],
         flops=2 * slots * tok_rows * width,
     )[0]

time: 220 us -> 217 us (0.986)
  blocking collectives: 60.4 us -> 29.4 us
  waiting for transfers between devices: 64.6 us -> 78.6 us
  starting transfers between devices: 23.4 us -> 35.5 us
    all_to_all x2 -> x1, blocking collectives: 60.4 us -> 29.4 us  [exchange(): lax.all_to_all(value, 'expert', split_axis=0, concat_axis=0, tiled=True)]
    ppermute x0 -> x7, waiting for transfers between devices: none -> 14 us  [per_device(): lax.ppermute(summed[r], 'expert', [(e, e ^ r) for e in range(experts)])]
    ppermute x0 -> x7, starting transfers between devices: none -> 12.1 us  [per_device(): lax.ppermute(summed[r], 'expert', [(e, e ^ r) for e in range(experts)])]
    pallas_call x12 -> x13, Pallas kernels: 48.5 us -> 49.6 us  [call(): pl.pallas_call(body, out_shape=[(pltpu.HBM if pieces else pltpu.VMEM)(o.s...]
  transfers between devices with their start and end apart: 16 -> 23, of which waited for: 11 -> 14; matrix products, arithmetic and copies ran while one was open for 6% -> 6% of each run, Pallas kernels for 17% -> 17%
where the time goes in v4:
time: 217 us; the launch traced here: 215 us
  waiting for transfers between devices  78.6 us (36%)
  Pallas kernels  51.8 us (24%)
  starting transfers between devices  35.5 us (16%)
  blocking collectives  29.4 us (14%)
  local copies, waits for them, and re-layouts  16.5 us (8%)
  other arithmetic  2.37 us (1%)
    pallas_call x13, Pallas kernels, call(): pl.pallas_call(body, out_shape=[(pltpu.HBM if pieces else pltpu.VMEM)(o.s...  49.6 us
    all_to_all x4, waiting for transfers between devices, exchange(): lax.all_to_all(value, 'expert', split_axis=0, concat_axis=0, tiled=True)  36.2 us
    all_to_all x1, blocking collectives, exchange(): lax.all_to_all(value, 'expert', split_axis=0, concat_axis=0, tiled=True)  29.4 us
    ppermute x12, waiting for transfers between devices, permute(): return lax.ppermute(value, 'context', pairs)  28.4 us
    all_to_all x4, starting transfers between devices, exchange(): lax.all_to_all(value, 'expert', split_axis=0, concat_axis=0, tiled=True)  19.1 us
    unnamed x32, local copies, waits for them, and re-layouts  16 us
    ppermute x7, waiting for transfers between devices, per_device(): lax.ppermute(summed[r], 'expert', [(e, e ^ r) for e in range(experts)])  14 us
    ppermute x7, starting transfers between devices, per_device(): lax.ppermute(summed[r], 'expert', [(e, e ^ r) for e in range(experts)])  12.1 us
  transfers between devices with their start and end apart: 23, of which 14 were waited for; matrix products, arithmetic and copies ran while one was open for 6% of the time, Pallas kernels for 17%

profile of v4, /device:TPU:0, one launch (start us, length us, event | category | flops | bytes accessed | tf_op | source)
XLA Modules:
  0.0 214.8 jit_solution(8178050238646373441)
XLA Ops:
  0.1 3.0 %shard_map.109.refs_1_ = bf16[256,2048]{1,0:T(8,128)(2,1)} custom-call(s32[14]{0:T(128)S(1)} %concatenate.9.refs_0_, s32[4,1,128]{2,1,0:T(1,128)} %bitcast.31, bf16[128,2048]{1,0:T(8,128)(2,1)} %bitcast.43), custom_call_target="tpu_custom_call" | custom-call | flops 134217728 | bytes 1573888 | tf_op jit(solution)/shard_map/pallas_call | solution.py:181
  3.1 7.3 %all-to-all-start = ((bf16[8,32,2048]{2,1,0:T(8,128)(2,1)}), bf16[8,32,2048]{2,1,0:T(8,128)(2,1)S(1)}, u32[]{:S(2)}, u32[]{:S(2)}) async-start(bf16[8,32,2048]{2,1,0:T(8,128)(2,1)} %bitcast.41), calls=%async_computation | async-start | bytes 2097152 | tf_op jit(solution)/shard_map/all_to_all | solution.py:466
  12.5 2.8 %collective-permute-done.1.refs_4_.refs_7_ = bf16[16,2048]{1,0:T(8,128)(2,1)S(1)} collective-permute-done((bf16[16,2048]{1,0:T(8,128)(2,1)S(1)}, bf16[16,2048]{1,0:T(8,128)(2,1)S(1)}, u32[]{:S(2)}, u32[]{:S(2)}) %collective-permute-start.1) | collective-permute-done | bytes 65568 | tf_op jit(solution)/shard_map/ppermute | solution.py:456
  15.2 10.2 %copy.17 = bf16[256,8,2,1024]{3,1,2,0:T(8,128)(2,1)} copy(bf16[256,8,2,1024]{3,2,1,0:T(2,128)(2,1)} %bitcast.42) | data formatting | bytes 16777216
  25.4 10.8 %all-to-all-done.refs_0_ = bf16[8,32,2048]{2,1,0:T(8,128)(2,1)S(1)} async-done(((bf16[8,32,2048]{2,1,0:T(8,128)(2,1)}), bf16[8,32,2048]{2,1,0:T(8,128)(2,1)S(1)}, u32[]{:S(2)}, u32[]{:S(2)}) %all-to-all-start) | async-done | bytes 1048608 | tf_op jit(solution)/shard_map/all_to_all | solution.py:466
  39.9 4.6 %shard_map.113.refs_1_.refs_4_ = bf16[8,2,32,1152]{3,2,1,0:T(8,128)(2,1)} custom-call(s32[14]{0:T(128)S(1)} %concatenate.9.refs_0_, bf16[8,32,2048]{2,1,0:T(8,128)(2,1)S(1)} %shard_map.111._.refs_1_, bf16[8,32,2048]{2,1,0:T(8,128)(2,1)S(1)} %collective-permute-done.3.refs_2_, bf16[2048,1024]{1,0:T(8,128)(2,1)S(1)} %shard_map.112.refs_3_, ...), custom_call_target="tpu_custom_call" | custom-call | flops 2415919104 | bytes 8257536 | tf_op jit(solution)/shard_map/pallas_call | solution.py:181
  44.5 4.3 %all-to-all-start.1 = ((bf16[8,2,32,1152]{3,2,1,0:T(8,128)(2,1)}), bf16[8,2,32,1152]{3,2,1,0:T(8,128)(2,1)}, u32[]{:S(2)}, u32[]{:S(2)}) async-start(bf16[8,2,32,1152]{3,2,1,0:T(8,128)(2,1)} %shard_map.113.refs_1_.refs_4_), calls=%async_computation.1 | async-start | bytes 2359296 | tf_op jit(solution)/shard_map/all_to_all | solution.py:466
  48.8 13.1 %collective-permute-done.4.refs_0_ = bf16[8,32,2048]{2,1,0:T(8,128)(2,1)} collective-permute-done((bf16[8,32,2048]{2,1,0:T(8,128)(2,1)S(1)}, bf16[8,32,2048]{2,1,0:T(8,128)(2,1)}, u32[]{:S(2)}, u32[]{:S(2)}) %collective-permute-start.4) | collective-permute-done | bytes 1048608 | tf_op jit(solution)/shard_map/ppermute | solution.py:456
  61.9 2.9 %collective-permute-done.5.refs_2_ = bf16[8,32,2048]{2,1,0:T(8,128)(2,1)S(1)} collective-permute-done((bf16[8,32,2048]{2,1,0:T(8,128)(2,1)}, bf16[8,32,2048]{2,1,0:T(8,128)(2,1)S(1)}, u32[]{:S(2)}, u32[]{:S(2)}) %collective-permute-start.5) | collective-permute-done | bytes 1048608 | tf_op jit(solution)/shard_map/ppermute | solution.py:456
  65.8 7.4 %shard_map.115.refs_3_ = bf16[8,2,32,1024]{3,2,1,0:T(8,128)(2,1)} custom-call(s32[14]{0:T(128)S(1)} %concatenate.9.refs_0_, bf16[8,32,2048]{2,1,0:T(8,128)(2,1)} %shard_map.114.refs_1_, bf16[8,32,2048]{2,1,0:T(8,128)(2,1)} %copy-done.8, bf16[2048,2048]{1,0:T(8,128)(2,1)} %bitcast.38), custom_call_target="tpu_custom_call" | custom-call | flops 2147483648 | bytes 11534336 | tf_op jit(solution)/shard_map/pallas_call | solution.py:181
  73.3 4.8 %all-to-all-done.1.refs_2_.refs_4_ = bf16[8,2,32,1152]{3,2,1,0:T(8,128)(2,1)} async-done(((bf16[8,2,32,1152]{3,2,1,0:T(8,128)(2,1)}), bf16[8,2,32,1152]{3,2,1,0:T(8,128)(2,1)}, u32[]{:S(2)}, u32[]{:S(2)}) %all-to-all-start.1) | async-done | bytes 1179680 | tf_op jit(solution)/shard_map/all_to_all | solution.py:466
  78.0 3.7 %all-to-all-start.2 = ((bf16[8,2,32,1024]{3,2,1,0:T(8,128)(2,1)}), bf16[8,2,32,1024]{3,2,1,0:T(8,128)(2,1)S(1)}, u32[]{:S(2)}, u32[]{:S(2)}) async-start(bf16[8,2,32,1024]{3,2,1,0:T(8,128)(2,1)} %shard_map.115.refs_3_), calls=%async_computation.2 | async-start | bytes 2097152 | tf_op jit(solution)/shard_map/all_to_all | solution.py:466
  81.9 6.1 %shard_map.116 = (bf16[256,1024]{1,0:T(8,128)(2,1)}, bf16[256,1024]{1,0:T(8,128)(2,1)}) custom-call(s32[14]{0:T(128)S(1)} %concatenate.9.refs_0_, bf16[8,32,2048]{2,1,0:T(8,128)(2,1)S(1)} %shard_map.111._.refs_1_, bf16[8,32,2048]{2,1,0:T(8,128)(2,1)S(1)} %collective-permute-done.3.refs_2_, bf16[2048,2048]{1,0:T(8,128)(2,1)} %bitcast.39, ...), custom_call_target="tpu_custom_call" | custom-call | flops 2147483648 | bytes 11534336 | tf_op jit(solution)/shard_map/pallas_call | solution.py:181
  88.0 6.8 %shard_map.117 = (bf16[256,1024]{1,0:T(8,128)(2,1)}, bf16[256,1024]{1,0:T(8,128)(2,1)}) custom-call(s32[14]{0:T(128)S(1)} %concatenate.9.refs_0_, bf16[8,32,2048]{2,1,0:T(8,128)(2,1)} %shard_map.114.refs_1_, bf16[8,32,2048]{2,1,0:T(8,128)(2,1)} %copy-done.8, bf16[2048,2048]{1,0:T(8,128)(2,1)} %bitcast.40, bf16[8,2,32,1152]{3,2,1,0:T(8,128)(2,1)} %shard_map.113.refs_1_.refs_4_), custom_call_target="tpu_custom_call" | custom-call | flops 2147483648 | bytes 11534336 | tf_op jit(solution)/shard_map/pallas_call | solution.py:181
  97.9 3.7 %collective-permute-done.7 = bf16[128,256]{1,0:T(8,128)(2,1)S(1)} collective-permute-done((bf16[128,256]{1,0:T(8,128)(2,1)}, bf16[128,256]{1,0:T(8,128)(2,1)S(1)}, u32[]{:S(2)}, u32[]{:S(2)}) %collective-permute-start.7) | collective-permute-done | bytes 65568 | tf_op jit(solution)/shard_map/ppermute | solution.py:456
  103.8 3.9 %all-to-all-done.2.refs_6_ = bf16[8,2,32,1024]{3,2,1,0:T(8,128)(2,1)S(1)} async-done(((bf16[8,2,32,1024]{3,2,1,0:T(8,128)(2,1)}), bf16[8,2,32,1024]{3,2,1,0:T(8,128)(2,1)S(1)}, u32[]{:S(2)}, u32[]{:S(2)}) %all-to-all-start.2) | async-done | bytes 1048608 | tf_op jit(solution)/shard_map/all_to_all | solution.py:466
  107.6 9.2 %shard_map.119 = (bf16[8,2,32,1024]{3,2,1,0:T(8,128)(2,1)}, bf16[8,2,32,1024]{3,2,1,0:T(8,128)(2,1)S(1)}) custom-call(s32[14]{0:T(128)S(1)} %concatenate.9.refs_0_, s32[4,1,128]{2,1,0:T(1,128)S(1)} %bitcast.33, f32[8,128]{1,0:T(8,128)S(1)} %maximum_maximum_fusion.refs_2_, f32[8,1024]{1,0:T(8,128)S(1)} %select_maximum_fusion.refs_3_, ...), custom_call_target="tpu_custom_call" | custom-call | flops 1744830464 | bytes 4587520 | tf_op jit(solution)/shard_map/pallas_call | solution.py:181
  116.9 29.4 %all_to_all.25.refs_1_ = bf16[8,2,32,1024]{3,2,1,0:T(8,128)(2,1)S(1)} all-to-all(bf16[8,2,32,1024]{3,2,1,0:T(8,128)(2,1)S(1)} %get-tuple-element.22), channel_id=1, replica_groups=mesh['expert'=8,'context'=4] {'expert'}, dimensions={0} | all-to-all | bytes 2097152 | tf_op jit(solution)/shard_map/all_to_all | solution.py:466
  146.3 3.8 %all-to-all-start.3 = ((bf16[8,2,32,1024]{3,2,1,0:T(8,128)(2,1)}), bf16[8,2,32,1024]{3,2,1,0:T(8,128)(2,1)S(1)}, u32[]{:S(2)}, u32[]{:S(2)}) async-start(bf16[8,2,32,1024]{3,2,1,0:T(8,128)(2,1)} %get-tuple-element.21), calls=%async_computation.3 | async-start | bytes 2097152 | tf_op jit(solution)/shard_map/all_to_all | solution.py:466
  158.8 16.8 %all-to-all-done.3.refs_1_ = bf16[8,2,32,1024]{3,2,1,0:T(8,128)(2,1)S(1)} async-done(((bf16[8,2,32,1024]{3,2,1,0:T(8,128)(2,1)}), bf16[8,2,32,1024]{3,2,1,0:T(8,128)(2,1)S(1)}, u32[]{:S(2)}, u32[]{:S(2)}) %all-to-all-start.3) | async-done | bytes 1048608 | tf_op jit(solution)/shard_map/all_to_all | solution.py:466
  179.7 4.0 %collective-permute-done.10.refs_4_.refs_3_ = bf16[8,32,2048]{2,1,0:T(8,128)(2,1)S(1)} collective-permute-done((bf16[8,32,2048]{2,1,0:T(8,128)(2,1)}, bf16[8,32,2048]{2,1,0:T(8,128)(2,1)S(1)}, u32[]{:S(2)}, u32[]{:S(2)}) %collective-permute-start.10) | collective-permute-done | bytes 1048608 | tf_op jit(solution)/shard_map/ppermute | solution.py:456
  190.1 2.8 %collective-permute-start.15 = (bf16[32,2048]{1,0:T(8,128)(2,1)S(1)}, bf16[32,2048]{1,0:T(8,128)(2,1)S(1)}, u32[]{:S(2)}, u32[]{:S(2)}) collective-permute-start(bf16[32,2048]{1,0:T(8,128)(2,1)S(1)} %get-tuple-element.29), channel_id=1, source_target_pairs={{0,16},{4,20},{8,24},{12,28},{16,0},{20,4},{24,8},{28,12},{1,17},{... | collective-permute-start | bytes 393224 | tf_op jit(solution)/shard_map/ppermute | solution.py:582
  194.3 3.3 %collective-permute-start.17 = (bf16[32,2048]{1,0:T(8,128)(2,1)S(1)}, bf16[32,2048]{1,0:T(8,128)(2,1)S(1)}, u32[]{:S(2)}, u32[]{:S(2)}) collective-permute-start(bf16[32,2048]{1,0:T(8,128)(2,1)S(1)} %get-tuple-element.31), channel_id=1, source_target_pairs={{0,24},{4,28},{8,16},{12,20},{16,8},{20,12},{24,0},{28,4},{1,25},{... | collective-permute-start | bytes 393224 | tf_op jit(solution)/shard_map/ppermute | solution.py:582
  199.8 12.8 %collective-permute-done.16.refs_7_ = bf16[32,2048]{1,0:T(8,128)(2,1)S(1)} collective-permute-done((bf16[32,2048]{1,0:T(8,128)(2,1)S(1)}, bf16[32,2048]{1,0:T(8,128)(2,1)S(1)}, u32[]{:S(2)}, u32[]{:S(2)}) %collective-permute-start.16) | collective-permute-done | bytes 131104 | tf_op jit(solution)/shard_map/ppermute | solution.py:582
  (85 shorter events, 37.0 us)
Async XLA Ops:
  3.1 33.1 %all-to-all-start = ((bf16[8,32,2048]{2,1,0:T(8,128)(2,1)}), bf16[8,32,2048]{2,1,0:T(8,128)(2,1)S(1)}, u32[]{:S(2)}, u32[]{:S(2)}) async-start(bf16[8,32,2048]{2,1,0:T(8,128)(2,1)} %bitcast.41), calls=%async_computation | async-start | bytes 2097152 | tf_op jit(solution)/shard_map/all_to_all | solution.py:466
  10.9 4.3 %collective-permute-start.1 = (bf16[16,2048]{1,0:T(8,128)(2,1)S(1)}, bf16[16,2048]{1,0:T(8,128)(2,1)S(1)}, u32[]{:S(2)}, u32[]{:S(2)}) collective-permute-start(bf16[16,2048]{1,0:T(8,128)(2,1)S(1)} %bitcast.27), channel_id=1, source_target_pairs={{0,2},{1,3},{2,0},{3,1},{4,6},{5,7},{6,4},{7,5},{8,10},{9,11},{10,... | collective-permute-start | bytes 196616 | tf_op jit(solution)/shard_map/ppermute | solution.py:456
  12.5 13.0 %collective-permute-start = (bf16[16,2048]{1,0:T(8,128)(2,1)S(1)}, bf16[16,2048]{1,0:T(8,128)(2,1)S(1)}, u32[]{:S(2)}, u32[]{:S(2)}) collective-permute-start(bf16[16,2048]{1,0:T(8,128)(2,1)S(1)} %bitcast.28), channel_id=1, source_target_pairs={{0,1},{1,0},{2,3},{3,2},{4,5},{5,4},{6,7},{7,6},{8,9},{9,8},{10,11... | collective-permute-start | bytes 196616 | tf_op jit(solution)/shard_map/ppermute | solution.py:456
  15.2 10.2 %collective-permute-start.2 = (bf16[16,2048]{1,0:T(8,128)(2,1)S(1)}, bf16[16,2048]{1,0:T(8,128)(2,1)S(1)}, u32[]{:S(2)}, u32[]{:S(2)}) collective-permute-start(bf16[16,2048]{1,0:T(8,128)(2,1)S(1)} %collective-permute-done.1.refs_4_.refs_7_), channel_id=1, source_target_pairs={{0,1},{1,0},{2,3},{3,2},{4,5},{5,4},{6,7},{7,6},{8,9},{9,8},{10,11... | collective-permute-start | bytes 196616 | tf_op jit(solution)/shard_map/ppermute | solution.py:456
  36.2 3.7 %collective-permute-start.3 = (bf16[8,32,2048]{2,1,0:T(8,128)(2,1)S(1)}, bf16[8,32,2048]{2,1,0:T(8,128)(2,1)S(1)}, u32[]{:S(2)}, u32[]{:S(2)}) collective-permute-start(bf16[8,32,2048]{2,1,0:T(8,128)(2,1)S(1)} %shard_map.111._.refs_1_), channel_id=1, source_target_pairs={{0,1},{1,0},{2,3},{3,2},{4,5},{5,4},{6,7},{7,6},{8,9},{9,8},{10,11... | collective-permute-start | bytes 3145736 | tf_op jit(solution)/shard_map/ppermute | solution.py:456
  36.2 25.7 %collective-permute-start.4 = (bf16[8,32,2048]{2,1,0:T(8,128)(2,1)S(1)}, bf16[8,32,2048]{2,1,0:T(8,128)(2,1)}, u32[]{:S(2)}, u32[]{:S(2)}) collective-permute-start(bf16[8,32,2048]{2,1,0:T(8,128)(2,1)S(1)} %shard_map.111._.refs_1_), channel_id=1, source_target_pairs={{0,2},{1,3},{2,0},{3,1},{4,6},{5,7},{6,4},{7,5},{8,10},{9,11},{10,... | collective-permute-start | bytes 3145736 | tf_op jit(solution)/shard_map/ppermute | solution.py:456
  44.5 33.5 %all-to-all-start.1 = ((bf16[8,2,32,1152]{3,2,1,0:T(8,128)(2,1)}), bf16[8,2,32,1152]{3,2,1,0:T(8,128)(2,1)}, u32[]{:S(2)}, u32[]{:S(2)}) async-start(bf16[8,2,32,1152]{3,2,1,0:T(8,128)(2,1)} %shard_map.113.refs_1_.refs_4_), calls=%async_computation.1 | async-start | bytes 2359296 | tf_op jit(solution)/shard_map/all_to_all | solution.py:466
  61.9 2.9 %collective-permute-start.5 = (bf16[8,32,2048]{2,1,0:T(8,128)(2,1)}, bf16[8,32,2048]{2,1,0:T(8,128)(2,1)S(1)}, u32[]{:S(2)}, u32[]{:S(2)}) collective-permute-start(bf16[8,32,2048]{2,1,0:T(8,128)(2,1)} %shard_map.114.refs_1_), channel_id=1, source_target_pairs={{0,1},{1,0},{2,3},{3,2},{4,5},{5,4},{6,7},{7,6},{8,9},{9,8},{10,11... | collective-permute-start | bytes 3145736 | tf_op jit(solution)/shard_map/ppermute | solution.py:456
  78.0 29.6 %all-to-all-start.2 = ((bf16[8,2,32,1024]{3,2,1,0:T(8,128)(2,1)}), bf16[8,2,32,1024]{3,2,1,0:T(8,128)(2,1)S(1)}, u32[]{:S(2)}, u32[]{:S(2)}) async-start(bf16[8,2,32,1024]{3,2,1,0:T(8,128)(2,1)} %shard_map.115.refs_3_), calls=%async_computation.2 | async-start | bytes 2097152 | tf_op jit(solution)/shard_map/all_to_all | solution.py:466
  97.1 4.5 %collective-permute-start.7 = (bf16[128,256]{1,0:T(8,128)(2,1)}, bf16[128,256]{1,0:T(8,128)(2,1)S(1)}, u32[]{:S(2)}, u32[]{:S(2)}) collective-permute-start(bf16[128,256]{1,0:T(8,128)(2,1)} %shard_map.118), channel_id=1, source_target_pairs={{0,2},{1,3},{2,0},{3,1},{4,6},{5,7},{6,4},{7,5},{8,10},{9,11},{10,... | collective-permute-start | bytes 196616 | tf_op jit(solution)/shard_map/ppermute | solution.py:456
  97.9 3.7 %collective-permute-start.6 = (bf16[128,256]{1,0:T(8,128)(2,1)}, bf16[128,256]{1,0:T(8,128)(2,1)S(1)}, u32[]{:S(2)}, u32[]{:S(2)}) collective-permute-start(bf16[128,256]{1,0:T(8,128)(2,1)} %shard_map.118), channel_id=1, source_target_pairs={{0,1},{1,0},{2,3},{3,2},{4,5},{5,4},{6,7},{7,6},{8,9},{9,8},{10,11... | collective-permute-start | bytes 196616 | tf_op jit(solution)/shard_map/ppermute | solution.py:456
  101.6 1.3 collective-permute-start.8
  116.9 33.2 %copy-start.5 = (bf16[256,1024]{1,0:T(8,128)(2,1)S(1)}, bf16[256,1024]{1,0:T(8,128)(2,1)}, u32[]{:S(2)}) copy-start(bf16[256,1024]{1,0:T(8,128)(2,1)} %get-tuple-element.23.refs_2_) | copy-start | bytes 1572868
  146.3 29.3 %all-to-all-start.3 = ((bf16[8,2,32,1024]{3,2,1,0:T(8,128)(2,1)}), bf16[8,2,32,1024]{3,2,1,0:T(8,128)(2,1)S(1)}, u32[]{:S(2)}, u32[]{:S(2)}) async-start(bf16[8,2,32,1024]{3,2,1,0:T(8,128)(2,1)} %get-tuple-element.21), calls=%async_computation.3 | async-start | bytes 2097152 | tf_op jit(solution)/shard_map/all_to_all | solution.py:466
  154.2 2.7 %collective-permute-start.9 = (bf16[8,32,2048]{2,1,0:T(8,128)(2,1)S(1)}, bf16[8,32,2048]{2,1,0:T(8,128)(2,1)S(1)}, u32[]{:S(2)}, u32[]{:S(2)}) collective-permute-start(bf16[8,32,2048]{2,1,0:T(8,128)(2,1)S(1)} %shard_map.121), channel_id=1, source_target_pairs={{0,1},{1,0},{2,3},{3,2},{4,5},{5,4},{6,7},{7,6},{8,9},{9,8},{10,11... | collective-permute-start | bytes 3145736 | tf_op jit(solution)/shard_map/ppermute | solution.py:456
  158.3 25.4 %collective-permute-start.10 = (bf16[8,32,2048]{2,1,0:T(8,128)(2,1)}, bf16[8,32,2048]{2,1,0:T(8,128)(2,1)S(1)}, u32[]{:S(2)}, u32[]{:S(2)}) collective-permute-start(bf16[8,32,2048]{2,1,0:T(8,128)(2,1)} %add_convert_fusion), channel_id=1, source_target_pairs={{0,2},{1,3},{2,0},{3,1},{4,6},{5,7},{6,4},{7,5},{8,10},{9,11},{10,... | collective-permute-start | bytes 3145736 | tf_op jit(solution)/shard_map/ppermute | solution.py:456
  179.7 5.9 %collective-permute-start.11 = (bf16[8,32,2048]{2,1,0:T(8,128)(2,1)S(1)}, bf16[8,32,2048]{2,1,0:T(8,128)(2,1)S(1)}, u32[]{:S(2)}, u32[]{:S(2)}) collective-permute-start(bf16[8,32,2048]{2,1,0:T(8,128)(2,1)S(1)} %shard_map.123), channel_id=1, source_target_pairs={{0,1},{1,0},{2,3},{3,2},{4,5},{5,4},{6,7},{7,6},{8,9},{9,8},{10,11... | collective-permute-start | bytes 3145736 | tf_op jit(solution)/shard_map/ppermute | solution.py:456
  186.6 7.8 %collective-permute-start.12 = (bf16[32,2048]{1,0:T(8,128)(2,1)S(1)}, bf16[32,2048]{1,0:T(8,128)(2,1)S(1)}, u32[]{:S(2)}, u32[]{:S(2)}) collective-permute-start(bf16[32,2048]{1,0:T(8,128)(2,1)S(1)} %get-tuple-element.26), channel_id=1, source_target_pairs={{0,4},{4,0},{8,12},{12,8},{16,20},{20,16},{24,28},{28,24},{1,5},{5... | collective-permute-start | bytes 393224 | tf_op jit(solution)/shard_map/ppermute | solution.py:582
  188.5 9.3 %collective-permute-start.13 = (bf16[32,2048]{1,0:T(8,128)(2,1)S(1)}, bf16[32,2048]{1,0:T(8,128)(2,1)S(1)}, u32[]{:S(2)}, u32[]{:S(2)}) collective-permute-start(bf16[32,2048]{1,0:T(8,128)(2,1)S(1)} %get-tuple-element.27), channel_id=1, source_target_pairs={{0,8},{4,12},{8,0},{12,4},{16,24},{20,28},{24,16},{28,20},{1,9},{5... | collective-permute-start | bytes 393224 | tf_op jit(solution)/shard_map/ppermute | solution.py:582
  190.0 9.9 %collective-permute-start.14 = (bf16[32,2048]{1,0:T(8,128)(2,1)S(1)}, bf16[32,2048]{1,0:T(8,128)(2,1)S(1)}, u32[]{:S(2)}, u32[]{:S(2)}) collective-permute-start(bf16[32,2048]{1,0:T(8,128)(2,1)S(1)} %get-tuple-element.28), channel_id=1, source_target_pairs={{0,12},{4,8},{8,4},{12,0},{16,28},{20,24},{24,20},{28,16},{1,13},{... | collective-permute-start | bytes 393224 | tf_op jit(solution)/shard_map/ppermute | solution.py:582
  190.1 9.7 %collective-permute-start.15 = (bf16[32,2048]{1,0:T(8,128)(2,1)S(1)}, bf16[32,2048]{1,0:T(8,128)(2,1)S(1)}, u32[]{:S(2)}, u32[]{:S(2)}) collective-permute-start(bf16[32,2048]{1,0:T(8,128)(2,1)S(1)} %get-tuple-element.29), channel_id=1, source_target_pairs={{0,16},{4,20},{8,24},{12,28},{16,0},{20,4},{24,8},{28,12},{1,17},{... | collective-permute-start | bytes 393224 | tf_op jit(solution)/shard_map/ppermute | solution.py:582
  192.9 19.8 %collective-permute-start.16 = (bf16[32,2048]{1,0:T(8,128)(2,1)S(1)}, bf16[32,2048]{1,0:T(8,128)(2,1)S(1)}, u32[]{:S(2)}, u32[]{:S(2)}) collective-permute-start(bf16[32,2048]{1,0:T(8,128)(2,1)S(1)} %get-tuple-element.30), channel_id=1, source_target_pairs={{0,20},{4,16},{8,28},{12,24},{16,4},{20,0},{24,12},{28,8},{1,21},{... | collective-permute-start | bytes 393224 | tf_op jit(solution)/shard_map/ppermute | solution.py:582
  194.3 18.3 %collective-permute-start.17 = (bf16[32,2048]{1,0:T(8,128)(2,1)S(1)}, bf16[32,2048]{1,0:T(8,128)(2,1)S(1)}, u32[]{:S(2)}, u32[]{:S(2)}) collective-permute-start(bf16[32,2048]{1,0:T(8,128)(2,1)S(1)} %get-tuple-element.31), channel_id=1, source_target_pairs={{0,24},{4,28},{8,16},{12,20},{16,8},{20,12},{24,0},{28,4},{1,25},{... | collective-permute-start | bytes 393224 | tf_op jit(solution)/shard_map/ppermute | solution.py:582
  197.8 14.9 %collective-permute-start.18 = (bf16[32,2048]{1,0:T(8,128)(2,1)S(1)}, bf16[32,2048]{1,0:T(8,128)(2,1)S(1)}, u32[]{:S(2)}, u32[]{:S(2)}) collective-permute-start(bf16[32,2048]{1,0:T(8,128)(2,1)S(1)} %get-tuple-element.32), channel_id=1, source_target_pairs={{0,28},{4,24},{8,20},{12,16},{16,12},{20,8},{24,4},{28,0},{1,29},{... | collective-permute-start | bytes 393224 | tf_op jit(solution)/shard_map/ppermute | solution.py:582
  (14 other events, 87.7 us)

commit v5 on v4

--- a/solution.py
+++ b/solution.py
@@ -294,10 +294,15 @@
     out.send(0)
 
 
-def gate_kernel(tile, info_ref, *refs):
+def gate_kernel(tile, by_peer, info_ref, *refs):
     count = len(refs) // 2
     weight, outs = refs[count], refs[count + 1 :]
-    rows = [flat_rows(ref.whole()[...]) for ref in refs[:count]]
+    rows = [ref.whole() for ref in refs[:count]]
+    if by_peer:
+        me = info_ref[info_ref.shape[0] - 1]
+        rows = [flat_rows(jnp.stack([ref[r ^ me] for r in range(ref.shape[0])])) for ref in rows]
+    else:
+        rows = [flat_rows(ref[...]) for ref in rows]
     for lo in range(0, weight.held.shape[1], tile):
         part = weight.whole()[:, lo : lo + tile]
         for block, out in zip(rows, outs):
@@ -306,13 +311,20 @@
         out.send(0)
 
 
-def output_kernel(at, experts, cap, tile, info_ref, scanned, gate, weight, out):
+def output_kernel(at, experts, cap, tile, info_ref, *refs):
+    scanned, (gate, weight, out) = refs[:-3], refs[-3:]
+    if len(scanned) > 1:
+        me = info_ref[info_ref.shape[0] - 1]
+        rows = flat_rows(jnp.stack([ref.held[at] for ref in scanned]))
+    else:
+        me = 0
+        rows = flat_rows(scanned[0].held[:, at])
     gates = jax.nn.silu(gate.held[...].astype(F32))
-    gated = (flat_rows(scanned.held[:, at]).astype(F32) * gates).astype(BF16)
+    gated = (rows.astype(F32) * gates).astype(BF16)
     for lo in range(0, weight.held.shape[1], tile):
         made = dot(gated, weight.held[:, lo : lo + tile]).astype(BF16)
-        for e in range(experts):
-            out.held[e, :, lo : lo + tile] = made[e * cap : (e + 1) * cap, :]
+        for r in range(experts):
+            out.held[r ^ me, :, lo : lo + tile] = made[r * cap : (r + 1) * cap, :]
 
 
 def scan_kernel(
@@ -329,7 +341,8 @@
     experts, cap, tok_rows, nstate, chn, heads = cfg
     blocks = ids_ref.shape[0]
     taps = 4
-    out_near, out_far, inner_ref, made_ref = refs
+    out_near, out_far, (inner_ref, made_ref) = refs[0], refs[1:-2], refs[-2:]
+    me = info_ref[info_ref.shape[0] - 1]
     far_ref, side_ref = far.whole(), side.whole()
     inner_ref[:8, :] = jnp.zeros((8, chn), F32)
 
@@ -404,7 +417,7 @@
 
     for q in range(blocks):
         b = info_ref[1 + q]
-        place = slot_rows(ids_ref[b], experts, cap).astype(BF16)
+        place = slot_rows(ids_ref[b], experts, cap, 0 if q < 2 else me).astype(BF16)
         start = pl.multiple_of(b * tok_rows, tok_rows)
         leaving = dot(place, made_ref[pl.ds(start, tok_rows), :]).astype(BF16)
         for e in range(experts):
@@ -412,7 +425,7 @@
             if q < 2:
                 out_near.held[e, q] = piece
             else:
-                out_far.held[e, q - 2] = piece
+                out_far[e].held[q - 2] = piece
 
 
 def per_device(
@@ -464,6 +477,13 @@
 
     def exchange(value):
         return lax.all_to_all(value, "expert", split_axis=0, concat_axis=0, tiled=True)
+
+    def to_peers(pieces):
+        sent = [
+            lax.ppermute(pieces[r], "expert", [(e, e ^ r) for e in range(experts)])
+            for r in range(experts - 1, 0, -1)
+        ]
+        return [pieces[0]] + sent[::-1]
 
     w_flat = w_inner[0].reshape(width, 2 * chans)
 
@@ -499,9 +519,9 @@
     near_back = exchange(near)
     far_back = exchange(far)
 
-    def gates(rows, fetch):
+    def gates(rows, fetch, by_peer):
         return call(
-            functools.partial(gate_kernel, 256),
+            functools.partial(gate_kernel, 256, by_peer),
             info,
             [fetch(part) for part in rows]
             + [columns(w_flat, 0, chans)],
@@ -510,8 +530,8 @@
             flops=2 * len(rows) * slots * width * chans,
         )
 
-    gate_near = gates([own, swapped], kept_in_vmem)
-    gate_far = gates(distant, full)
+    gate_near = gates([own, swapped], kept_in_vmem, False)
+    gate_far = gates(distant, full, True)
 
     lanes = (slice(None),) * 3 + (pl.ds(chans, LANES),)
     side = call(
@@ -537,13 +557,13 @@
     chan_rows = jnp.pad(chan_rows, ((0, 2), (0, 0)))
     cfg = (experts, cap, tok_rows, nstate, chans, heads)
     each = list(range(shards))
-    near_out, far_out = call(
+    near_out, *far_out = call(
         functools.partial(scan_kernel, cfg),
         info,
         [full(near_back), kept_in_vmem(sides), kept_in_vmem(far_back)],
         [
             (shape(experts, 2, cap, chans), None),
-            (shape(experts, far_count, cap, chans), None),
+            *[(shape(far_count, cap, chans), None)] * experts,
         ],
         small=[ids, head_rows, chan_rows],
         scratch=[
@@ -553,13 +573,14 @@
         flops=2 * shards * tok_rows * chans * (2 * slots + 2 * nstate + 2 * tok_rows + 768),
         exps=shards * tok_rows * tok_rows * heads,
     )
-    far_ret = exchange(far_out)
-    near_ret = exchange(near_out)
+    far_ret = to_peers(far_out)
+    near_ret = exchange(tie([near_out], after_vmem=far_ret, hbm=True)[0])
+
     def output(scanned, gate, at, after=()):
         return call(
             functools.partial(output_kernel, at, experts, cap, 512),
             info,
-            [kept_in_vmem(array) for array in (scanned, gate, w_out[0])],
+            [kept_in_vmem(array) for array in (*scanned, gate, w_out[0])],
             [(shape(experts, cap, width), None)],
             after_vmem=after,
             flops=2 * slots * width * chans,
@@ -570,19 +591,15 @@
     for k in range(1, chips):
         pair = output(far_ret, gate_far[2 * k - 2], 2 * k - 2).astype(F32) + others[k - 1].astype(F32)
         hopped.append(permute(pair.astype(BF16), hop(chips - k)))
-    part_swap = permute(output(near_ret, gate_near[1], 1), swap)
-    part_own = output(near_ret, gate_near[0], 0, hopped)
+    part_swap = permute(output([near_ret], gate_near[1], 1), swap)
+    part_own = output([near_ret], gate_near[0], 0, hopped)
     summed = call(
         functools.partial(sum_kernel, experts, 1 + chips),
         info,
         [kept_in_vmem(part) for part in (part_own, part_swap, *hopped)],
         [(shape(cap, width), None)] * experts,
     )
-    returned = [
-        lax.ppermute(summed[r], "expert", [(e, e ^ r) for e in range(experts)])
-        for r in range(experts - 1, 0, -1)
-    ]
-    returned = [summed[0]] + returned[::-1]
+    returned = to_peers(summed)
     result = call(
         functools.partial(collect_kernel, experts, cap),
         info, [kept_in_vmem(part) for part in returned], [(shape(tok_rows, width), once)],

time: 217 us -> 216 us (level)
  blocking collectives: 29.4 us -> 0 us
  waiting for transfers between devices: 78.6 us -> 93.1 us
  starting transfers between devices: 35.5 us -> 48.6 us
    all_to_all x1 -> x0, blocking collectives: 29.4 us -> none  [exchange(): lax.all_to_all(value, 'expert', split_axis=0, concat_axis=0, tiled=True)]
    ppermute x7 -> x14, waiting for transfers between devices: 14 us -> 28.5 us  [to_peers(): lax.ppermute(pieces[r], 'expert', [(e, e ^ r) for e in range(experts)])]
    ppermute x7 -> x14, starting transfers between devices: 12.1 us -> 22 us  [to_peers(): lax.ppermute(pieces[r], 'expert', [(e, e ^ r) for e in range(experts)])]
    all_to_all x4, starting transfers between devices: 19.1 us -> 22.2 us  [exchange(): lax.all_to_all(value, 'expert', split_axis=0, concat_axis=0, tiled=True)]
    unnamed x32 -> x34, local copies, waits for them, and re-layouts: 16 us -> 16.9 us
  transfers between devices with their start and end apart: 23 -> 30, of which waited for: 14 -> 18; matrix products, arithmetic and copies ran while one was open for 6% -> 6% of each run, Pallas kernels for 17% -> 17%
where the time goes in v5:
time: 216 us; the launch traced here: 214 us
  waiting for transfers between devices  93.1 us (43%)
  Pallas kernels  51.8 us (24%)
  starting transfers between devices  48.6 us (22%)
  local copies, waits for them, and re-layouts  17.4 us (8%)
  other arithmetic  2.38 us (1%)
    pallas_call x13, Pallas kernels, call(): pl.pallas_call(body, out_shape=[(pltpu.HBM if pieces else pltpu.VMEM)(o.s...  49.6 us
    all_to_all x4, waiting for transfers between devices, exchange(): lax.all_to_all(value, 'expert', split_axis=0, concat_axis=0, tiled=True)  35.7 us
    ppermute x12, waiting for transfers between devices, permute(): return lax.ppermute(value, 'context', pairs)  28.8 us
    ppermute x14, waiting for transfers between devices, to_peers(): lax.ppermute(pieces[r], 'expert', [(e, e ^ r) for e in range(experts)])  28.5 us
    all_to_all x4, starting transfers between devices, exchange(): lax.all_to_all(value, 'expert', split_axis=0, concat_axis=0, tiled=True)  22.2 us
    ppermute x14, starting transfers between devices, to_peers(): lax.ppermute(pieces[r], 'expert', [(e, e ^ r) for e in range(experts)])  22 us
    unnamed x34, local copies, waits for them, and re-layouts  16.9 us
  transfers between devices with their start and end apart: 30, of which 18 were waited for; matrix products, arithmetic and copies ran while one was open for 6% of the time, Pallas kernels for 17%

profile of v5, /device:TPU:0, one launch (start us, length us, event | category | flops | bytes accessed | tf_op | source)
XLA Modules:
  0.0 213.8 jit_solution(1340367414224334228)
XLA Ops:
  0.1 3.0 %shard_map.109.refs_1_ = bf16[256,2048]{1,0:T(8,128)(2,1)} custom-call(s32[14]{0:T(128)S(1)} %concatenate.9.refs_0_, s32[4,1,128]{2,1,0:T(1,128)} %bitcast.31, bf16[128,2048]{1,0:T(8,128)(2,1)} %bitcast.43), custom_call_target="tpu_custom_call" | custom-call | flops 134217728 | bytes 1573888 | tf_op jit(solution)/shard_map/pallas_call | solution.py:181
  3.1 7.3 %all-to-all-start = ((bf16[8,32,2048]{2,1,0:T(8,128)(2,1)}), bf16[8,32,2048]{2,1,0:T(8,128)(2,1)S(1)}, u32[]{:S(2)}, u32[]{:S(2)}) async-start(bf16[8,32,2048]{2,1,0:T(8,128)(2,1)} %bitcast.41), calls=%async_computation | async-start | bytes 2097152 | tf_op jit(solution)/shard_map/all_to_all | solution.py:479
  15.2 10.2 %copy.18 = bf16[256,8,2,1024]{3,1,2,0:T(8,128)(2,1)} copy(bf16[256,8,2,1024]{3,2,1,0:T(2,128)(2,1)} %bitcast.42) | data formatting | bytes 16777216
  25.5 10.7 %all-to-all-done.refs_0_ = bf16[8,32,2048]{2,1,0:T(8,128)(2,1)S(1)} async-done(((bf16[8,32,2048]{2,1,0:T(8,128)(2,1)}), bf16[8,32,2048]{2,1,0:T(8,128)(2,1)S(1)}, u32[]{:S(2)}, u32[]{:S(2)}) %all-to-all-start) | async-done | bytes 1048608 | tf_op jit(solution)/shard_map/all_to_all | solution.py:479
  39.9 4.6 %shard_map.113.refs_1_.refs_4_ = bf16[8,2,32,1152]{3,2,1,0:T(8,128)(2,1)} custom-call(s32[14]{0:T(128)S(1)} %concatenate.9.refs_0_, bf16[8,32,2048]{2,1,0:T(8,128)(2,1)S(1)} %shard_map.111._.refs_1_, bf16[8,32,2048]{2,1,0:T(8,128)(2,1)S(1)} %collective-permute-done.3.refs_2_, bf16[2048,1024]{1,0:T(8,128)(2,1)S(1)} %shard_map.112.refs_3_, ...), custom_call_target="tpu_custom_call" | custom-call | flops 2415919104 | bytes 8257536 | tf_op jit(solution)/shard_map/pallas_call | solution.py:181
  44.5 4.3 %all-to-all-start.1 = ((bf16[8,2,32,1152]{3,2,1,0:T(8,128)(2,1)}), bf16[8,2,32,1152]{3,2,1,0:T(8,128)(2,1)}, u32[]{:S(2)}, u32[]{:S(2)}) async-start(bf16[8,2,32,1152]{3,2,1,0:T(8,128)(2,1)} %shard_map.113.refs_1_.refs_4_), calls=%async_computation.1 | async-start | bytes 2359296 | tf_op jit(solution)/shard_map/all_to_all | solution.py:479
  48.8 13.1 %collective-permute-done.4.refs_0_ = bf16[8,32,2048]{2,1,0:T(8,128)(2,1)} collective-permute-done((bf16[8,32,2048]{2,1,0:T(8,128)(2,1)S(1)}, bf16[8,32,2048]{2,1,0:T(8,128)(2,1)}, u32[]{:S(2)}, u32[]{:S(2)}) %collective-permute-start.4) | collective-permute-done | bytes 1048608 | tf_op jit(solution)/shard_map/ppermute | solution.py:469
  61.9 2.9 %collective-permute-done.5.refs_2_ = bf16[8,32,2048]{2,1,0:T(8,128)(2,1)S(1)} collective-permute-done((bf16[8,32,2048]{2,1,0:T(8,128)(2,1)}, bf16[8,32,2048]{2,1,0:T(8,128)(2,1)S(1)}, u32[]{:S(2)}, u32[]{:S(2)}) %collective-permute-start.5) | collective-permute-done | bytes 1048608 | tf_op jit(solution)/shard_map/ppermute | solution.py:469
  65.8 7.4 %shard_map.115.refs_3_ = bf16[8,2,32,1024]{3,2,1,0:T(8,128)(2,1)} custom-call(s32[14]{0:T(128)S(1)} %concatenate.9.refs_0_, bf16[8,32,2048]{2,1,0:T(8,128)(2,1)} %shard_map.114.refs_1_, bf16[8,32,2048]{2,1,0:T(8,128)(2,1)} %copy-done.9, bf16[2048,2048]{1,0:T(8,128)(2,1)} %bitcast.38), custom_call_target="tpu_custom_call" | custom-call | flops 2147483648 | bytes 11534336 | tf_op jit(solution)/shard_map/pallas_call | solution.py:181
  73.3 4.7 %all-to-all-done.1.refs_2_.refs_4_ = bf16[8,2,32,1152]{3,2,1,0:T(8,128)(2,1)} async-done(((bf16[8,2,32,1152]{3,2,1,0:T(8,128)(2,1)}), bf16[8,2,32,1152]{3,2,1,0:T(8,128)(2,1)}, u32[]{:S(2)}, u32[]{:S(2)}) %all-to-all-start.1) | async-done | bytes 1179680 | tf_op jit(solution)/shard_map/all_to_all | solution.py:479
  78.0 3.7 %all-to-all-start.2 = ((bf16[8,2,32,1024]{3,2,1,0:T(8,128)(2,1)}), bf16[8,2,32,1024]{3,2,1,0:T(8,128)(2,1)S(1)}, u32[]{:S(2)}, u32[]{:S(2)}) async-start(bf16[8,2,32,1024]{3,2,1,0:T(8,128)(2,1)} %shard_map.115.refs_3_), calls=%async_computation.2 | async-start | bytes 2097152 | tf_op jit(solution)/shard_map/all_to_all | solution.py:479
  81.9 6.1 %shard_map.116 = (bf16[256,1024]{1,0:T(8,128)(2,1)}, bf16[256,1024]{1,0:T(8,128)(2,1)}) custom-call(s32[14]{0:T(128)S(1)} %concatenate.9.refs_0_, bf16[8,32,2048]{2,1,0:T(8,128)(2,1)S(1)} %shard_map.111._.refs_1_, bf16[8,32,2048]{2,1,0:T(8,128)(2,1)S(1)} %collective-permute-done.3.refs_2_, bf16[2048,2048]{1,0:T(8,128)(2,1)} %bitcast.39, ...), custom_call_target="tpu_custom_call" | custom-call | flops 2147483648 | bytes 11534336 | tf_op jit(solution)/shard_map/pallas_call | solution.py:181
  88.0 6.7 %shard_map.117 = (bf16[256,1024]{1,0:T(8,128)(2,1)}, bf16[256,1024]{1,0:T(8,128)(2,1)}) custom-call(s32[14]{0:T(128)S(1)} %concatenate.9.refs_0_, bf16[8,32,2048]{2,1,0:T(8,128)(2,1)} %shard_map.114.refs_1_, bf16[8,32,2048]{2,1,0:T(8,128)(2,1)} %copy-done.9, bf16[2048,2048]{1,0:T(8,128)(2,1)} %bitcast.40, bf16[8,2,32,1152]{3,2,1,0:T(8,128)(2,1)} %shard_map.113.refs_1_.refs_4_), custom_call_target="tpu_custom_call" | custom-call | flops 2147483648 | bytes 11534336 | tf_op jit(solution)/shard_map/pallas_call | solution.py:181
  97.9 3.7 %collective-permute-done.7 = bf16[128,256]{1,0:T(8,128)(2,1)S(1)} collective-permute-done((bf16[128,256]{1,0:T(8,128)(2,1)}, bf16[128,256]{1,0:T(8,128)(2,1)S(1)}, u32[]{:S(2)}, u32[]{:S(2)}) %collective-permute-start.7) | collective-permute-done | bytes 65568 | tf_op jit(solution)/shard_map/ppermute | solution.py:469
  103.7 3.9 %all-to-all-done.2.refs_6_ = bf16[8,2,32,1024]{3,2,1,0:T(8,128)(2,1)S(1)} async-done(((bf16[8,2,32,1024]{3,2,1,0:T(8,128)(2,1)}), bf16[8,2,32,1024]{3,2,1,0:T(8,128)(2,1)S(1)}, u32[]{:S(2)}, u32[]{:S(2)}) %all-to-all-start.2) | async-done | bytes 1048608 | tf_op jit(solution)/shard_map/all_to_all | solution.py:479
  107.6 9.2 %shard_map.119 = (bf16[8,2,32,1024]{3,2,1,0:T(8,128)(2,1)S(1)}, bf16[2,32,1024]{2,1,0:T(8,128)(2,1)S(1)}, bf16[2,32,1024]{2,1,0:T(8,128)(2,1)S(1)}, bf16[2,32,10...) custom-call(s32[14]{0:T(128)S(1)} %concatenate.9.refs_0_, ...), custom_call_target="tpu_custom_call" | custom-call | flops 1744830464 | bytes 4587520 | tf_op jit(solution)/shard_map/pallas_call | solution.py:181
  120.7 2.9 %collective-permute-start.13 = (bf16[2,32,1024]{2,1,0:T(8,128)(2,1)S(1)}, bf16[2,32,1024]{2,1,0:T(8,128)(2,1)S(1)}, u32[]{:S(2)}, u32[]{:S(2)}) collective-permute-start(bf16[2,32,1024]{2,1,0:T(8,128)(2,1)S(1)} %get-tuple-element.34), channel_id=1, source_target_pairs={{0,20},{4,16},{8,28},{12,24},{16,4},{20,0},{24,12},{28,8},{1,21},{... | collective-permute-start | bytes 393224 | tf_op jit(solution)/shard_map/ppermute | solution.py:483
  129.5 9.6 %collective-permute-done.12.refs_5_ = bf16[2,32,1024]{2,1,0:T(8,128)(2,1)S(1)} collective-permute-done((bf16[2,32,1024]{2,1,0:T(8,128)(2,1)S(1)}, bf16[2,32,1024]{2,1,0:T(8,128)(2,1)S(1)}, u32[]{:S(2)}, u32[]{:S(2)}) %collective-permute-start.12) | collective-permute-done | bytes 131104 | tf_op jit(solution)/shard_map/ppermute | solution.py:483
  139.1 2.9 %collective-permute-done.13.refs_6_ = bf16[2,32,1024]{2,1,0:T(8,128)(2,1)S(1)} collective-permute-done((bf16[2,32,1024]{2,1,0:T(8,128)(2,1)S(1)}, bf16[2,32,1024]{2,1,0:T(8,128)(2,1)S(1)}, u32[]{:S(2)}, u32[]{:S(2)}) %collective-permute-start.13) | collective-permute-done | bytes 131104 | tf_op jit(solution)/shard_map/ppermute | solution.py:483
  142.0 6.9 %all-to-all-start.3 = ((bf16[8,2,32,1024]{3,2,1,0:T(8,128)(2,1)}), bf16[8,2,32,1024]{3,2,1,0:T(8,128)(2,1)S(1)}, u32[]{:S(2)}, u32[]{:S(2)}) async-start(bf16[8,2,32,1024]{3,2,1,0:T(8,128)(2,1)} %shard_map.120), calls=%async_computation.3 | async-start | bytes 2097152 | tf_op jit(solution)/shard_map/all_to_all | solution.py:479
  157.7 16.3 %all-to-all-done.3.refs_1_ = bf16[8,2,32,1024]{3,2,1,0:T(8,128)(2,1)S(1)} async-done(((bf16[8,2,32,1024]{3,2,1,0:T(8,128)(2,1)}), bf16[8,2,32,1024]{3,2,1,0:T(8,128)(2,1)S(1)}, u32[]{:S(2)}, u32[]{:S(2)}) %all-to-all-start.3) | async-done | bytes 1048608 | tf_op jit(solution)/shard_map/all_to_all | solution.py:479
  178.2 4.4 %collective-permute-done.17.refs_4_.refs_3_ = bf16[8,32,2048]{2,1,0:T(8,128)(2,1)S(1)} collective-permute-done((bf16[8,32,2048]{2,1,0:T(8,128)(2,1)}, bf16[8,32,2048]{2,1,0:T(8,128)(2,1)S(1)}, u32[]{:S(2)}, u32[]{:S(2)}) %collective-permute-start.17) | collective-permute-done | bytes 1048608 | tf_op jit(solution)/shard_map/ppermute | solution.py:469
  193.4 3.3 %collective-permute-start.24 = (bf16[32,2048]{1,0:T(8,128)(2,1)S(1)}, bf16[32,2048]{1,0:T(8,128)(2,1)S(1)}, u32[]{:S(2)}, u32[]{:S(2)}) collective-permute-start(bf16[32,2048]{1,0:T(8,128)(2,1)S(1)} %get-tuple-element.45), channel_id=1, source_target_pairs={{0,24},{4,28},{8,16},{12,20},{16,8},{20,12},{24,0},{28,4},{1,25},{... | collective-permute-start | bytes 393224 | tf_op jit(solution)/shard_map/ppermute | solution.py:483
  198.8 12.9 %collective-permute-done.23.refs_7_ = bf16[32,2048]{1,0:T(8,128)(2,1)S(1)} collective-permute-done((bf16[32,2048]{1,0:T(8,128)(2,1)S(1)}, bf16[32,2048]{1,0:T(8,128)(2,1)S(1)}, u32[]{:S(2)}, u32[]{:S(2)}) %collective-permute-start.23) | collective-permute-done | bytes 131104 | tf_op jit(solution)/shard_map/ppermute | solution.py:483
  (101 shorter events, 52.3 us)
Async XLA Ops:
  3.1 33.1 %all-to-all-start = ((bf16[8,32,2048]{2,1,0:T(8,128)(2,1)}), bf16[8,32,2048]{2,1,0:T(8,128)(2,1)S(1)}, u32[]{:S(2)}, u32[]{:S(2)}) async-start(bf16[8,32,2048]{2,1,0:T(8,128)(2,1)} %bitcast.41), calls=%async_computation | async-start | bytes 2097152 | tf_op jit(solution)/shard_map/all_to_all | solution.py:479
  12.4 13.0 %collective-permute-start = (bf16[16,2048]{1,0:T(8,128)(2,1)S(1)}, bf16[16,2048]{1,0:T(8,128)(2,1)S(1)}, u32[]{:S(2)}, u32[]{:S(2)}) collective-permute-start(bf16[16,2048]{1,0:T(8,128)(2,1)S(1)} %bitcast.28), channel_id=1, source_target_pairs={{0,1},{1,0},{2,3},{3,2},{4,5},{5,4},{6,7},{7,6},{8,9},{9,8},{10,11... | collective-permute-start | bytes 196616 | tf_op jit(solution)/shard_map/ppermute | solution.py:469
  15.2 10.2 %collective-permute-start.2 = (bf16[16,2048]{1,0:T(8,128)(2,1)S(1)}, bf16[16,2048]{1,0:T(8,128)(2,1)S(1)}, u32[]{:S(2)}, u32[]{:S(2)}) collective-permute-start(bf16[16,2048]{1,0:T(8,128)(2,1)S(1)} %collective-permute-done.1.refs_4_.refs_7_), channel_id=1, source_target_pairs={{0,1},{1,0},{2,3},{3,2},{4,5},{5,4},{6,7},{7,6},{8,9},{9,8},{10,11... | collective-permute-start | bytes 196616 | tf_op jit(solution)/shard_map/ppermute | solution.py:469
  36.2 25.7 %collective-permute-start.4 = (bf16[8,32,2048]{2,1,0:T(8,128)(2,1)S(1)}, bf16[8,32,2048]{2,1,0:T(8,128)(2,1)}, u32[]{:S(2)}, u32[]{:S(2)}) collective-permute-start(bf16[8,32,2048]{2,1,0:T(8,128)(2,1)S(1)} %shard_map.111._.refs_1_), channel_id=1, source_target_pairs={{0,2},{1,3},{2,0},{3,1},{4,6},{5,7},{6,4},{7,5},{8,10},{9,11},{10,... | collective-permute-start | bytes 3145736 | tf_op jit(solution)/shard_map/ppermute | solution.py:469
  44.5 33.5 %all-to-all-start.1 = ((bf16[8,2,32,1152]{3,2,1,0:T(8,128)(2,1)}), bf16[8,2,32,1152]{3,2,1,0:T(8,128)(2,1)}, u32[]{:S(2)}, u32[]{:S(2)}) async-start(bf16[8,2,32,1152]{3,2,1,0:T(8,128)(2,1)} %shard_map.113.refs_1_.refs_4_), calls=%async_computation.1 | async-start | bytes 2359296 | tf_op jit(solution)/shard_map/all_to_all | solution.py:479
  78.0 29.6 %all-to-all-start.2 = ((bf16[8,2,32,1024]{3,2,1,0:T(8,128)(2,1)}), bf16[8,2,32,1024]{3,2,1,0:T(8,128)(2,1)S(1)}, u32[]{:S(2)}, u32[]{:S(2)}) async-start(bf16[8,2,32,1024]{3,2,1,0:T(8,128)(2,1)} %shard_map.115.refs_3_), calls=%async_computation.2 | async-start | bytes 2097152 | tf_op jit(solution)/shard_map/all_to_all | solution.py:479
  97.0 4.5 %collective-permute-start.7 = (bf16[128,256]{1,0:T(8,128)(2,1)}, bf16[128,256]{1,0:T(8,128)(2,1)S(1)}, u32[]{:S(2)}, u32[]{:S(2)}) collective-permute-start(bf16[128,256]{1,0:T(8,128)(2,1)} %shard_map.118), channel_id=1, source_target_pairs={{0,2},{1,3},{2,0},{3,1},{4,6},{5,7},{6,4},{7,5},{8,10},{9,11},{10,... | collective-permute-start | bytes 196616 | tf_op jit(solution)/shard_map/ppermute | solution.py:469
  117.8 8.7 %collective-permute-start.10 = (bf16[2,32,1024]{2,1,0:T(8,128)(2,1)S(1)}, bf16[2,32,1024]{2,1,0:T(8,128)(2,1)S(1)}, u32[]{:S(2)}, u32[]{:S(2)}) collective-permute-start(bf16[2,32,1024]{2,1,0:T(8,128)(2,1)S(1)} %get-tuple-element.31), channel_id=1, source_target_pairs={{0,8},{4,12},{8,0},{12,4},{16,24},{20,28},{24,16},{28,20},{1,9},{5... | collective-permute-start | bytes 393224 | tf_op jit(solution)/shard_map/ppermute | solution.py:483
  117.8 11.7 %collective-permute-start.11 = (bf16[2,32,1024]{2,1,0:T(8,128)(2,1)S(1)}, bf16[2,32,1024]{2,1,0:T(8,128)(2,1)S(1)}, u32[]{:S(2)}, u32[]{:S(2)}) collective-permute-start(bf16[2,32,1024]{2,1,0:T(8,128)(2,1)S(1)} %get-tuple-element.32), channel_id=1, source_target_pairs={{0,12},{4,8},{8,4},{12,0},{16,28},{20,24},{24,20},{28,16},{1,13},{... | collective-permute-start | bytes 393224 | tf_op jit(solution)/shard_map/ppermute | solution.py:483
  120.6 18.5 %collective-permute-start.12 = (bf16[2,32,1024]{2,1,0:T(8,128)(2,1)S(1)}, bf16[2,32,1024]{2,1,0:T(8,128)(2,1)S(1)}, u32[]{:S(2)}, u32[]{:S(2)}) collective-permute-start(bf16[2,32,1024]{2,1,0:T(8,128)(2,1)S(1)} %get-tuple-element.33), channel_id=1, source_target_pairs={{0,16},{4,20},{8,24},{12,28},{16,0},{20,4},{24,8},{28,12},{1,17},{... | collective-permute-start | bytes 393224 | tf_op jit(solution)/shard_map/ppermute | solution.py:483
  120.7 21.3 %collective-permute-start.13 = (bf16[2,32,1024]{2,1,0:T(8,128)(2,1)S(1)}, bf16[2,32,1024]{2,1,0:T(8,128)(2,1)S(1)}, u32[]{:S(2)}, u32[]{:S(2)}) collective-permute-start(bf16[2,32,1024]{2,1,0:T(8,128)(2,1)S(1)} %get-tuple-element.34), channel_id=1, source_target_pairs={{0,20},{4,16},{8,28},{12,24},{16,4},{20,0},{24,12},{28,8},{1,21},{... | collective-permute-start | bytes 393224 | tf_op jit(solution)/shard_map/ppermute | solution.py:483
  123.6 18.4 %collective-permute-start.14 = (bf16[2,32,1024]{2,1,0:T(8,128)(2,1)S(1)}, bf16[2,32,1024]{2,1,0:T(8,128)(2,1)S(1)}, u32[]{:S(2)}, u32[]{:S(2)}) collective-permute-start(bf16[2,32,1024]{2,1,0:T(8,128)(2,1)S(1)} %get-tuple-element.35), channel_id=1, source_target_pairs={{0,24},{4,28},{8,16},{12,20},{16,8},{20,12},{24,0},{28,4},{1,25},{... | collective-permute-start | bytes 393224 | tf_op jit(solution)/shard_map/ppermute | solution.py:483
  126.5 15.5 %collective-permute-start.15 = (bf16[2,32,1024]{2,1,0:T(8,128)(2,1)S(1)}, bf16[2,32,1024]{2,1,0:T(8,128)(2,1)S(1)}, u32[]{:S(2)}, u32[]{:S(2)}) collective-permute-start(bf16[2,32,1024]{2,1,0:T(8,128)(2,1)S(1)} %get-tuple-element.36), channel_id=1, source_target_pairs={{0,28},{4,24},{8,20},{12,16},{16,12},{20,8},{24,4},{28,0},{1,29},{... | collective-permute-start | bytes 393224 | tf_op jit(solution)/shard_map/ppermute | solution.py:483
  129.4 12.6 %collective-permute-start.9 = (bf16[2,32,1024]{2,1,0:T(8,128)(2,1)S(1)}, bf16[2,32,1024]{2,1,0:T(8,128)(2,1)S(1)}, u32[]{:S(2)}, u32[]{:S(2)}) collective-permute-start(bf16[2,32,1024]{2,1,0:T(8,128)(2,1)S(1)} %get-tuple-element.30), channel_id=1, source_target_pairs={{0,4},{4,0},{8,12},{12,8},{16,20},{20,16},{24,28},{28,24},{1,5},{5... | collective-permute-start | bytes 393224 | tf_op jit(solution)/shard_map/ppermute | solution.py:483
  142.0 32.0 %all-to-all-start.3 = ((bf16[8,2,32,1024]{3,2,1,0:T(8,128)(2,1)}), bf16[8,2,32,1024]{3,2,1,0:T(8,128)(2,1)S(1)}, u32[]{:S(2)}, u32[]{:S(2)}) async-start(bf16[8,2,32,1024]{3,2,1,0:T(8,128)(2,1)} %shard_map.120), calls=%async_computation.3 | async-start | bytes 2097152 | tf_op jit(solution)/shard_map/all_to_all | solution.py:479
  157.2 25.4 %collective-permute-start.17 = (bf16[8,32,2048]{2,1,0:T(8,128)(2,1)}, bf16[8,32,2048]{2,1,0:T(8,128)(2,1)S(1)}, u32[]{:S(2)}, u32[]{:S(2)}) collective-permute-start(bf16[8,32,2048]{2,1,0:T(8,128)(2,1)} %add_convert_fusion), channel_id=1, source_target_pairs={{0,2},{1,3},{2,0},{3,1},{4,6},{5,7},{6,4},{7,5},{8,10},{9,11},{10,... | collective-permute-start | bytes 3145736 | tf_op jit(solution)/shard_map/ppermute | solution.py:469
  178.1 6.3 %collective-permute-start.18 = (bf16[8,32,2048]{2,1,0:T(8,128)(2,1)S(1)}, bf16[8,32,2048]{2,1,0:T(8,128)(2,1)S(1)}, u32[]{:S(2)}, u32[]{:S(2)}) collective-permute-start(bf16[8,32,2048]{2,1,0:T(8,128)(2,1)S(1)} %shard_map.124), channel_id=1, source_target_pairs={{0,1},{1,0},{2,3},{3,2},{4,5},{5,4},{6,7},{7,6},{8,9},{9,8},{10,11... | collective-permute-start | bytes 3145736 | tf_op jit(solution)/shard_map/ppermute | solution.py:469
  185.5 8.0 %collective-permute-start.19 = (bf16[32,2048]{1,0:T(8,128)(2,1)S(1)}, bf16[32,2048]{1,0:T(8,128)(2,1)S(1)}, u32[]{:S(2)}, u32[]{:S(2)}) collective-permute-start(bf16[32,2048]{1,0:T(8,128)(2,1)S(1)} %get-tuple-element.40), channel_id=1, source_target_pairs={{0,4},{4,0},{8,12},{12,8},{16,20},{20,16},{24,28},{28,24},{1,5},{5... | collective-permute-start | bytes 393224 | tf_op jit(solution)/shard_map/ppermute | solution.py:483
  187.6 9.4 %collective-permute-start.20 = (bf16[32,2048]{1,0:T(8,128)(2,1)S(1)}, bf16[32,2048]{1,0:T(8,128)(2,1)S(1)}, u32[]{:S(2)}, u32[]{:S(2)}) collective-permute-start(bf16[32,2048]{1,0:T(8,128)(2,1)S(1)} %get-tuple-element.41), channel_id=1, source_target_pairs={{0,8},{4,12},{8,0},{12,4},{16,24},{20,28},{24,16},{28,20},{1,9},{5... | collective-permute-start | bytes 393224 | tf_op jit(solution)/shard_map/ppermute | solution.py:483
  189.0 9.8 %collective-permute-start.21 = (bf16[32,2048]{1,0:T(8,128)(2,1)S(1)}, bf16[32,2048]{1,0:T(8,128)(2,1)S(1)}, u32[]{:S(2)}, u32[]{:S(2)}) collective-permute-start(bf16[32,2048]{1,0:T(8,128)(2,1)S(1)} %get-tuple-element.42), channel_id=1, source_target_pairs={{0,12},{4,8},{8,4},{12,0},{16,28},{20,24},{24,20},{28,16},{1,13},{... | collective-permute-start | bytes 393224 | tf_op jit(solution)/shard_map/ppermute | solution.py:483
  189.1 9.7 %collective-permute-start.22 = (bf16[32,2048]{1,0:T(8,128)(2,1)S(1)}, bf16[32,2048]{1,0:T(8,128)(2,1)S(1)}, u32[]{:S(2)}, u32[]{:S(2)}) collective-permute-start(bf16[32,2048]{1,0:T(8,128)(2,1)S(1)} %get-tuple-element.43), channel_id=1, source_target_pairs={{0,16},{4,20},{8,24},{12,28},{16,0},{20,4},{24,8},{28,12},{1,17},{... | collective-permute-start | bytes 393224 | tf_op jit(solution)/shard_map/ppermute | solution.py:483
  191.9 19.8 %collective-permute-start.23 = (bf16[32,2048]{1,0:T(8,128)(2,1)S(1)}, bf16[32,2048]{1,0:T(8,128)(2,1)S(1)}, u32[]{:S(2)}, u32[]{:S(2)}) collective-permute-start(bf16[32,2048]{1,0:T(8,128)(2,1)S(1)} %get-tuple-element.44), channel_id=1, source_target_pairs={{0,20},{4,16},{8,28},{12,24},{16,4},{20,0},{24,12},{28,8},{1,21},{... | collective-permute-start | bytes 393224 | tf_op jit(solution)/shard_map/ppermute | solution.py:483
  193.4 18.4 %collective-permute-start.24 = (bf16[32,2048]{1,0:T(8,128)(2,1)S(1)}, bf16[32,2048]{1,0:T(8,128)(2,1)S(1)}, u32[]{:S(2)}, u32[]{:S(2)}) collective-permute-start(bf16[32,2048]{1,0:T(8,128)(2,1)S(1)} %get-tuple-element.45), channel_id=1, source_target_pairs={{0,24},{4,28},{8,16},{12,20},{16,8},{20,12},{24,0},{28,4},{1,25},{... | collective-permute-start | bytes 393224 | tf_op jit(solution)/shard_map/ppermute | solution.py:483
  197.0 14.8 %collective-permute-start.25 = (bf16[32,2048]{1,0:T(8,128)(2,1)S(1)}, bf16[32,2048]{1,0:T(8,128)(2,1)S(1)}, u32[]{:S(2)}, u32[]{:S(2)}) collective-permute-start(bf16[32,2048]{1,0:T(8,128)(2,1)S(1)} %get-tuple-element.46), channel_id=1, source_target_pairs={{0,28},{4,24},{8,20},{12,16},{16,12},{20,8},{24,4},{28,0},{1,29},{... | collective-permute-start | bytes 393224 | tf_op jit(solution)/shard_map/ppermute | solution.py:483
  (22 other events, 114.2 us)

commit v6 on v5

--- a/solution.py
+++ b/solution.py
@@ -426,6 +426,8 @@
                 out_near.held[e, q] = piece
             else:
                 out_far[e].held[q - 2] = piece
+        if q == 1:
+            out_near.send(0)
 
 
 def per_device(
@@ -562,7 +564,7 @@
         info,
         [full(near_back), kept_in_vmem(sides), kept_in_vmem(far_back)],
         [
-            (shape(experts, 2, cap, chans), None),
+            (shape(experts, 2, cap, chans), once),
             *[(shape(far_count, cap, chans), None)] * experts,
         ],
         small=[ids, head_rows, chan_rows],

time: 216 us -> 215 us (level)
    unnamed x34 -> x32, local copies, waits for them, and re-layouts: 16.9 us -> 16 us
where the time goes in v6:
time: 215 us; the launch traced here: 213 us
  waiting for transfers between devices  93 us (43%)
  Pallas kernels  52.3 us (24%)
  starting transfers between devices  48.7 us (23%)
  local copies, waits for them, and re-layouts  16.5 us (8%)
  other arithmetic  2.35 us (1%)
    pallas_call x13, Pallas kernels, call(): pl.pallas_call(body, out_shape=[(pltpu.HBM if pieces else pltpu.VMEM)(o.s...  50.1 us
    all_to_all x4, waiting for transfers between devices, exchange(): lax.all_to_all(value, 'expert', split_axis=0, concat_axis=0, tiled=True)  35.7 us
    ppermute x12, waiting for transfers between devices, permute(): return lax.ppermute(value, 'context', pairs)  28.8 us
    ppermute x14, waiting for transfers between devices, to_peers(): lax.ppermute(pieces[r], 'expert', [(e, e ^ r) for e in range(experts)])  28.5 us
    all_to_all x4, starting transfers between devices, exchange(): lax.all_to_all(value, 'expert', split_axis=0, concat_axis=0, tiled=True)  22.3 us
    ppermute x14, starting transfers between devices, to_peers(): lax.ppermute(pieces[r], 'expert', [(e, e ^ r) for e in range(experts)])  22.1 us
    unnamed x32, local copies, waits for them, and re-layouts  16 us
    ppermute x12, starting transfers between devices, permute(): return lax.ppermute(value, 'context', pairs)  4.33 us
  transfers between devices with their start and end apart: 30, of which 18 were waited for; matrix products, arithmetic and copies ran while one was open for 6% of the time, Pallas kernels for 17%

profile of v6, /device:TPU:0, one launch (start us, length us, event | category | flops | bytes accessed | tf_op | source)
XLA Modules:
  0.0 213.3 jit_solution(14787738102488256589)
XLA Ops:
  0.1 3.0 %shard_map.109.refs_1_ = bf16[256,2048]{1,0:T(8,128)(2,1)} custom-call(s32[14]{0:T(128)S(1)} %concatenate.9.refs_0_, s32[4,1,128]{2,1,0:T(1,128)} %bitcast.31, bf16[128,2048]{1,0:T(8,128)(2,1)} %bitcast.43), custom_call_target="tpu_custom_call" | custom-call | flops 134217728 | bytes 1573888 | tf_op jit(solution)/shard_map/pallas_call | solution.py:181
  3.1 7.3 %all-to-all-start = ((bf16[8,32,2048]{2,1,0:T(8,128)(2,1)}), bf16[8,32,2048]{2,1,0:T(8,128)(2,1)S(1)}, u32[]{:S(2)}, u32[]{:S(2)}) async-start(bf16[8,32,2048]{2,1,0:T(8,128)(2,1)} %bitcast.41), calls=%async_computation | async-start | bytes 2097152 | tf_op jit(solution)/shard_map/all_to_all | solution.py:481
  15.2 10.2 %copy.18 = bf16[256,8,2,1024]{3,1,2,0:T(8,128)(2,1)} copy(bf16[256,8,2,1024]{3,2,1,0:T(2,128)(2,1)} %bitcast.42) | data formatting | bytes 16777216
  25.5 10.7 %all-to-all-done.refs_0_ = bf16[8,32,2048]{2,1,0:T(8,128)(2,1)S(1)} async-done(((bf16[8,32,2048]{2,1,0:T(8,128)(2,1)}), bf16[8,32,2048]{2,1,0:T(8,128)(2,1)S(1)}, u32[]{:S(2)}, u32[]{:S(2)}) %all-to-all-start) | async-done | bytes 1048608 | tf_op jit(solution)/shard_map/all_to_all | solution.py:481
  39.9 4.6 %shard_map.113.refs_1_.refs_4_ = bf16[8,2,32,1152]{3,2,1,0:T(8,128)(2,1)} custom-call(s32[14]{0:T(128)S(1)} %concatenate.9.refs_0_, bf16[8,32,2048]{2,1,0:T(8,128)(2,1)S(1)} %shard_map.111._.refs_1_, bf16[8,32,2048]{2,1,0:T(8,128)(2,1)S(1)} %collective-permute-done.3.refs_2_, bf16[2048,1024]{1,0:T(8,128)(2,1)S(1)} %shard_map.112.refs_3_, ...), custom_call_target="tpu_custom_call" | custom-call | flops 2415919104 | bytes 8257536 | tf_op jit(solution)/shard_map/pallas_call | solution.py:181
  44.5 4.3 %all-to-all-start.1 = ((bf16[8,2,32,1152]{3,2,1,0:T(8,128)(2,1)}), bf16[8,2,32,1152]{3,2,1,0:T(8,128)(2,1)}, u32[]{:S(2)}, u32[]{:S(2)}) async-start(bf16[8,2,32,1152]{3,2,1,0:T(8,128)(2,1)} %shard_map.113.refs_1_.refs_4_), calls=%async_computation.1 | async-start | bytes 2359296 | tf_op jit(solution)/shard_map/all_to_all | solution.py:481
  48.8 13.1 %collective-permute-done.4.refs_0_ = bf16[8,32,2048]{2,1,0:T(8,128)(2,1)} collective-permute-done((bf16[8,32,2048]{2,1,0:T(8,128)(2,1)S(1)}, bf16[8,32,2048]{2,1,0:T(8,128)(2,1)}, u32[]{:S(2)}, u32[]{:S(2)}) %collective-permute-start.4) | collective-permute-done | bytes 1048608 | tf_op jit(solution)/shard_map/ppermute | solution.py:471
  61.9 2.9 %collective-permute-done.5.refs_2_ = bf16[8,32,2048]{2,1,0:T(8,128)(2,1)S(1)} collective-permute-done((bf16[8,32,2048]{2,1,0:T(8,128)(2,1)}, bf16[8,32,2048]{2,1,0:T(8,128)(2,1)S(1)}, u32[]{:S(2)}, u32[]{:S(2)}) %collective-permute-start.5) | collective-permute-done | bytes 1048608 | tf_op jit(solution)/shard_map/ppermute | solution.py:471
  65.8 7.4 %shard_map.115.refs_3_ = bf16[8,2,32,1024]{3,2,1,0:T(8,128)(2,1)} custom-call(s32[14]{0:T(128)S(1)} %concatenate.9.refs_0_, bf16[8,32,2048]{2,1,0:T(8,128)(2,1)} %shard_map.114.refs_1_, bf16[8,32,2048]{2,1,0:T(8,128)(2,1)} %copy-done.8, bf16[2048,2048]{1,0:T(8,128)(2,1)} %bitcast.38), custom_call_target="tpu_custom_call" | custom-call | flops 2147483648 | bytes 11534336 | tf_op jit(solution)/shard_map/pallas_call | solution.py:181
  73.3 4.7 %all-to-all-done.1.refs_2_.refs_4_ = bf16[8,2,32,1152]{3,2,1,0:T(8,128)(2,1)} async-done(((bf16[8,2,32,1152]{3,2,1,0:T(8,128)(2,1)}), bf16[8,2,32,1152]{3,2,1,0:T(8,128)(2,1)}, u32[]{:S(2)}, u32[]{:S(2)}) %all-to-all-start.1) | async-done | bytes 1179680 | tf_op jit(solution)/shard_map/all_to_all | solution.py:481
  78.0 3.7 %all-to-all-start.2 = ((bf16[8,2,32,1024]{3,2,1,0:T(8,128)(2,1)}), bf16[8,2,32,1024]{3,2,1,0:T(8,128)(2,1)S(1)}, u32[]{:S(2)}, u32[]{:S(2)}) async-start(bf16[8,2,32,1024]{3,2,1,0:T(8,128)(2,1)} %shard_map.115.refs_3_), calls=%async_computation.2 | async-start | bytes 2097152 | tf_op jit(solution)/shard_map/all_to_all | solution.py:481
  81.9 6.1 %shard_map.116 = (bf16[256,1024]{1,0:T(8,128)(2,1)}, bf16[256,1024]{1,0:T(8,128)(2,1)}) custom-call(s32[14]{0:T(128)S(1)} %concatenate.9.refs_0_, bf16[8,32,2048]{2,1,0:T(8,128)(2,1)S(1)} %shard_map.111._.refs_1_, bf16[8,32,2048]{2,1,0:T(8,128)(2,1)S(1)} %collective-permute-done.3.refs_2_, bf16[2048,2048]{1,0:T(8,128)(2,1)} %bitcast.39, ...), custom_call_target="tpu_custom_call" | custom-call | flops 2147483648 | bytes 11534336 | tf_op jit(solution)/shard_map/pallas_call | solution.py:181
  88.0 6.7 %shard_map.117 = (bf16[256,1024]{1,0:T(8,128)(2,1)}, bf16[256,1024]{1,0:T(8,128)(2,1)}) custom-call(s32[14]{0:T(128)S(1)} %concatenate.9.refs_0_, bf16[8,32,2048]{2,1,0:T(8,128)(2,1)} %shard_map.114.refs_1_, bf16[8,32,2048]{2,1,0:T(8,128)(2,1)} %copy-done.8, bf16[2048,2048]{1,0:T(8,128)(2,1)} %bitcast.40, bf16[8,2,32,1152]{3,2,1,0:T(8,128)(2,1)} %shard_map.113.refs_1_.refs_4_), custom_call_target="tpu_custom_call" | custom-call | flops 2147483648 | bytes 11534336 | tf_op jit(solution)/shard_map/pallas_call | solution.py:181
  97.9 3.7 %collective-permute-done.7 = bf16[128,256]{1,0:T(8,128)(2,1)S(1)} collective-permute-done((bf16[128,256]{1,0:T(8,128)(2,1)}, bf16[128,256]{1,0:T(8,128)(2,1)S(1)}, u32[]{:S(2)}, u32[]{:S(2)}) %collective-permute-start.7) | collective-permute-done | bytes 65568 | tf_op jit(solution)/shard_map/ppermute | solution.py:471
  103.7 3.9 %all-to-all-done.2.refs_6_ = bf16[8,2,32,1024]{3,2,1,0:T(8,128)(2,1)S(1)} async-done(((bf16[8,2,32,1024]{3,2,1,0:T(8,128)(2,1)}), bf16[8,2,32,1024]{3,2,1,0:T(8,128)(2,1)S(1)}, u32[]{:S(2)}, u32[]{:S(2)}) %all-to-all-start.2) | async-done | bytes 1048608 | tf_op jit(solution)/shard_map/all_to_all | solution.py:481
  107.6 9.6 %shard_map.119 = (bf16[8,2,32,1024]{3,2,1,0:T(8,128)(2,1)}, bf16[2,32,1024]{2,1,0:T(8,128)(2,1)S(1)}, bf16[2,32,1024]{2,1,0:T(8,128)(2,1)S(1)}, bf16[2,32,1024]{...) custom-call(s32[14]{0:T(128)S(1)} %concatenate.9.refs_0_, ...), custom_call_target="tpu_custom_call" | custom-call | flops 1744830464 | bytes 4587520 | tf_op jit(solution)/shard_map/pallas_call | solution.py:181
  120.3 2.9 %collective-permute-start.13 = (bf16[2,32,1024]{2,1,0:T(8,128)(2,1)S(1)}, bf16[2,32,1024]{2,1,0:T(8,128)(2,1)S(1)}, u32[]{:S(2)}, u32[]{:S(2)}) collective-permute-start(bf16[2,32,1024]{2,1,0:T(8,128)(2,1)S(1)} %get-tuple-element.34), channel_id=1, source_target_pairs={{0,20},{4,16},{8,28},{12,24},{16,4},{20,0},{24,12},{28,8},{1,21},{... | collective-permute-start | bytes 393224 | tf_op jit(solution)/shard_map/ppermute | solution.py:485
  129.0 9.6 %collective-permute-done.12.refs_5_ = bf16[2,32,1024]{2,1,0:T(8,128)(2,1)S(1)} collective-permute-done((bf16[2,32,1024]{2,1,0:T(8,128)(2,1)S(1)}, bf16[2,32,1024]{2,1,0:T(8,128)(2,1)S(1)}, u32[]{:S(2)}, u32[]{:S(2)}) %collective-permute-start.12) | collective-permute-done | bytes 131104 | tf_op jit(solution)/shard_map/ppermute | solution.py:485
  138.6 2.9 %collective-permute-done.13.refs_6_ = bf16[2,32,1024]{2,1,0:T(8,128)(2,1)S(1)} collective-permute-done((bf16[2,32,1024]{2,1,0:T(8,128)(2,1)S(1)}, bf16[2,32,1024]{2,1,0:T(8,128)(2,1)S(1)}, u32[]{:S(2)}, u32[]{:S(2)}) %collective-permute-start.13) | collective-permute-done | bytes 131104 | tf_op jit(solution)/shard_map/ppermute | solution.py:485
  141.6 6.9 %all-to-all-start.3 = ((bf16[8,2,32,1024]{3,2,1,0:T(8,128)(2,1)}), bf16[8,2,32,1024]{3,2,1,0:T(8,128)(2,1)S(1)}, u32[]{:S(2)}, u32[]{:S(2)}) async-start(bf16[8,2,32,1024]{3,2,1,0:T(8,128)(2,1)} %shard_map.120), calls=%async_computation.3 | async-start | bytes 2097152 | tf_op jit(solution)/shard_map/all_to_all | solution.py:481
  157.2 16.3 %all-to-all-done.3.refs_1_ = bf16[8,2,32,1024]{3,2,1,0:T(8,128)(2,1)S(1)} async-done(((bf16[8,2,32,1024]{3,2,1,0:T(8,128)(2,1)}), bf16[8,2,32,1024]{3,2,1,0:T(8,128)(2,1)S(1)}, u32[]{:S(2)}, u32[]{:S(2)}) %all-to-all-start.3) | async-done | bytes 1048608 | tf_op jit(solution)/shard_map/all_to_all | solution.py:481
  177.7 4.4 %collective-permute-done.17.refs_4_.refs_3_ = bf16[8,32,2048]{2,1,0:T(8,128)(2,1)S(1)} collective-permute-done((bf16[8,32,2048]{2,1,0:T(8,128)(2,1)}, bf16[8,32,2048]{2,1,0:T(8,128)(2,1)S(1)}, u32[]{:S(2)}, u32[]{:S(2)}) %collective-permute-start.17) | collective-permute-done | bytes 1048608 | tf_op jit(solution)/shard_map/ppermute | solution.py:471
  192.9 3.3 %collective-permute-start.24 = (bf16[32,2048]{1,0:T(8,128)(2,1)S(1)}, bf16[32,2048]{1,0:T(8,128)(2,1)S(1)}, u32[]{:S(2)}, u32[]{:S(2)}) collective-permute-start(bf16[32,2048]{1,0:T(8,128)(2,1)S(1)} %get-tuple-element.45), channel_id=1, source_target_pairs={{0,24},{4,28},{8,16},{12,20},{16,8},{20,12},{24,0},{28,4},{1,25},{... | collective-permute-start | bytes 393224 | tf_op jit(solution)/shard_map/ppermute | solution.py:485
  198.3 12.9 %collective-permute-done.23.refs_7_ = bf16[32,2048]{1,0:T(8,128)(2,1)S(1)} collective-permute-done((bf16[32,2048]{1,0:T(8,128)(2,1)S(1)}, bf16[32,2048]{1,0:T(8,128)(2,1)S(1)}, u32[]{:S(2)}, u32[]{:S(2)}) %collective-permute-start.23) | collective-permute-done | bytes 131104 | tf_op jit(solution)/shard_map/ppermute | solution.py:485
  (99 shorter events, 51.5 us)
Async XLA Ops:
  3.1 33.1 %all-to-all-start = ((bf16[8,32,2048]{2,1,0:T(8,128)(2,1)}), bf16[8,32,2048]{2,1,0:T(8,128)(2,1)S(1)}, u32[]{:S(2)}, u32[]{:S(2)}) async-start(bf16[8,32,2048]{2,1,0:T(8,128)(2,1)} %bitcast.41), calls=%async_computation | async-start | bytes 2097152 | tf_op jit(solution)/shard_map/all_to_all | solution.py:481
  12.5 13.0 %collective-permute-start = (bf16[16,2048]{1,0:T(8,128)(2,1)S(1)}, bf16[16,2048]{1,0:T(8,128)(2,1)S(1)}, u32[]{:S(2)}, u32[]{:S(2)}) collective-permute-start(bf16[16,2048]{1,0:T(8,128)(2,1)S(1)} %bitcast.28), channel_id=1, source_target_pairs={{0,1},{1,0},{2,3},{3,2},{4,5},{5,4},{6,7},{7,6},{8,9},{9,8},{10,11... | collective-permute-start | bytes 196616 | tf_op jit(solution)/shard_map/ppermute | solution.py:471
  15.2 10.2 %collective-permute-start.2 = (bf16[16,2048]{1,0:T(8,128)(2,1)S(1)}, bf16[16,2048]{1,0:T(8,128)(2,1)S(1)}, u32[]{:S(2)}, u32[]{:S(2)}) collective-permute-start(bf16[16,2048]{1,0:T(8,128)(2,1)S(1)} %collective-permute-done.1.refs_4_.refs_7_), channel_id=1, source_target_pairs={{0,1},{1,0},{2,3},{3,2},{4,5},{5,4},{6,7},{7,6},{8,9},{9,8},{10,11... | collective-permute-start | bytes 196616 | tf_op jit(solution)/shard_map/ppermute | solution.py:471
  36.2 25.7 %collective-permute-start.4 = (bf16[8,32,2048]{2,1,0:T(8,128)(2,1)S(1)}, bf16[8,32,2048]{2,1,0:T(8,128)(2,1)}, u32[]{:S(2)}, u32[]{:S(2)}) collective-permute-start(bf16[8,32,2048]{2,1,0:T(8,128)(2,1)S(1)} %shard_map.111._.refs_1_), channel_id=1, source_target_pairs={{0,2},{1,3},{2,0},{3,1},{4,6},{5,7},{6,4},{7,5},{8,10},{9,11},{10,... | collective-permute-start | bytes 3145736 | tf_op jit(solution)/shard_map/ppermute | solution.py:471
  44.5 33.5 %all-to-all-start.1 = ((bf16[8,2,32,1152]{3,2,1,0:T(8,128)(2,1)}), bf16[8,2,32,1152]{3,2,1,0:T(8,128)(2,1)}, u32[]{:S(2)}, u32[]{:S(2)}) async-start(bf16[8,2,32,1152]{3,2,1,0:T(8,128)(2,1)} %shard_map.113.refs_1_.refs_4_), calls=%async_computation.1 | async-start | bytes 2359296 | tf_op jit(solution)/shard_map/all_to_all | solution.py:481
  78.0 29.6 %all-to-all-start.2 = ((bf16[8,2,32,1024]{3,2,1,0:T(8,128)(2,1)}), bf16[8,2,32,1024]{3,2,1,0:T(8,128)(2,1)S(1)}, u32[]{:S(2)}, u32[]{:S(2)}) async-start(bf16[8,2,32,1024]{3,2,1,0:T(8,128)(2,1)} %shard_map.115.refs_3_), calls=%async_computation.2 | async-start | bytes 2097152 | tf_op jit(solution)/shard_map/all_to_all | solution.py:481
  97.1 4.5 %collective-permute-start.7 = (bf16[128,256]{1,0:T(8,128)(2,1)}, bf16[128,256]{1,0:T(8,128)(2,1)S(1)}, u32[]{:S(2)}, u32[]{:S(2)}) collective-permute-start(bf16[128,256]{1,0:T(8,128)(2,1)} %shard_map.118), channel_id=1, source_target_pairs={{0,2},{1,3},{2,0},{3,1},{4,6},{5,7},{6,4},{7,5},{8,10},{9,11},{10,... | collective-permute-start | bytes 196616 | tf_op jit(solution)/shard_map/ppermute | solution.py:471
  117.2 8.8 %collective-permute-start.10 = (bf16[2,32,1024]{2,1,0:T(8,128)(2,1)S(1)}, bf16[2,32,1024]{2,1,0:T(8,128)(2,1)S(1)}, u32[]{:S(2)}, u32[]{:S(2)}) collective-permute-start(bf16[2,32,1024]{2,1,0:T(8,128)(2,1)S(1)} %get-tuple-element.31), channel_id=1, source_target_pairs={{0,8},{4,12},{8,0},{12,4},{16,24},{20,28},{24,16},{28,20},{1,9},{5... | collective-permute-start | bytes 393224 | tf_op jit(solution)/shard_map/ppermute | solution.py:485
  117.3 11.6 %collective-permute-start.11 = (bf16[2,32,1024]{2,1,0:T(8,128)(2,1)S(1)}, bf16[2,32,1024]{2,1,0:T(8,128)(2,1)S(1)}, u32[]{:S(2)}, u32[]{:S(2)}) collective-permute-start(bf16[2,32,1024]{2,1,0:T(8,128)(2,1)S(1)} %get-tuple-element.32), channel_id=1, source_target_pairs={{0,12},{4,8},{8,4},{12,0},{16,28},{20,24},{24,20},{28,16},{1,13},{... | collective-permute-start | bytes 393224 | tf_op jit(solution)/shard_map/ppermute | solution.py:485
  120.2 18.5 %collective-permute-start.12 = (bf16[2,32,1024]{2,1,0:T(8,128)(2,1)S(1)}, bf16[2,32,1024]{2,1,0:T(8,128)(2,1)S(1)}, u32[]{:S(2)}, u32[]{:S(2)}) collective-permute-start(bf16[2,32,1024]{2,1,0:T(8,128)(2,1)S(1)} %get-tuple-element.33), channel_id=1, source_target_pairs={{0,16},{4,20},{8,24},{12,28},{16,0},{20,4},{24,8},{28,12},{1,17},{... | collective-permute-start | bytes 393224 | tf_op jit(solution)/shard_map/ppermute | solution.py:485
  120.3 21.2 %collective-permute-start.13 = (bf16[2,32,1024]{2,1,0:T(8,128)(2,1)S(1)}, bf16[2,32,1024]{2,1,0:T(8,128)(2,1)S(1)}, u32[]{:S(2)}, u32[]{:S(2)}) collective-permute-start(bf16[2,32,1024]{2,1,0:T(8,128)(2,1)S(1)} %get-tuple-element.34), channel_id=1, source_target_pairs={{0,20},{4,16},{8,28},{12,24},{16,4},{20,0},{24,12},{28,8},{1,21},{... | collective-permute-start | bytes 393224 | tf_op jit(solution)/shard_map/ppermute | solution.py:485
  123.1 18.4 %collective-permute-start.14 = (bf16[2,32,1024]{2,1,0:T(8,128)(2,1)S(1)}, bf16[2,32,1024]{2,1,0:T(8,128)(2,1)S(1)}, u32[]{:S(2)}, u32[]{:S(2)}) collective-permute-start(bf16[2,32,1024]{2,1,0:T(8,128)(2,1)S(1)} %get-tuple-element.35), channel_id=1, source_target_pairs={{0,24},{4,28},{8,16},{12,20},{16,8},{20,12},{24,0},{28,4},{1,25},{... | collective-permute-start | bytes 393224 | tf_op jit(solution)/shard_map/ppermute | solution.py:485
  126.0 15.5 %collective-permute-start.15 = (bf16[2,32,1024]{2,1,0:T(8,128)(2,1)S(1)}, bf16[2,32,1024]{2,1,0:T(8,128)(2,1)S(1)}, u32[]{:S(2)}, u32[]{:S(2)}) collective-permute-start(bf16[2,32,1024]{2,1,0:T(8,128)(2,1)S(1)} %get-tuple-element.36), channel_id=1, source_target_pairs={{0,28},{4,24},{8,20},{12,16},{16,12},{20,8},{24,4},{28,0},{1,29},{... | collective-permute-start | bytes 393224 | tf_op jit(solution)/shard_map/ppermute | solution.py:485
  128.9 12.6 %collective-permute-start.9 = (bf16[2,32,1024]{2,1,0:T(8,128)(2,1)S(1)}, bf16[2,32,1024]{2,1,0:T(8,128)(2,1)S(1)}, u32[]{:S(2)}, u32[]{:S(2)}) collective-permute-start(bf16[2,32,1024]{2,1,0:T(8,128)(2,1)S(1)} %get-tuple-element.30), channel_id=1, source_target_pairs={{0,4},{4,0},{8,12},{12,8},{16,20},{20,16},{24,28},{28,24},{1,5},{5... | collective-permute-start | bytes 393224 | tf_op jit(solution)/shard_map/ppermute | solution.py:485
  141.6 32.0 %all-to-all-start.3 = ((bf16[8,2,32,1024]{3,2,1,0:T(8,128)(2,1)}), bf16[8,2,32,1024]{3,2,1,0:T(8,128)(2,1)S(1)}, u32[]{:S(2)}, u32[]{:S(2)}) async-start(bf16[8,2,32,1024]{3,2,1,0:T(8,128)(2,1)} %shard_map.120), calls=%async_computation.3 | async-start | bytes 2097152 | tf_op jit(solution)/shard_map/all_to_all | solution.py:481
  156.7 25.4 %collective-permute-start.17 = (bf16[8,32,2048]{2,1,0:T(8,128)(2,1)}, bf16[8,32,2048]{2,1,0:T(8,128)(2,1)S(1)}, u32[]{:S(2)}, u32[]{:S(2)}) collective-permute-start(bf16[8,32,2048]{2,1,0:T(8,128)(2,1)} %add_convert_fusion), channel_id=1, source_target_pairs={{0,2},{1,3},{2,0},{3,1},{4,6},{5,7},{6,4},{7,5},{8,10},{9,11},{10,... | collective-permute-start | bytes 3145736 | tf_op jit(solution)/shard_map/ppermute | solution.py:471
  177.6 6.3 %collective-permute-start.18 = (bf16[8,32,2048]{2,1,0:T(8,128)(2,1)S(1)}, bf16[8,32,2048]{2,1,0:T(8,128)(2,1)S(1)}, u32[]{:S(2)}, u32[]{:S(2)}) collective-permute-start(bf16[8,32,2048]{2,1,0:T(8,128)(2,1)S(1)} %shard_map.124), channel_id=1, source_target_pairs={{0,1},{1,0},{2,3},{3,2},{4,5},{5,4},{6,7},{7,6},{8,9},{9,8},{10,11... | collective-permute-start | bytes 3145736 | tf_op jit(solution)/shard_map/ppermute | solution.py:471
  185.0 7.9 %collective-permute-start.19 = (bf16[32,2048]{1,0:T(8,128)(2,1)S(1)}, bf16[32,2048]{1,0:T(8,128)(2,1)S(1)}, u32[]{:S(2)}, u32[]{:S(2)}) collective-permute-start(bf16[32,2048]{1,0:T(8,128)(2,1)S(1)} %get-tuple-element.40), channel_id=1, source_target_pairs={{0,4},{4,0},{8,12},{12,8},{16,20},{20,16},{24,28},{28,24},{1,5},{5... | collective-permute-start | bytes 393224 | tf_op jit(solution)/shard_map/ppermute | solution.py:485
  187.0 9.4 %collective-permute-start.20 = (bf16[32,2048]{1,0:T(8,128)(2,1)S(1)}, bf16[32,2048]{1,0:T(8,128)(2,1)S(1)}, u32[]{:S(2)}, u32[]{:S(2)}) collective-permute-start(bf16[32,2048]{1,0:T(8,128)(2,1)S(1)} %get-tuple-element.41), channel_id=1, source_target_pairs={{0,8},{4,12},{8,0},{12,4},{16,24},{20,28},{24,16},{28,20},{1,9},{5... | collective-permute-start | bytes 393224 | tf_op jit(solution)/shard_map/ppermute | solution.py:485
  188.5 9.8 %collective-permute-start.21 = (bf16[32,2048]{1,0:T(8,128)(2,1)S(1)}, bf16[32,2048]{1,0:T(8,128)(2,1)S(1)}, u32[]{:S(2)}, u32[]{:S(2)}) collective-permute-start(bf16[32,2048]{1,0:T(8,128)(2,1)S(1)} %get-tuple-element.42), channel_id=1, source_target_pairs={{0,12},{4,8},{8,4},{12,0},{16,28},{20,24},{24,20},{28,16},{1,13},{... | collective-permute-start | bytes 393224 | tf_op jit(solution)/shard_map/ppermute | solution.py:485
  188.6 9.7 %collective-permute-start.22 = (bf16[32,2048]{1,0:T(8,128)(2,1)S(1)}, bf16[32,2048]{1,0:T(8,128)(2,1)S(1)}, u32[]{:S(2)}, u32[]{:S(2)}) collective-permute-start(bf16[32,2048]{1,0:T(8,128)(2,1)S(1)} %get-tuple-element.43), channel_id=1, source_target_pairs={{0,16},{4,20},{8,24},{12,28},{16,0},{20,4},{24,8},{28,12},{1,17},{... | collective-permute-start | bytes 393224 | tf_op jit(solution)/shard_map/ppermute | solution.py:485
  191.4 19.8 %collective-permute-start.23 = (bf16[32,2048]{1,0:T(8,128)(2,1)S(1)}, bf16[32,2048]{1,0:T(8,128)(2,1)S(1)}, u32[]{:S(2)}, u32[]{:S(2)}) collective-permute-start(bf16[32,2048]{1,0:T(8,128)(2,1)S(1)} %get-tuple-element.44), channel_id=1, source_target_pairs={{0,20},{4,16},{8,28},{12,24},{16,4},{20,0},{24,12},{28,8},{1,21},{... | collective-permute-start | bytes 393224 | tf_op jit(solution)/shard_map/ppermute | solution.py:485
  192.9 18.3 %collective-permute-start.24 = (bf16[32,2048]{1,0:T(8,128)(2,1)S(1)}, bf16[32,2048]{1,0:T(8,128)(2,1)S(1)}, u32[]{:S(2)}, u32[]{:S(2)}) collective-permute-start(bf16[32,2048]{1,0:T(8,128)(2,1)S(1)} %get-tuple-element.45), channel_id=1, source_target_pairs={{0,24},{4,28},{8,16},{12,20},{16,8},{20,12},{24,0},{28,4},{1,25},{... | collective-permute-start | bytes 393224 | tf_op jit(solution)/shard_map/ppermute | solution.py:485
  196.5 14.8 %collective-permute-start.25 = (bf16[32,2048]{1,0:T(8,128)(2,1)S(1)}, bf16[32,2048]{1,0:T(8,128)(2,1)S(1)}, u32[]{:S(2)}, u32[]{:S(2)}) collective-permute-start(bf16[32,2048]{1,0:T(8,128)(2,1)S(1)} %get-tuple-element.46), channel_id=1, source_target_pairs={{0,28},{4,24},{8,20},{12,16},{16,12},{20,8},{24,4},{28,0},{1,29},{... | collective-permute-start | bytes 393224 | tf_op jit(solution)/shard_map/ppermute | solution.py:485
  (21 other events, 113.2 us)
